TPU v7x, 128 devices: a whole 4x4x4 slice. The times are simulated.
128 devices in a mesh: dp: 4 (over y), table: 32 (over z, x, core).
Axes of the slice: x: 4, y: 4, z: 4, core: 2. Of those that a mesh axis runs over, the one named last changes fastest.
Arguments:
- pooled_a: bfloat16 [16384, 32, 32], P('dp', 'table'), may hold values from -6 to 6
- pooled_b: bfloat16 [16384, 32, 64], P('dp', 'table'), may hold values from -6 to 6
- pooled_c: bfloat16 [16384, 32, 128], P('dp', 'table'), may hold values from -6 to 6
- pooled_d: bfloat16 [16384, 32, 256], P('dp', 'table'), may hold values from -6 to 6
- proj_a: bfloat16 [32, 32, 512], P('table'), may hold values from -1 to 1
- proj_b: bfloat16 [32, 64, 512], P('table'), may hold values from -0.75 to 0.75
- proj_c: bfloat16 [32, 128, 512], P('table'), may hold values from -0.5 to 0.5
- proj_d: bfloat16 [32, 256, 512], P('table'), may hold values from -0.375 to 0.375
- slot_table: int32 [128], replicated, may hold values from 0 to 127, each once
- norm_gain: float32 [512], replicated, may hold values from 0.1 to 1.9
- grad_gram: bfloat16 [16384, 128, 128], P(('dp', 'table')), may hold values from -6 to 6
Outputs:
- grad_pooled_a: bfloat16 [16384, 32, 32], P('dp', 'table')
- grad_pooled_b: bfloat16 [16384, 32, 64], P('dp', 'table')
- grad_pooled_c: bfloat16 [16384, 32, 128], P('dp', 'table')
- grad_pooled_d: bfloat16 [16384, 32, 256], P('dp', 'table')
- grad_proj_a: float32 [32, 32, 512], P('table', None, 'dp')
- grad_proj_b: float32 [32, 64, 512], P('table', None, 'dp')
- grad_proj_c: float32 [32, 128, 512], P('table', None, 'dp')
- grad_proj_d: float32 [32, 256, 512], P('table', None, 'dp')
Inputs may be any that keep to these rules, and one draw needn't show every extreme that they name: `slot_table`: each table id stands in exactly one slot.
All inputs are finite; a program needn't handle non-finite values.
Results may differ from a plain program's by a relative error of at most 0.014.
Values may be sent and summed in bfloat16 or wider, within the bound.
No kernel may reach another device: no remote copies, remote signals or barrier semaphores. Data moves between devices by JAX's collectives and lax.ppermute only.
A program may use at most 320 MiB of HBM per device.

v0:
```python
import jax
import jax.numpy as jnp
from jax import lax
from jax.sharding import PartitionSpec as P


def own_project(pooled, weight):
    return jnp.einsum("btw,twd->btd", pooled, weight, preferred_element_type=jnp.float32).astype(
        jnp.bfloat16
    )


def owner_grads(pooled, weight, back):
    grad_in = jnp.einsum("btd,twd->btw", back, weight, preferred_element_type=jnp.float32).astype(
        jnp.bfloat16
    )
    grad_weight = jnp.einsum("btw,btd->twd", pooled, back, preferred_element_type=jnp.float32)
    return (grad_in, grad_weight)


def on_device(
    pooled_a,
    pooled_b,
    pooled_c,
    pooled_d,
    proj_a,
    proj_b,
    proj_c,
    proj_d,
    slot_table,
    norm_gain,
    grad_gram,
):
    ntable = lax.axis_size("table")
    ntab = grad_gram.shape[1]
    width = norm_gain.shape[0]
    total_rows = grad_gram.shape[0] * ntable * lax.axis_size("dp")
    wide = (
        lax.all_to_all(
            own_project(pooled_a, proj_a), "table", split_axis=0, concat_axis=1, tiled=True
        ),
        lax.all_to_all(
            own_project(pooled_b, proj_b), "table", split_axis=0, concat_axis=1, tiled=True
        ),
        lax.all_to_all(
            own_project(pooled_c, proj_c), "table", split_axis=0, concat_axis=1, tiled=True
        ),
        lax.all_to_all(
            own_project(pooled_d, proj_d), "table", split_axis=0, concat_axis=1, tiled=True
        ),
    )
    projected = jnp.concatenate(wide, axis=1)
    pf = projected.astype(jnp.float32)
    inv_rms = lax.rsqrt(jnp.mean(pf * pf, axis=-1, keepdims=True) + 1e-06)
    normed = (pf * inv_rms * norm_gain).astype(jnp.bfloat16)
    onehot = (slot_table[:, None] == jnp.arange(ntab, dtype=jnp.int32)[None, :]).astype(
        jnp.bfloat16
    )
    half_moved = jnp.einsum(
        "rij,tj->rit", grad_gram, onehot, preferred_element_type=jnp.float32
    ).astype(jnp.bfloat16)
    slot_grad = jnp.einsum(
        "si,rit->rst", onehot, half_moved, preferred_element_type=jnp.float32
    ).astype(jnp.bfloat16)
    grad_normed = jnp.einsum("rst,rtd->rsd", slot_grad, normed, preferred_element_type=jnp.float32)
    grad_normed = grad_normed + jnp.einsum(
        "rts,rtd->rsd", slot_grad, normed, preferred_element_type=jnp.float32
    )
    grad_normed = grad_normed / jnp.sqrt(jnp.float32(width))
    h = norm_gain * grad_normed
    grad_projected = (
        inv_rms * h - pf * inv_rms**3 * jnp.mean(pf * h, axis=-1, keepdims=True)
    ).astype(jnp.bfloat16)
    pieces = [grad_projected[:, k * ntable : (k + 1) * ntable] for k in range(4)]
    back = (
        lax.all_to_all(pieces[0], "table", split_axis=1, concat_axis=0, tiled=True),
        lax.all_to_all(pieces[1], "table", split_axis=1, concat_axis=0, tiled=True),
        lax.all_to_all(pieces[2], "table", split_axis=1, concat_axis=0, tiled=True),
        lax.all_to_all(pieces[3], "table", split_axis=1, concat_axis=0, tiled=True),
    )
    grad_a, weight_a = owner_grads(pooled_a, proj_a, back[0])
    grad_b, weight_b = owner_grads(pooled_b, proj_b, back[1])
    grad_c, weight_c = owner_grads(pooled_c, proj_c, back[2])
    grad_d, weight_d = owner_grads(pooled_d, proj_d, back[3])
    summed = (
        lax.psum_scatter(
            weight_a.astype(jnp.bfloat16), "dp", scatter_dimension=2, tiled=True
        ).astype(jnp.float32),
        lax.psum_scatter(
            weight_b.astype(jnp.bfloat16), "dp", scatter_dimension=2, tiled=True
        ).astype(jnp.float32),
        lax.psum_scatter(
            weight_c.astype(jnp.bfloat16), "dp", scatter_dimension=2, tiled=True
        ).astype(jnp.float32),
        lax.psum_scatter(
            weight_d.astype(jnp.bfloat16), "dp", scatter_dimension=2, tiled=True
        ).astype(jnp.float32),
    )
    scale = 1.0 / jnp.sqrt(jnp.float32(total_rows))
    return (
        grad_a,
        grad_b,
        grad_c,
        grad_d,
        summed[0] * scale,
        summed[1] * scale,
        summed[2] * scale,
        summed[3] * scale,
    )


def solution(mesh):
    in_specs = (
        P("dp", "table", None),
        P("dp", "table", None),
        P("dp", "table", None),
        P("dp", "table", None),
        P("table", None, None),
        P("table", None, None),
        P("table", None, None),
        P("table", None, None),
        P(),
        P(),
        P(("dp", "table"), None, None),
    )
    out_specs = (
        P("dp", "table", None),
        P("dp", "table", None),
        P("dp", "table", None),
        P("dp", "table", None),
        P("table", None, "dp"),
        P("table", None, "dp"),
        P("table", None, "dp"),
        P("table", None, "dp"),
    )
    return jax.shard_map(
        on_device, mesh=mesh, in_specs=in_specs, out_specs=out_specs, check_vma=False
    )
```

profile of v0, /device:TPU:0, one launch (start us, length us, event | category | flops | bytes accessed | tf_op | source)
XLA Modules:
  0.0 790.6 jit_solution(16884772043928497036)
XLA Ops:
  12.1 6.7 reduce.3
  18.8 6.5 copy.85
  25.3 7.8 reshape.141
  33.1 8.5 %all-to-all-start = ((bf16[32,2,32768]{2,1,0:T(2,128)(2,1)}), bf16[32,2,32768]{2,1,0:T(2,128)(2,1)}, u32[]{:S(2)}, u32[]{:S(2)}) async-start(bf16[32,2,32768]{2,1,0:T(2,128)(2,1)} %reshape.141), calls=%async_computation | async-start | bytes 8388608 | tf_op jit(solution)/shard_map/all_to_all | solution.py:39
  44.9 6.8 reduce.2
  51.7 6.4 copy.84
  58.1 7.9 reshape.139
  66.0 29.1 %all-to-all-done = bf16[32,2,32768]{2,1,0:T(2,128)(2,1)} async-done(((bf16[32,2,32768]{2,1,0:T(2,128)(2,1)}), bf16[32,2,32768]{2,1,0:T(2,128)(2,1)}, u32[]{:S(2)}, u32[]{:S(2)}) %all-to-all-start) | async-done | bytes 4194336 | tf_op jit(solution)/shard_map/all_to_all | solution.py:39
  95.1 5.3 all-to-all-start.1
  103.7 6.7 reduce.1
  110.4 6.5 copy.83
  116.9 7.8 reshape.137
  124.7 29.2 %all-to-all-done.1 = bf16[32,2,32768]{2,1,0:T(2,128)(2,1)} async-done(((bf16[32,2,32768]{2,1,0:T(2,128)(2,1)}), bf16[32,2,32768]{2,1,0:T(2,128)(2,1)}, u32[]{:S(2)}, u32[]{:S(2)}) %all-to-all-start.1) | async-done | bytes 4194336 | tf_op jit(solution)/shard_map/all_to_all | solution.py:42
  153.9 4.9 all-to-all-start.2
  162.1 6.8 reduce
  168.9 6.5 copy.82
  175.4 7.9 reshape.135
  183.3 28.9 %all-to-all-done.2 = bf16[32,2,32768]{2,1,0:T(2,128)(2,1)} async-done(((bf16[32,2,32768]{2,1,0:T(2,128)(2,1)}), bf16[32,2,32768]{2,1,0:T(2,128)(2,1)}, u32[]{:S(2)}, u32[]{:S(2)}) %all-to-all-start.2) | async-done | bytes 4194336 | tf_op jit(solution)/shard_map/all_to_all | solution.py:45
  212.2 5.0 all-to-all-start.3
  217.3 6.6 fusion.24
  223.9 19.8 %reshape.142 = bf16[4096,1,512]{2,1,0:T(2,128)(2,1)} reshape(bf16[32,2,32768]{2,1,0:T(2,128)(2,1)} %all-to-all-done) | data formatting | bytes 8388608
  243.7 6.6 copy.68
  250.3 19.8 %reshape.140 = bf16[4096,1,512]{2,1,0:T(2,128)(2,1)} reshape(bf16[32,2,32768]{2,1,0:T(2,128)(2,1)} %all-to-all-done.1) | data formatting | bytes 8388608
  270.0 6.5 copy.69
  276.6 19.8 %reshape.138 = bf16[4096,1,512]{2,1,0:T(2,128)(2,1)} reshape(bf16[32,2,32768]{2,1,0:T(2,128)(2,1)} %all-to-all-done.2) | data formatting | bytes 8388608
  296.4 6.5 copy.70
  302.9 19.8 %reshape.136 = bf16[4096,1,512]{2,1,0:T(2,128)(2,1)} reshape(bf16[32,2,32768]{2,1,0:T(2,128)(2,1)} %all-to-all-done.3) | data formatting | bytes 8388608
  328.6 10.6 %copy_bitcast_fusion.2 = (bf16[128,32,512]{2,1,0:T(8,128)(2,1)S(1)}, bf16[128,32,512]{2,1,0:T(8,128)(2,1)S(1)}) fusion(bf16[32,128,1,512]{3,1,0,2:T(8,128)(2,1)S(1)} %bitcast.174, bf16[32,128,1,512]{3,1,0,2:T(8,128)(2,1)S(1)} %bitcast.173), kind=kLoop, calls=%fused_computation.35 | loop fusion | bytes 16777216 | tf_op jit(solution)/shard_map/all_to_all | solution.py:42
  339.2 10.4 %copy_bitcast_fusion = (bf16[128,32,512]{2,1,0:T(8,128)(2,1)S(1)}, bf16[128,32,512]{2,1,0:T(8,128)(2,1)S(1)}) fusion(bf16[32,128,1,512]{3,1,0,2:T(8,128)(2,1)S(1)} %bitcast.176, bf16[32,128,1,512]{3,1,0,2:T(8,128)(2,1)S(1)} %bitcast.175), kind=kLoop, calls=%fused_computation.33 | loop fusion | bytes 16777216 | tf_op jit(solution)/shard_map/all_to_all | solution.py:48
  353.5 19.1 %fusion.7 = f32[128,128,512]{2,1,0:T(8,128)} fusion(bf16[128,128,128]{2,1,0:T(8,128)(2,1)} %fusion.24, f32[512]{0:T(512)S(1)} %copy-done.22, f32[128,128]{1,0:T(8,128)S(1)} %get-tuple-element.45, bf16[128,32,512]{2,1,0:T(8,128)(2,1)} %copy-done.4, bf16[128,32,512]{2,1,0:T(8,128)(2,1)} %copy-done.5, bf16[128,32,512]{2,1,0:T(8,128)(2,1)} %copy-done.1, ...), kind=kOutput, calls=%fused_computation.13 | convolution fusion | flops 2239758336 | bytes 54593536 | tf_op jit(solution)/shard_map/rts,rtd->rsd/dot_general | solution.py:66
  372.6 36.7 %fusion.6 = (f32[128,128]{1,0:T(8,128)S(1)}, f32[128,128,512]{2,1,0:T(8,128)}) fusion(f32[512]{0:T(512)S(1)} %broadcast_multiply_fusion.1, f32[128,128,512]{2,1,0:T(8,128)} %fusion.7, bf16[128,32,512]{2,1,0:T(8,128)(2,1)} %copy-done.4, bf16[128,32,512]{2,1,0:T(8,128)(2,1)} %copy-done.5, bf16[128,32,512]{2,1,0:T(8,128)(2,1)} %copy-done.1, ...), kind=kOutput, calls=%fused_computation.10 | convolution fusion | flops 2340405248 | bytes 88215552 | tf_op jit(solution)/shard_map/rst,rtd->rsd/dot_general | solution.py:65
  409.4 31.5 %fusion.5 = bf16[128,128,512]{2,1,0:T(8,128)(2,1)} fusion(f32[128,128]{1,0:T(8,128)S(1)} %broadcast_multiply_fusion, f32[128,128]{1,0:T(8,128)S(1)} %get-tuple-element.44, f32[128,128]{1,0:T(8,128)S(1)} %get-tuple-element.45, f32[512]{0:T(512)S(1)} %broadcast_multiply_fusion.1, f32[128,128,512]{2,1,0:T(8,128)} %get-tuple-element.47, ...), kind=kLoop, calls=%fused_computation.9 | loop fusion | flops 125829120 | bytes 100861952 | tf_op jit(solution)/shard_map/convert_element_type | solution.py:73
  440.9 11.4 %fusion.58 = (bf16[128,32,512]{2,1,0:T(8,128)(2,1)S(1)}, bf16[128,32,512]{2,1,0:T(8,128)(2,1)}, bf16[128,32,512]{2,1,0:T(8,128)(2,1)}, bf16[128,32,512]{2,1,0:T(8,128)(2,1)}) fusion(bf16[128,128,512]{2,1,0:T(8,128)(2,1)} %fusion.5), kind=kLoop, calls=%fused_computation.80 | loop fusion | bytes 33554432 | tf_op jit(solution)/shard_map/slice | solution.py:74
  456.7 7.6 all-to-all-start.7
  464.3 6.5 copy.59
  470.8 47.0 %all-to-all-done.7 = bf16[128,32,512]{2,0,1:T(8,128)(2,1)} async-done(((bf16[128,32,512]{2,0,1:T(8,128)(2,1)}), bf16[128,32,512]{2,0,1:T(8,128)(2,1)}, u32[]{:S(2)}, u32[]{:S(2)}) %all-to-all-start.7) | async-done | bytes 4194336 | tf_op jit(solution)/shard_map/all_to_all | solution.py:79
  517.8 5.0 all-to-all-start.6
  522.9 6.6 copy.58
  529.4 46.9 %all-to-all-done.6 = bf16[128,32,512]{2,0,1:T(8,128)(2,1)} async-done(((bf16[128,32,512]{2,0,1:T(8,128)(2,1)}), bf16[128,32,512]{2,0,1:T(8,128)(2,1)}, u32[]{:S(2)}, u32[]{:S(2)}) %all-to-all-start.6) | async-done | bytes 4194336 | tf_op jit(solution)/shard_map/all_to_all | solution.py:78
  576.3 4.9 all-to-all-start.5
  581.2 6.5 copy.57
  587.6 47.0 %all-to-all-done.5 = bf16[128,32,512]{2,0,1:T(8,128)(2,1)} async-done(((bf16[128,32,512]{2,0,1:T(8,128)(2,1)}), bf16[128,32,512]{2,0,1:T(8,128)(2,1)}, u32[]{:S(2)}, u32[]{:S(2)}) %all-to-all-start.5) | async-done | bytes 4194336 | tf_op jit(solution)/shard_map/all_to_all | solution.py:77
  634.6 4.9 all-to-all-start.4
  642.7 4.9 fusion.15
  655.9 37.1 %all-to-all-done.4 = bf16[128,32,512]{2,0,1:T(8,128)(2,1)} async-done(((bf16[128,32,512]{2,0,1:T(8,128)(2,1)}), bf16[128,32,512]{2,0,1:T(8,128)(2,1)}, u32[]{:S(2)}, u32[]{:S(2)}) %all-to-all-start.4) | async-done | bytes 4194336 | tf_op jit(solution)/shard_map/all_to_all | solution.py:76
  716.0 21.1 %reduce-scatter.15.cloned.1.call-done = bf16[128,64]{1,0:T(8,128)(2,1)} async-done(((bf16[512,64]{1,0:T(8,128)(2,1)}), bf16[128,64]{1,0:T(8,128)(2,1)}) %reduce-scatter.15.cloned.1.call-update) | async-done | bytes 16400
  738.6 21.0 %reduce-scatter.9.cloned.1.call-done = bf16[1,128,128]{1,2,0:T(8,128)(2,1)} async-done(((bf16[1,128,512]{1,2,0:T(8,128)(2,1)}), bf16[1,128,128]{1,2,0:T(8,128)(2,1)}) %reduce-scatter.9.cloned.1.call-update) | async-done | bytes 32784 | tf_op jit(solution)/shard_map/reduce_scatter | solution.py:92
  761.1 21.2 %reduce-scatter.11.cloned.1.call-done = bf16[1,256,128]{1,2,0:T(8,128)(2,1)} async-done(((bf16[1,256,512]{1,2,0:T(8,128)(2,1)}), bf16[1,256,128]{1,2,0:T(8,128)(2,1)}) %reduce-scatter.11.cloned.1.call-update) | async-done | bytes 65552 | tf_op jit(solution)/shard_map/reduce_scatter | solution.py:95
  (88 shorter events, 67.9 us)
Async XLA Ops:
  7.2 151.6 %copy-start = (bf16[4096,1,256]{2,0,1:T(8,128)(2,1)S(1)}, bf16[4096,1,256]{2,0,1:T(8,128)(2,1)}, u32[]{:S(2)}) copy-start(bf16[4096,1,256]{2,0,1:T(8,128)(2,1)} %param.14) | copy-start | bytes 6291460
  33.1 8.5 %copy-start.9 = (bf16[4096,1,64]{0,2,1:T(8,128)(2,1)S(1)}, bf16[4096,1,64]{0,2,1:T(8,128)(2,1)}, u32[]{:S(2)}) copy-start(bf16[4096,1,64]{0,2,1:T(8,128)(2,1)} %param.12) | copy-start | bytes 1572868
  33.1 8.5 %copy-start.18 = (bf16[1,64,512]{2,1,0:T(8,128)(2,1)S(1)}, bf16[1,64,512]{2,1,0:T(8,128)(2,1)}, u32[]{:S(2)}) copy-start(bf16[1,64,512]{2,1,0:T(8,128)(2,1)} %param.16) | copy-start | bytes 196612
  33.1 62.0 %all-to-all-start = ((bf16[32,2,32768]{2,1,0:T(2,128)(2,1)}), bf16[32,2,32768]{2,1,0:T(2,128)(2,1)}, u32[]{:S(2)}, u32[]{:S(2)}) async-start(bf16[32,2,32768]{2,1,0:T(2,128)(2,1)} %reshape.141), calls=%async_computation | async-start | bytes 8388608 | tf_op jit(solution)/shard_map/all_to_all | solution.py:39
  66.0 34.5 %copy-start.12 = (bf16[4096,1,128]{2,0,1:T(8,128)(2,1)S(1)}, bf16[4096,1,128]{2,0,1:T(8,128)(2,1)}, u32[]{:S(2)}) copy-start(bf16[4096,1,128]{2,0,1:T(8,128)(2,1)} %param.13) | copy-start | bytes 3145732
  66.0 34.5 %copy-start.14 = (bf16[1,128,512]{2,1,0:T(8,128)(2,1)S(1)}, bf16[1,128,512]{2,1,0:T(8,128)(2,1)}, u32[]{:S(2)}) copy-start(bf16[1,128,512]{2,1,0:T(8,128)(2,1)} %param.17) | copy-start | bytes 393220
  95.1 58.8 %all-to-all-start.1 = ((bf16[32,2,32768]{2,1,0:T(2,128)(2,1)}), bf16[32,2,32768]{2,1,0:T(2,128)(2,1)}, u32[]{:S(2)}, u32[]{:S(2)}) async-start(bf16[32,2,32768]{2,1,0:T(2,128)(2,1)} %reshape.139), calls=%async_computation.1 | async-start | bytes 8388608 | tf_op jit(solution)/shard_map/all_to_all | solution.py:42
  124.7 34.1 %copy-start.16 = (bf16[1,256,512]{2,1,0:T(8,128)(2,1)S(1)}, bf16[1,256,512]{2,1,0:T(8,128)(2,1)}, u32[]{:S(2)}) copy-start(bf16[1,256,512]{2,1,0:T(8,128)(2,1)} %param.18) | copy-start | bytes 786436
  153.9 58.3 %all-to-all-start.2 = ((bf16[32,2,32768]{2,1,0:T(2,128)(2,1)}), bf16[32,2,32768]{2,1,0:T(2,128)(2,1)}, u32[]{:S(2)}, u32[]{:S(2)}) async-start(bf16[32,2,32768]{2,1,0:T(2,128)(2,1)} %reshape.137), calls=%async_computation.2 | async-start | bytes 8388608 | tf_op jit(solution)/shard_map/all_to_all | solution.py:45
  183.3 34.0 %copy-start.22 = (f32[512]{0:T(512)S(1)}, f32[512]{0:T(512)}, u32[]{:S(2)}) copy-start(f32[512]{0:T(512)} %param.20) | copy-start | bytes 6148
  183.3 34.0 %copy-start.21 = (s32[128]{0:T(128)S(1)}, s32[128]{0:T(128)}, u32[]{:S(2)}) copy-start(s32[128]{0:T(128)} %param.19) | copy-start | bytes 1540
  212.2 90.7 %all-to-all-start.3 = ((bf16[32,2,32768]{2,1,0:T(2,128)(2,1)}), bf16[32,2,32768]{2,1,0:T(2,128)(2,1)}, u32[]{:S(2)}, u32[]{:S(2)}) async-start(bf16[32,2,32768]{2,1,0:T(2,128)(2,1)} %reshape.135), calls=%async_computation.3 | async-start | bytes 8388608 | tf_op jit(solution)/shard_map/all_to_all | solution.py:48
  322.7 4.8 copy-start.6
  322.7 5.9 copy-start.7
  328.6 10.6 %copy-start.8 = (bf16[4096,1,512]{2,0,1:T(8,128)(2,1)S(1)}, bf16[4096,1,512]{2,0,1:T(8,128)(2,1)}, u32[]{:S(2)}) copy-start(bf16[4096,1,512]{2,0,1:T(8,128)(2,1)} %copy.70) | copy-start | bytes 12582916
  339.1 10.4 %copy-start.1 = (bf16[128,32,512]{2,1,0:T(8,128)(2,1)}, bf16[128,32,512]{2,1,0:T(8,128)(2,1)S(1)}, u32[]{:S(2)}) copy-start(bf16[128,32,512]{2,1,0:T(8,128)(2,1)S(1)} %get-tuple-element.50) | copy-start | bytes 12582916
  339.1 10.4 %copy-start.3 = (bf16[128,32,512]{2,1,0:T(8,128)(2,1)}, bf16[128,32,512]{2,1,0:T(8,128)(2,1)S(1)}, u32[]{:S(2)}) copy-start(bf16[128,32,512]{2,1,0:T(8,128)(2,1)S(1)} %get-tuple-element.51) | copy-start | bytes 12582916
  349.5 4.0 copy-start.4
  349.5 4.0 copy-start.5
  372.6 36.8 %copy-start.2 = (bf16[128,32,512]{2,1,0:T(8,128)(2,1)S(1)}, bf16[128,32,512]{2,1,0:T(8,128)(2,1)}, u32[]{:S(2)}) copy-start(bf16[128,32,512]{2,1,0:T(8,128)(2,1)} %copy-done.1) | copy-start | bytes 12582916
  456.7 61.1 %all-to-all-start.7 = ((bf16[128,32,512]{2,0,1:T(8,128)(2,1)}), bf16[128,32,512]{2,0,1:T(8,128)(2,1)}, u32[]{:S(2)}, u32[]{:S(2)}) async-start(bf16[128,32,512]{2,0,1:T(8,128)(2,1)} %copy.60), calls=%async_computation.7 | async-start | bytes 8388608 | tf_op jit(solution)/shard_map/all_to_all | solution.py:79
  517.8 58.5 %all-to-all-start.6 = ((bf16[128,32,512]{2,0,1:T(8,128)(2,1)}), bf16[128,32,512]{2,0,1:T(8,128)(2,1)}, u32[]{:S(2)}, u32[]{:S(2)}) async-start(bf16[128,32,512]{2,0,1:T(8,128)(2,1)} %copy.59), calls=%async_computation.6 | async-start | bytes 8388608 | tf_op jit(solution)/shard_map/all_to_all | solution.py:78
  576.3 58.3 %all-to-all-start.5 = ((bf16[128,32,512]{2,0,1:T(8,128)(2,1)}), bf16[128,32,512]{2,0,1:T(8,128)(2,1)}, u32[]{:S(2)}, u32[]{:S(2)}) async-start(bf16[128,32,512]{2,0,1:T(8,128)(2,1)} %copy.58), calls=%async_computation.5 | async-start | bytes 8388608 | tf_op jit(solution)/shard_map/all_to_all | solution.py:77
  587.6 52.0 %copy-start.10 = (bf16[4096,1,64]{0,2,1:T(8,128)(2,1)S(1)}, bf16[4096,1,64]{0,2,1:T(8,128)(2,1)}, u32[]{:S(2)}) copy-start(bf16[4096,1,64]{0,2,1:T(8,128)(2,1)} %param.12) | copy-start | bytes 1572868
  634.6 58.4 %all-to-all-start.4 = ((bf16[128,32,512]{2,0,1:T(8,128)(2,1)}), bf16[128,32,512]{2,0,1:T(8,128)(2,1)}, u32[]{:S(2)}, u32[]{:S(2)}) async-start(bf16[128,32,512]{2,0,1:T(8,128)(2,1)} %copy.57), calls=%async_computation.4 | async-start | bytes 8388608 | tf_op jit(solution)/shard_map/all_to_all | solution.py:76
  639.5 3.1 copy-start.17
  639.5 74.9 %reduce-scatter.13.cloned.1.call-start = ((), (), s32[]{:S(2)}) async-start(), calls=%async_computation.14 | async-start | bytes 163840
  642.7 4.9 copy-start.13
  651.7 41.3 %copy-start.11 = (bf16[4096,1,32]{0,2,1:T(8,128)(2,1)S(1)}, bf16[4096,1,32]{0,2,1:T(8,128)(2,1)}, u32[]{:S(2)}) copy-start(bf16[4096,1,32]{0,2,1:T(8,128)(2,1)} %param.11) | copy-start | bytes 786436
  655.9 41.0 %copy-start.15 = (bf16[1,128,512]{2,1,0:T(8,128)(2,1)S(1)}, bf16[1,128,512]{2,1,0:T(8,128)(2,1)}, u32[]{:S(2)}) copy-start(bf16[1,128,512]{2,1,0:T(8,128)(2,1)} %param.17) | copy-start | bytes 393220
  696.2 6.1 copy-start.19
  696.9 40.2 %reduce-scatter.15.cloned.1.call-start = ((), (), s32[]{:S(2)}) async-start(), calls=%async_computation.15 | async-start | bytes 163840
  701.4 5.4 copy-start.20
  702.2 57.4 %reduce-scatter.9.cloned.1.call-start = ((), (), s32[]{:S(2)}) async-start(), calls=%async_computation.12 | async-start | bytes 163840 | tf_op jit(solution)/shard_map/reduce_scatter | solution.py:92
  706.7 75.6 %reduce-scatter.11.cloned.1.call-start = ((), (), s32[]{:S(2)}) async-start(), calls=%async_computation.13 | async-start | bytes 327680 | tf_op jit(solution)/shard_map/reduce_scatter | solution.py:95
Sparse Core Ops, SparseCore 0:
  697.0 17.3 reduce-scatter.12
  716.9 20.1 reduce-scatter.14
  739.4 20.1 reduce-scatter.8
  761.9 20.2 reduce-scatter.10
where the time goes:
time: 801 us; the launch traced here: 791 us
  waiting for transfers between devices  332 us (41%)
  local copies, waits for them, and re-layouts  224 us (28%)
  matrix products  109 us (14%)
  other arithmetic  65.3 us (8%)
  starting transfers between devices  46.3 us (6%)
  between operations  14.4 us (2%)
    unnamed x72, local copies, waits for them, and re-layouts  167 us
    all_to_all x1, waiting for transfers between devices, on_device(): lax.all_to_all(pieces[3], 'table', split_axis=1, concat_axis=0, tiled=True)  47 us
    all_to_all x1, waiting for transfers between devices, on_device(): lax.all_to_all(pieces[1], 'table', split_axis=1, concat_axis=0, tiled=True)  47 us
    all_to_all x1, waiting for transfers between devices, on_device(): lax.all_to_all(pieces[2], 'table', split_axis=1, concat_axis=0, tiled=True)  46.9 us
    all_to_all x1, waiting for transfers between devices, on_device(): lax.all_to_all(pieces[0], 'table', split_axis=1, concat_axis=0, tiled=True)  37.1 us
    dot_general x1, matrix products, on_device(): jnp.einsum('rst,rtd->rsd', slot_grad, normed, preferred_element_type=jnp....  36.7 us
    slice x5, local copies, waits for them, and re-layouts, on_device(): pieces = [grad_projected[:, k * ntable:(k + 1) * ntable] for k in range(4)]  35.3 us
    convert_element_type x1, other arithmetic, on_device(): grad_projected = (inv_rms * h - pf * inv_rms ** 3 * jnp.mean(pf * h, axis...  31.5 us
  transfers between devices with their start and end apart: 12, of which 11 were waited for; matrix products, arithmetic and copies ran while one was open for 27% of the time, Pallas kernels for 0%

commit v1 on v0

v1 whole, which is shorter than its diff:
```python
import jax
import jax.numpy as jnp
import numpy as np
from jax import lax
from jax.experimental import pallas as pl
from jax.experimental.pallas import tpu as pltpu
from jax.sharding import Mesh, PartitionSpec as P

F32 = jnp.float32
BF16 = jnp.bfloat16
PLANE = ("z", "x", "c")
MIB = 1024 * 1024
ROWS = 224
GROUP = 8
UNROLL = 8


def dot(a, b, dims=((1,), (0,))):
    return lax.dot_general(a, b, (dims, ((), ())), preferred_element_type=F32)


def owner_forward_body(at_ref, bt_ref, c_ref, d_ref, wd_ref, u_ref):
    rows, width = c_ref.shape[0], wd_ref.shape[1]
    narrow = jnp.concatenate(
        [bt_ref[...], at_ref[...], jnp.zeros((32, rows), BF16)], axis=0
    )
    u_ref[:, 0:width] = dot(d_ref[...], wd_ref[...]).astype(BF16)
    u_ref[:, width : width + 128] = c_ref[...]
    u_ref[:, width + 128 : width + 256] = narrow.T


def owner_forward(at, bt, c, d, wd, rows=512):
    total, width = c.shape[0], wd.shape[1]
    return pl.pallas_call(
        owner_forward_body,
        grid=(total // rows,),
        in_specs=[
            pl.BlockSpec((at.shape[0], rows), lambda i: (0, i)),
            pl.BlockSpec((bt.shape[0], rows), lambda i: (0, i)),
            pl.BlockSpec((rows, c.shape[1]), lambda i: (i, 0)),
            pl.BlockSpec((rows, d.shape[1]), lambda i: (i, 0)),
            pl.BlockSpec(wd.shape, lambda i: (0, 0)),
        ],
        out_specs=pl.BlockSpec((rows, width + 256), lambda i: (i, 0)),
        out_shape=jax.ShapeDtypeStruct((total, width + 256), BF16),
        compiler_params=pltpu.CompilerParams(vmem_limit_bytes=40 * MIB),
        cost_estimate=pl.CostEstimate(
            flops=2 * total * 256 * width, bytes_accessed=total * 2 * (480 + 768), transcendentals=0
        ),
        name="owner_forward",
    )(at, bt, c, d, wd)


def padded_weights(w):
    zeros = lambda n: jnp.zeros((n, w.shape[1]), w.dtype)
    wc = w[0:128]
    wb = jnp.concatenate([w[128:192], zeros(64)], axis=0)
    wa = jnp.concatenate([zeros(64), w[192:224], zeros(32)], axis=0)
    return wa, wb, wc


def middle_body(
    steps, at_ref, table_ref, gain_ref, pd_ref, x_ref, w00, w01, w02, w03, w10, w11, w12, w13,
    g_ref, gu_ref, v00, v01, v02, v03, v10, v11, v12, v13, scr, nrm, acc,
):
    i = pl.program_id(0)
    nb = x_ref.shape[1]
    ns = nb + 1
    width = gain_ref.shape[1]
    lanes = range(width // 128)
    plane = 128 * ns
    weights = ((w00, w01, w02, w03), (w10, w11, w12, w13))
    weight_grads = ((v00, v01, v02, v03), (v10, v11, v12, v13))
    z, x, core = at_ref[0], at_ref[1], at_ref[2]

    def put(slot, value):
        start = table_ref[slot] * ns
        for q in lanes:
            scr[pl.ds(q * plane + start, nb), :] = value[:, q * 128 : (q + 1) * 128]

    def take(slot):
        start = table_ref[slot] * ns
        pieces = [scr[pl.ds(q * plane + start, nb), :].astype(BF16) for q in lanes]
        return jnp.concatenate(pieces, axis=1)

    def strided(q, r, b):
        return pl.ds(q * plane + r * ns + b, 32, stride=ns)

    def tables(dz):
        zabs = lax.rem(z - dz + 4, 4)
        for dx in range(4):
            for side in range(2):
                t = lax.rem(x - dx + 4, 4) * 2 + lax.rem(core + side, 2)
                w = jnp.concatenate([weights[side][q][dx] for q in lanes], axis=1)
                yield dx, side, t, zabs * GROUP + t, padded_weights(w)

    @pl.when(i < 4)
    def _():
        for dx, side, t, j, (wa, wb, wc) in tables(i):
            xc = x_ref[t, :, 0:128]
            xn = x_ref[t, :, 128:256]
            put(j, dot(xn, wa).astype(BF16).astype(F32))
            put(32 + j, dot(xn, wb).astype(BF16).astype(F32))
            put(64 + j, dot(xc, wc).astype(BF16).astype(F32))
            put(96 + j, pd_ref[t].astype(F32))

    @pl.when((i >= 4) & (i < 4 + steps))
    def _():
        per = g_ref.shape[0]
        gain = gain_ref[...]
        scaled = gain * (1.0 / np.sqrt(width).astype(np.float32))
        base = (i - 4) * per

        def one(s, u):
            b = base + s
            for r in range(0, 128, 32):
                pf = jnp.concatenate([scr[strided(q, r, b), :] for q in lanes], axis=1)
                inv = lax.rsqrt(jnp.sum(pf * pf, axis=1, keepdims=True) * (1.0 / width) + 1e-06)
                nrm[u, r : r + 32, :] = (pf * inv * gain).astype(BF16)
            g = g_ref[s]
            n = nrm[u]
            acc[u] = dot(jnp.concatenate([g, g.T], axis=1), jnp.concatenate([n, n], axis=0))
            for r in range(0, 128, 32):
                pf = jnp.concatenate([scr[strided(q, r, b), :] for q in lanes], axis=1)
                h = acc[u, r : r + 32, :] * scaled
                inv = lax.rsqrt(jnp.sum(pf * pf, axis=1, keepdims=True) * (1.0 / width) + 1e-06)
                m = jnp.sum(pf * h, axis=1, keepdims=True) * (1.0 / width)
                out = inv * h - pf * (inv * inv * inv * m)
                for q in lanes:
                    scr[strided(q, r, b), :] = out[:, q * 128 : (q + 1) * 128]

        def several(v, carry):
            for u in range(UNROLL):
                one(v * UNROLL + u, u)
            return carry

        lax.fori_loop(0, per // UNROLL, several, 0)

    @pl.when(i >= 4 + steps)
    def _():
        last, first = ((1,), (1,)), ((0,), (0,))
        for dx, side, t, j, (wa, wb, wc) in tables(i - 4 - steps):
            xc = x_ref[t, :, 0:128]
            xn = x_ref[t, :, 128:256]
            ga, gb, gc = take(j), take(32 + j), take(64 + j)
            gu_ref[t, :, 0:width] = take(96 + j)
            gu_ref[t, :, width : width + 128] = dot(gc, wc, last).astype(BF16)
            gu_ref[t, :, width + 128 : width + 256] = (
                dot(ga, wa, last) + dot(gb, wb, last)
            ).astype(BF16)
            vc = dot(xc, gc, first).astype(BF16)
            vb = dot(xn, gb, first)[0:64].astype(BF16)
            va = dot(xn, ga, first)[64:96].astype(BF16)
            for q in lanes:
                part = slice(q * 128, (q + 1) * 128)
                weight_grads[side][q][dx, 0:128, :] = vc[:, part]
                weight_grads[side][q][dx, 128:192, :] = vb[:, part]
                weight_grads[side][q][dx, 192:224, :] = va[:, part]


def middle(at, table, gain, u, ws, g, per=16):
    ntab, nb, full = u.shape
    width = gain.shape[1]
    steps = nb // per

    def turn(i):
        return jnp.where(i < 4, i, jnp.where(i < 4 + steps, 3, i - 4 - steps))

    def by_table(i, at):
        return lax.rem(at[0] - turn(i) + 4, 4)

    def forward_only(i, at):
        return lax.rem(at[0] - jnp.minimum(i, 3) + 4, 4)

    def late(i):
        return jnp.maximum(i - 4 - steps, 0)

    def backward_only(i, at):
        return lax.rem(at[0] - late(i) + 4, 4)

    weight_in = pl.BlockSpec((4, ROWS, 128), lambda i, at, tb: (turn(i), 0, 0))
    weight_out = pl.BlockSpec((4, ROWS, 128), lambda i, at, tb: (late(i), 0, 0))
    return pl.pallas_call(
        lambda *refs: middle_body(steps, *refs),
        grid_spec=pltpu.PrefetchScalarGridSpec(
            num_scalar_prefetch=2,
            grid=(8 + steps,),
            in_specs=[
                pl.BlockSpec((1, width), lambda i, at, tb: (0, 0)),
                pl.BlockSpec((GROUP, nb, width), lambda i, at, tb: (forward_only(i, at), 0, 0)),
                pl.BlockSpec(
                    (GROUP, nb, 256), lambda i, at, tb: (by_table(i, at), 0, width // 256)
                ),
            ]
            + [weight_in] * 8
            + [
                pl.BlockSpec(
                    (per, 128, 128), lambda i, at, tb: (jnp.clip(i - 4, 0, steps - 1), 0, 0)
                ),
            ],
            out_specs=[
                pl.BlockSpec((GROUP, nb, full), lambda i, at, tb: (backward_only(i, at), 0, 0)),
            ]
            + [weight_out] * 8,
            scratch_shapes=[
                pltpu.VMEM((width * (nb + 1), 128), F32),
                pltpu.VMEM((UNROLL, 128, width), BF16),
                pltpu.VMEM((UNROLL, 128, width), F32),
            ],
        ),
        out_shape=[jax.ShapeDtypeStruct((ntab, nb, full), BF16)]
        + [jax.ShapeDtypeStruct((16, ROWS, 128), BF16)] * 8,
        compiler_params=pltpu.CompilerParams(vmem_limit_bytes=58 * MIB),
        cost_estimate=pl.CostEstimate(
            flops=15 * 10**9, bytes_accessed=40 * 10**6, transcendentals=0
        ),
        name="middle",
    )(at, table, gain, u, u, *ws, g)


def owner_backward_body(
    gp_ref, gx_ref, d_ref, wd_ref, gat_ref, gbt_ref, gc_ref, gd_ref, gw_ref, acc
):
    i = pl.program_id(0)
    gc_ref[...] = gx_ref[:, 0:128]
    narrow = gx_ref[:, 128:256].T
    gbt_ref[...] = narrow[0:64]
    gat_ref[...] = narrow[64:96]
    gp = gp_ref[...]
    gd_ref[...] = dot(gp, wd_ref[...], ((1,), (1,))).astype(BF16)

    @pl.when(i == 0)
    def _():
        acc[...] = jnp.zeros_like(acc)

    acc[...] += dot(d_ref[...], gp, ((0,), (0,)))

    @pl.when(i == pl.num_programs(0) - 1)
    def _():
        gw_ref[...] = acc[...].astype(BF16)


def owner_backward(gu, d, wd, rows=512):
    total = gu.shape[0]
    wdim, width = wd.shape
    return pl.pallas_call(
        owner_backward_body,
        grid=(total // rows,),
        in_specs=[
            pl.BlockSpec((rows, width), lambda i: (i, 0)),
            pl.BlockSpec((rows, 256), lambda i: (i, width // 256)),
            pl.BlockSpec((rows, wdim), lambda i: (i, 0)),
            pl.BlockSpec(wd.shape, lambda i: (0, 0)),
        ],
        out_specs=[
            pl.BlockSpec((32, rows), lambda i: (0, i)),
            pl.BlockSpec((64, rows), lambda i: (0, i)),
            pl.BlockSpec((rows, 128), lambda i: (i, 0)),
            pl.BlockSpec((rows, wdim), lambda i: (i, 0)),
            pl.BlockSpec((wdim, width), lambda i: (0, 0)),
        ],
        out_shape=[
            jax.ShapeDtypeStruct((32, total), BF16),
            jax.ShapeDtypeStruct((64, total), BF16),
            jax.ShapeDtypeStruct((total, 128), BF16),
            jax.ShapeDtypeStruct((total, wdim), BF16),
            jax.ShapeDtypeStruct((wdim, width), BF16),
        ],
        scratch_shapes=[pltpu.VMEM((wdim, width), F32)],
        compiler_params=pltpu.CompilerParams(vmem_limit_bytes=40 * MIB),
        cost_estimate=pl.CostEstimate(
            flops=4 * total * wdim * width, bytes_accessed=total * 2 * 1500, transcendentals=0
        ),
        name="owner_backward",
    )(gu, gu, d, wd)


def exchange(x):
    return lax.all_to_all(x, PLANE, split_axis=0, concat_axis=0, tiled=True)


def shift(x, axis, k):
    n = lax.axis_size(axis)
    return lax.ppermute(x, axis, [(i, (i + k) % n) for i in range(n)])


def add(*parts):
    total = parts[0].astype(F32)
    for p in parts[1:]:
        total = total + p.astype(F32)
    return total


def turn_features(w, y):
    blocks = w.reshape(w.shape[0], 4, 128)
    order = lax.rem(y - jnp.arange(4) + 4, 4)
    return jnp.take(blocks, order, axis=1).reshape(w.shape)


def gather_plane(w, y):
    part = lax.dynamic_slice_in_dim(w, y * 128, 128, axis=1)
    part = jnp.stack([part, shift(part, "x", 1), shift(part, "x", 2), shift(part, "x", -1)])
    return jnp.concatenate([part, shift(part, "z", 1), shift(part, "z", 2), shift(part, "z", -1)])


def gather_quarters(part):
    below, above = shift(part, "y", 1), shift(part, "y", -1)
    far = jnp.concatenate([shift(below[:8], "y", 1), shift(above[8:], "y", -1)])
    own = (part, below, far, above)
    return own + tuple(shift(p, "c", 1) for p in own)


def scatter_weight_grads(own, other):
    s = [add(o, shift(p, "c", 1)).astype(BF16) for o, p in zip(own, other)]
    from_above, from_below = shift(s[2][:8], "y", -1), shift(s[2][8:], "y", 1)
    down = jnp.concatenate([add(s[1][:8], from_above).astype(BF16), s[1][8:]])
    up = jnp.concatenate([s[3][:8], add(s[3][8:], from_below).astype(BF16)])
    part = add(s[0], shift(down, "y", -1), shift(up, "y", 1)).astype(BF16)
    for axis in ("z", "x"):
        n = part.shape[0] // 4
        part = add(
            part[:n],
            shift(part[n : 2 * n], axis, -1),
            shift(part[2 * n : 3 * n], axis, -2),
            shift(part[3 * n :], axis, -3),
        ).astype(BF16)
    return part[0]


def on_device(
    pooled_a, pooled_b, pooled_c, pooled_d, proj_a, proj_b, proj_c, proj_d,
    slot_table, norm_gain, grad_gram,
):
    total = pooled_a.shape[0]
    nb = grad_gram.shape[0]
    owners = total // nb
    y = lax.axis_index("y")
    at = jnp.stack([lax.axis_index("z"), lax.axis_index("x"), lax.axis_index("c")]).astype(jnp.int32)
    wd = turn_features(proj_d[0], y)
    gain = turn_features(norm_gain[None], y)
    d = pooled_d[:, 0]
    part = gather_plane(jnp.concatenate([proj_c[0], proj_b[0], proj_a[0]], axis=0), y)
    u = owner_forward(
        pooled_a.transpose(1, 2, 0)[0], pooled_b.transpose(1, 2, 0)[0], pooled_c[:, 0], d, wd
    )
    u, part = lax.optimization_barrier((u, part))
    ws = gather_quarters(part)
    u = exchange(u.reshape(owners, nb, -1))
    gu, *gws = middle(at, slot_table, gain, u, ws, grad_gram)
    gu = exchange(gu).reshape(total, -1)
    gat, gbt, gc, gd, gwd = owner_backward(gu, d, wd)
    scale = 1.0 / np.sqrt(total * lax.axis_size("y")).astype(np.float32)
    gw = scatter_weight_grads(gws[:4], gws[4:]).astype(F32) * scale
    q = [gwd[:, r * 128 : (r + 1) * 128] for r in range(4)]
    gwd = add(q[0], shift(q[1], "y", -1), shift(q[2], "y", -2), shift(q[3], "y", -3)) * scale
    return (
        gat.T[:, None],
        gbt.T[:, None],
        gc[:, None],
        gd[:, None],
        gw[192:224][None],
        gw[128:192][None],
        gw[0:128][None],
        gwd[None],
    )


def solution(mesh):
    fine = Mesh(np.array(mesh.devices).reshape(4, 4, 4, 2), ("y", "z", "x", "c"))
    pooled = P("y", PLANE, None)
    weight = P(PLANE, None, None)
    in_specs = (pooled,) * 4 + (weight,) * 4 + (P(), P(), P(("y",) + PLANE, None, None))
    out_specs = (pooled,) * 4 + (P(PLANE, None, "y"),) * 4
    return jax.shard_map(
        on_device, mesh=fine, in_specs=in_specs, out_specs=out_specs, check_vma=False
    )
```

time: 801 us -> 276 us (0.34); the launches traced: 791 us -> 274 us
  local copies, waits for them, and re-layouts: 224 us -> 13.4 us
  waiting for transfers between devices: 332 us -> 147 us
  matrix products: 109 us -> 0 us
  other arithmetic: 65.3 us -> 5.39 us
  Pallas kernels: 0 us -> 55.4 us
  between operations: 14.4 us -> 1.04 us
    all_to_all x8 -> x2, waiting for transfers between devices: 265 us -> 36.3 us  [exchange(): return lax.all_to_all(x, PLANE, split_axis=0, concat_axis=0, tiled=True)]
    unnamed x72 -> x36, local copies, waits for them, and re-layouts: 167 us -> 8 us
    ppermute x0 -> x31, waiting for transfers between devices: none -> 110 us  [shift(): return lax.ppermute(x, axis, [(i, (i + k) % n) for i in range(n)])]
    dot_general x15 -> x0, matrix products: 109 us -> none  [the longest x1 36.7 us: on_device(): jnp.einsum('rst,rtd->rsd', slot_grad, normed, preferred_element_type=jnp....]
    convert_element_type x5 -> x7, other arithmetic: 58.5 us -> 1.62 us  [the longest x3 0.78 us: scatter_weight_grads(): s = [add(o, shift(p, 'c', 1)).astype(BF16) for o, p in zip(own, other)]]
    pallas_call x0 -> x3, Pallas kernels: none -> 55.4 us  [the longest x1 42.2 us: middle(): pl.pallas_call(lambda *refs: middle_body(steps, *refs), grid_spec=pltpu.P...]
    ppermute x0 -> x31, starting transfers between devices: none -> 42.4 us  [shift(): return lax.ppermute(x, axis, [(i, (i + k) % n) for i in range(n)])]
    reduce_scatter x2 -> x0, waiting for transfers between devices: 42.2 us -> none  [the longest x1 21.2 us: on_device(): lax.psum_scatter(weight_d.astype(jnp.bfloat16), 'dp', scatter_dimension=2...]
  transfers between devices with their start and end apart: 12 -> 33, of which waited for: 11 -> 12; matrix products, arithmetic and copies ran while one was open for 27% -> 4% of each run, Pallas kernels for 0% -> 5%
where the time goes in v1:
time: 276 us; the launch traced here: 274 us
  waiting for transfers between devices  147 us (53%)
  Pallas kernels  55.4 us (20%)
  starting transfers between devices  52.3 us (19%)
  local copies, waits for them, and re-layouts  13.4 us (5%)
  other arithmetic  5.39 us (2%)
    ppermute x31, waiting for transfers between devices, shift(): return lax.ppermute(x, axis, [(i, (i + k) % n) for i in range(n)])  110 us
    ppermute x31, starting transfers between devices, shift(): return lax.ppermute(x, axis, [(i, (i + k) % n) for i in range(n)])  42.4 us
    pallas_call x1, Pallas kernels, middle(): pl.pallas_call(lambda *refs: middle_body(steps, *refs), grid_spec=pltpu.P...  42.2 us
    all_to_all x2, waiting for transfers between devices, exchange(): return lax.all_to_all(x, PLANE, split_axis=0, concat_axis=0, tiled=True)  36.3 us
    pallas_call x1, Pallas kernels, owner_backward(): pl.pallas_call(owner_backward_body, grid=(total // rows,), in_specs=[pl.B...  10.7 us
    all_to_all x2, starting transfers between devices, exchange(): return lax.all_to_all(x, PLANE, split_axis=0, concat_axis=0, tiled=True)  9.94 us
    unnamed x36, local copies, waits for them, and re-layouts  8 us
  transfers between devices with their start and end apart: 33, of which 12 were waited for; matrix products, arithmetic and copies ran while one was open for 4% of the time, Pallas kernels for 5%

profile of v1, /device:TPU:0, one launch (start us, length us, event | category | flops | bytes accessed | tf_op | source)
XLA Modules:
  0.0 274.1 jit_solution(12864760339873648526)
XLA Ops:
  0.7 1.6 constant_dynamic-update-slice_fusion.6
  2.3 3.1 %collective-permute-start.1 = (bf16[224,128]{1,0:T(8,128)(2,1)S(1)}, bf16[224,128]{1,0:T(8,128)(2,1)S(1)}, u32[]{:S(2)}, u32[]{:S(2)}) collective-permute-start(bf16[224,128]{1,0:T(8,128)(2,1)S(1)} %get-tuple-element.41), channel_id=1, source_target_pairs={{0,4},{2,6},{4,0},{6,2},{1,5},{3,7},{5,1},{7,3},{8,12},{10,14},{12... | collective-permute-start | bytes 172040 | tf_op jit(solution)/shard_map/ppermute | solution.py:284
  5.4 0.6 collective-permute-start
  6.0 2.6 collective-permute-start.2
  8.7 1.1 copy.20
  10.0 0.6 gather_fusion.1
  10.7 1.2 copy-done.4
  11.9 1.0 copy-done.5
  12.9 2.5 owner_forward.1
  15.5 2.7 copy-done.2
  18.2 4.1 %collective-permute-start.5 = (bf16[4,224,128]{2,1,0:T(8,128)(2,1)S(1)}, bf16[4,224,128]{2,1,0:T(8,128)(2,1)S(1)}, u32[]{:S(2)}, u32[]{:S(2)}) collective-permute-start(bf16[4,224,128]{2,1,0:T(8,128)(2,1)S(1)} %pad_maximum_fusion.2), channel_id=1, source_target_pairs={{0,24},{8,0},{16,8},{24,16},{1,25},{9,1},{17,9},{25,17},{2,26},{10... | collective-permute-start | bytes 688136 | tf_op jit(solution)/shard_map/ppermute | solution.py:284
  22.3 1.3 collective-permute-start.3
  23.6 11.0 %collective-permute-done.3 = bf16[4,224,128]{2,1,0:T(8,128)(2,1)S(1)} collective-permute-done((bf16[4,224,128]{2,1,0:T(8,128)(2,1)S(1)}, bf16[4,224,128]{2,1,0:T(8,128)(2,1)S(1)}, u32[]{:S(2)}, u32[]{:S(2)}) %collective-permute-start.3) | collective-permute-done | bytes 229408 | tf_op jit(solution)/shard_map/ppermute | solution.py:284
  34.8 0.9 copy-done.13
  35.7 4.9 %all-to-all-start = ((bf16[32,128,768]{2,1,0:T(8,128)(2,1)}), bf16[32,128,768]{2,1,0:T(8,128)(2,1)}, u32[]{:S(2)}, u32[]{:S(2)}) async-start(bf16[32,128,768]{2,1,0:T(8,128)(2,1)} %bitcast.53), calls=%async_computation | async-start | bytes 12582912 | tf_op jit(solution)/shard_map/all_to_all | solution.py:279
  40.7 1.6 collective-permute-start.6
  42.3 1.7 collective-permute-start.8
  44.0 20.6 %collective-permute-done.6.refs_6_ = bf16[16,224,128]{2,1,0:T(8,128)(2,1)S(1)} collective-permute-done((bf16[16,224,128]{2,1,0:T(8,128)(2,1)}, bf16[16,224,128]{2,1,0:T(8,128)(2,1)S(1)}, u32[]{:S(2)}, u32[]{:S(2)}) %collective-permute-start.6) | collective-permute-done | bytes 917536 | tf_op jit(solution)/shard_map/ppermute | solution.py:284
  65.0 1.0 slice.100
  66.0 3.0 %collective-permute-start.9 = (bf16[8,224,128]{2,1,0:T(8,128)(2,1)S(1)}, bf16[8,224,128]{2,1,0:T(8,128)(2,1)S(1)}, u32[]{:S(2)}, u32[]{:S(2)}) collective-permute-start(bf16[8,224,128]{2,1,0:T(8,128)(2,1)S(1)} %slice.100), channel_id=1, source_target_pairs={{0,96},{32,0},{64,32},{96,64},{1,97},{33,1},{65,33},{97,65},{2,98}... | collective-permute-start | bytes 1376264 | tf_op jit(solution)/shard_map/ppermute | solution.py:284
  69.5 8.2 %collective-permute-done.7 = bf16[8,224,128]{2,1,0:T(8,128)(2,1)S(1)} collective-permute-done((bf16[8,224,128]{2,1,0:T(8,128)(2,1)S(1)}, bf16[8,224,128]{2,1,0:T(8,128)(2,1)S(1)}, u32[]{:S(2)}, u32[]{:S(2)}) %collective-permute-start.7) | collective-permute-done | bytes 458784 | tf_op jit(solution)/shard_map/ppermute | solution.py:284
  77.7 0.8 constant_dynamic-update-slice_fusion.8
  78.6 0.8 constant_dynamic-update-slice_fusion.7.refs_7_
  80.0 0.6 pad_add_fusion.refs_0_
  81.2 1.0 collective-permute-done.12.refs_11_
  82.2 36.3 %all-to-all-done.refs_3_.refs_4_ = bf16[32,128,768]{2,1,0:T(8,128)(2,1)} async-done(((bf16[32,128,768]{2,1,0:T(8,128)(2,1)}), bf16[32,128,768]{2,1,0:T(8,128)(2,1)}, u32[]{:S(2)}, u32[]{:S(2)}) %all-to-all-start) | async-done | bytes 6291488 | tf_op jit(solution)/shard_map/all_to_all | solution.py:279
  118.6 42.2 %middle.1 = (bf16[32,128,768]{2,1,0:T(8,128)(2,1)}, bf16[16,224,128]{2,1,0:T(8,128)(2,1)}, bf16[16,224,128]{2,1,0:T(8,128)(2,1)}, bf16[16,224,128]{2,1,0:T(8,128...) custom-call(s32[3]{0:T(128)} %pad_add_fusion.refs_0_, ...), custom_call_target="tpu_custom_call" | custom-call | flops 15000000512 | bytes 40000000 | tf_op jit(solution)/shard_map/middle/pallas_call | solution.py:183
  160.8 5.0 %all-to-all-start.1 = ((bf16[32,128,768]{2,1,0:T(8,128)(2,1)}), bf16[32,128,768]{2,1,0:T(8,128)(2,1)}, u32[]{:S(2)}, u32[]{:S(2)}) async-start(bf16[32,128,768]{2,1,0:T(8,128)(2,1)} %get-tuple-element.26), calls=%async_computation.1 | async-start | bytes 12582912 | tf_op jit(solution)/shard_map/all_to_all | solution.py:279
  166.9 1.7 collective-permute-done.16
  169.0 3.1 %collective-permute-start.17 = (bf16[8,224,128]{2,1,0:T(8,128)(2,1)S(1)}, bf16[8,224,128]{2,1,0:T(8,128)(2,1)S(1)}, u32[]{:S(2)}, u32[]{:S(2)}) collective-permute-start(bf16[8,224,128]{2,1,0:T(8,128)(2,1)S(1)} %get-tuple-element.45), channel_id=1, source_target_pairs={{0,96},{32,0},{64,32},{96,64},{1,97},{33,1},{65,33},{97,65},{2,98}... | collective-permute-start | bytes 1376264 | tf_op jit(solution)/shard_map/ppermute | solution.py:284
  172.7 9.5 %collective-permute-done.17 = bf16[8,224,128]{2,1,0:T(8,128)(2,1)S(1)} collective-permute-done((bf16[8,224,128]{2,1,0:T(8,128)(2,1)S(1)}, bf16[8,224,128]{2,1,0:T(8,128)(2,1)S(1)}, u32[]{:S(2)}, u32[]{:S(2)}) %collective-permute-start.17) | collective-permute-done | bytes 458784 | tf_op jit(solution)/shard_map/ppermute | solution.py:284
  182.4 3.8 %collective-permute-start.18 = (bf16[16,224,128]{2,1,0:T(8,128)(2,1)S(1)}, bf16[16,224,128]{2,1,0:T(8,128)(2,1)S(1)}, u32[]{:S(2)}, u32[]{:S(2)}) collective-permute-start(bf16[16,224,128]{2,1,0:T(8,128)(2,1)S(1)} %pad_maximum_fusion), channel_id=1, source_target_pairs={{0,96},{32,0},{64,32},{96,64},{1,97},{33,1},{65,33},{97,65},{2,98}... | collective-permute-start | bytes 2752520 | tf_op jit(solution)/shard_map/ppermute | solution.py:284
  186.4 18.9 %collective-permute-done.18 = bf16[16,224,128]{2,1,0:T(8,128)(2,1)S(1)} collective-permute-done((bf16[16,224,128]{2,1,0:T(8,128)(2,1)S(1)}, bf16[16,224,128]{2,1,0:T(8,128)(2,1)S(1)}, u32[]{:S(2)}, u32[]{:S(2)}) %collective-permute-start.18) | collective-permute-done | bytes 917536 | tf_op jit(solution)/shard_map/ppermute | solution.py:284
  205.3 3.7 %collective-permute-done.21 = bf16[16,224,128]{2,1,0:T(8,128)(2,1)S(1)} collective-permute-done((bf16[16,224,128]{2,1,0:T(8,128)(2,1)S(1)}, bf16[16,224,128]{2,1,0:T(8,128)(2,1)S(1)}, u32[]{:S(2)}, u32[]{:S(2)}) %collective-permute-start.21) | collective-permute-done | bytes 917536 | tf_op jit(solution)/shard_map/ppermute | solution.py:284
  209.6 3.1 %collective-permute-start.22 = (bf16[4,224,128]{2,1,0:T(8,128)(2,1)S(1)}, bf16[4,224,128]{2,1,0:T(8,128)(2,1)S(1)}, u32[]{:S(2)}, u32[]{:S(2)}) collective-permute-start(bf16[4,224,128]{2,1,0:T(8,128)(2,1)S(1)} %get-tuple-element.42), channel_id=1, source_target_pairs={{0,24},{8,0},{16,8},{24,16},{1,25},{9,1},{17,9},{25,17},{2,26},{10... | collective-permute-start | bytes 688136 | tf_op jit(solution)/shard_map/ppermute | solution.py:284
  212.6 2.3 collective-permute-start.23
  214.9 28.3 %collective-permute-done.22 = bf16[4,224,128]{2,1,0:T(8,128)(2,1)S(1)} collective-permute-done((bf16[4,224,128]{2,1,0:T(8,128)(2,1)S(1)}, bf16[4,224,128]{2,1,0:T(8,128)(2,1)S(1)}, u32[]{:S(2)}, u32[]{:S(2)}) %collective-permute-start.22) | collective-permute-done | bytes 229408 | tf_op jit(solution)/shard_map/ppermute | solution.py:284
  243.2 5.3 %collective-permute-done.23 = bf16[4,224,128]{2,1,0:T(8,128)(2,1)S(1)} collective-permute-done((bf16[4,224,128]{2,1,0:T(8,128)(2,1)S(1)}, bf16[4,224,128]{2,1,0:T(8,128)(2,1)S(1)}, u32[]{:S(2)}, u32[]{:S(2)}) %collective-permute-start.23) | collective-permute-done | bytes 229408 | tf_op jit(solution)/shard_map/ppermute | solution.py:284
  248.7 3.1 %collective-permute-start.25 = (bf16[1,224,128]{2,1,0:T(8,128)(2,1)S(1)}, bf16[1,224,128]{2,1,0:T(8,128)(2,1)S(1)}, u32[]{:S(2)}, u32[]{:S(2)}) collective-permute-start(bf16[1,224,128]{2,1,0:T(8,128)(2,1)S(1)} %get-tuple-element.50), channel_id=1, source_target_pairs={{0,6},{2,0},{4,2},{6,4},{1,7},{3,1},{5,3},{7,5},{8,14},{10,8},{12,... | collective-permute-start | bytes 172040 | tf_op jit(solution)/shard_map/ppermute | solution.py:284
  251.8 1.5 collective-permute-start.26
  253.3 10.7 %owner_backward.1 = (bf16[32,4096]{1,0:T(8,128)(2,1)}, bf16[64,4096]{1,0:T(8,128)(2,1)}, bf16[4096,128]{1,0:T(8,128)(2,1)}, bf16[4096,256]{1,0:T(8,128)(2,1)}, bf16[256,512]{1,0:T(8,128)(2,1)S(1)}) custom-call(bf16[4096,768]{1,0:T(8,128)(2,1)} %bitcast.23.gp_ref.gx_ref, bf16[4096,768]{1,0:T(8,128)(2,1)} %bitcast.23.gp_ref.gx_ref, ...), custom_call_target="tpu_custom_call" | custom-call | flops 2147483648 | bytes 12288000 | tf_op jit(solution)/shard_map/owner_backward/pallas_call | solution.py:246
  264.1 3.2 %collective-permute-start.28 = (bf16[256,128]{1,0:T(8,128)(2,1)S(1)}, bf16[256,128]{1,0:T(8,128)(2,1)S(1)}, u32[]{:S(2)}, u32[]{:S(2)}) collective-permute-start(bf16[256,128]{1,0:T(8,128)(2,1)S(1)} %get-tuple-element.47), channel_id=1, source_target_pairs={{0,96},{32,0},{64,32},{96,64},{1,97},{33,1},{65,33},{97,65},{2,98}... | collective-permute-start | bytes 196616 | tf_op jit(solution)/shard_map/ppermute | solution.py:284
  267.3 2.2 collective-permute-start.29
  269.5 0.6 slice.115
  270.1 0.6 slice.116
  270.8 0.6 slice.117
  271.4 2.1 collective-permute-done.30
  273.4 0.7 multiply_bitcast_fusion
  (93 shorter events, 6.0 us)
Async XLA Ops:
  0.6 78.8 %copy-start = (f32[512]{0:T(512)S(1)}, f32[512]{0:T(512)}, u32[]{:S(2)}) copy-start(f32[512]{0:T(512)} %param.20) | copy-start | bytes 6148
  0.7 10.0 %copy-start.3 = (bf16[4096,1,256]{2,0,1:T(8,128)(2,1)S(1)}, bf16[4096,1,256]{2,0,1:T(8,128)(2,1)}, u32[]{:S(2)}) copy-start(bf16[4096,1,256]{2,0,1:T(8,128)(2,1)} %param.14) | copy-start | bytes 6291460
  0.7 10.0 %copy-start.6 = (bf16[4096,1,32]{0,2,1:T(8,128)(2,1)S(1)}, bf16[4096,1,32]{0,2,1:T(8,128)(2,1)}, u32[]{:S(2)}) copy-start(bf16[4096,1,32]{0,2,1:T(8,128)(2,1)} %param.11) | copy-start | bytes 786436
  2.3 15.9 %collective-permute-start.1 = (bf16[224,128]{1,0:T(8,128)(2,1)S(1)}, bf16[224,128]{1,0:T(8,128)(2,1)S(1)}, u32[]{:S(2)}, u32[]{:S(2)}) collective-permute-start(bf16[224,128]{1,0:T(8,128)(2,1)S(1)} %get-tuple-element.41), channel_id=1, source_target_pairs={{0,4},{2,6},{4,0},{6,2},{1,5},{3,7},{5,1},{7,3},{8,12},{10,14},{12... | collective-permute-start | bytes 172040 | tf_op jit(solution)/shard_map/ppermute | solution.py:284
  5.4 12.8 %collective-permute-start = (bf16[224,128]{1,0:T(8,128)(2,1)S(1)}, bf16[224,128]{1,0:T(8,128)(2,1)S(1)}, u32[]{:S(2)}, u32[]{:S(2)}) collective-permute-start(bf16[224,128]{1,0:T(8,128)(2,1)S(1)} %get-tuple-element.41), channel_id=1, source_target_pairs={{0,2},{2,4},{4,6},{6,0},{1,3},{3,5},{5,7},{7,1},{8,10},{10,12},{12... | collective-permute-start | bytes 172040 | tf_op jit(solution)/shard_map/ppermute | solution.py:284
  6.0 12.2 %collective-permute-start.2 = (bf16[224,128]{1,0:T(8,128)(2,1)S(1)}, bf16[224,128]{1,0:T(8,128)(2,1)S(1)}, u32[]{:S(2)}, u32[]{:S(2)}) collective-permute-start(bf16[224,128]{1,0:T(8,128)(2,1)S(1)} %get-tuple-element.41), channel_id=1, source_target_pairs={{0,6},{2,0},{4,2},{6,4},{1,7},{3,1},{5,3},{7,5},{8,14},{10,8},{12,... | collective-permute-start | bytes 172040 | tf_op jit(solution)/shard_map/ppermute | solution.py:284
  10.7 1.2 copy-start.4
  11.9 1.0 copy-start.5
  12.9 10.6 %copy-start.12 = (bf16[16,224,128]{2,1,0:T(8,128)(2,1)S(1)}, bf16[16,224,128]{2,1,0:T(8,128)(2,1)}, u32[]{:S(2)}) copy-start(bf16[16,224,128]{2,1,0:T(8,128)(2,1)} %get-tuple-element.40) | copy-start | bytes 2752516
  15.5 2.7 copy-start.2
  18.2 16.5 %collective-permute-start.5 = (bf16[4,224,128]{2,1,0:T(8,128)(2,1)S(1)}, bf16[4,224,128]{2,1,0:T(8,128)(2,1)S(1)}, u32[]{:S(2)}, u32[]{:S(2)}) collective-permute-start(bf16[4,224,128]{2,1,0:T(8,128)(2,1)S(1)} %pad_maximum_fusion.2), channel_id=1, source_target_pairs={{0,24},{8,0},{16,8},{24,16},{1,25},{9,1},{17,9},{25,17},{2,26},{10... | collective-permute-start | bytes 688136 | tf_op jit(solution)/shard_map/ppermute | solution.py:284
  22.3 12.4 %collective-permute-start.4 = (bf16[4,224,128]{2,1,0:T(8,128)(2,1)S(1)}, bf16[4,224,128]{2,1,0:T(8,128)(2,1)S(1)}, u32[]{:S(2)}, u32[]{:S(2)}) collective-permute-start(bf16[4,224,128]{2,1,0:T(8,128)(2,1)S(1)} %pad_maximum_fusion.2), channel_id=1, source_target_pairs={{0,16},{8,24},{16,0},{24,8},{1,17},{9,25},{17,1},{25,9},{2,18},{10... | collective-permute-start | bytes 688136 | tf_op jit(solution)/shard_map/ppermute | solution.py:284
  22.3 12.3 %collective-permute-start.3 = (bf16[4,224,128]{2,1,0:T(8,128)(2,1)S(1)}, bf16[4,224,128]{2,1,0:T(8,128)(2,1)S(1)}, u32[]{:S(2)}, u32[]{:S(2)}) collective-permute-start(bf16[4,224,128]{2,1,0:T(8,128)(2,1)S(1)} %pad_maximum_fusion.2), channel_id=1, source_target_pairs={{0,8},{8,16},{16,24},{24,0},{1,9},{9,17},{17,25},{25,1},{2,10},{10... | collective-permute-start | bytes 688136 | tf_op jit(solution)/shard_map/ppermute | solution.py:284
  34.8 0.9 copy-start.13
  35.7 82.8 %all-to-all-start = ((bf16[32,128,768]{2,1,0:T(8,128)(2,1)}), bf16[32,128,768]{2,1,0:T(8,128)(2,1)}, u32[]{:S(2)}, u32[]{:S(2)}) async-start(bf16[32,128,768]{2,1,0:T(8,128)(2,1)} %bitcast.53), calls=%async_computation | async-start | bytes 12582912 | tf_op jit(solution)/shard_map/all_to_all | solution.py:279
  40.7 23.9 %collective-permute-start.6 = (bf16[16,224,128]{2,1,0:T(8,128)(2,1)}, bf16[16,224,128]{2,1,0:T(8,128)(2,1)S(1)}, u32[]{:S(2)}, u32[]{:S(2)}) collective-permute-start(bf16[16,224,128]{2,1,0:T(8,128)(2,1)} %copy-done.13), channel_id=1, source_target_pairs={{0,32},{32,64},{64,96},{96,0},{1,33},{33,65},{65,97},{97,1},{2,34}... | collective-permute-start | bytes 2752520 | tf_op jit(solution)/shard_map/ppermute | solution.py:284
  42.3 22.7 %collective-permute-start.8 = (bf16[16,224,128]{2,1,0:T(8,128)(2,1)}, bf16[16,224,128]{2,1,0:T(8,128)(2,1)}, u32[]{:S(2)}, u32[]{:S(2)}) collective-permute-start(bf16[16,224,128]{2,1,0:T(8,128)(2,1)} %copy-done.13), channel_id=1, source_target_pairs={{0,96},{32,0},{64,32},{96,64},{1,97},{33,1},{65,33},{97,65},{2,98}... | collective-permute-start | bytes 2752520 | tf_op jit(solution)/shard_map/ppermute | solution.py:284
  64.6 14.8 %copy-start.11 = (bf16[16,224,128]{2,1,0:T(8,128)(2,1)}, bf16[16,224,128]{2,1,0:T(8,128)(2,1)S(1)}, u32[]{:S(2)}) copy-start(bf16[16,224,128]{2,1,0:T(8,128)(2,1)S(1)} %collective-permute-done.6.refs_6_) | copy-start | bytes 2752516
  64.6 13.1 %collective-permute-start.7 = (bf16[8,224,128]{2,1,0:T(8,128)(2,1)S(1)}, bf16[8,224,128]{2,1,0:T(8,128)(2,1)S(1)}, u32[]{:S(2)}, u32[]{:S(2)}) collective-permute-start(bf16[8,224,128]{2,1,0:T(8,128)(2,1)S(1)} %slice.99), channel_id=1, source_target_pairs={{0,32},{32,64},{64,96},{96,0},{1,33},{33,65},{65,97},{97,1},{2,34}... | collective-permute-start | bytes 1376264 | tf_op jit(solution)/shard_map/ppermute | solution.py:284
  66.0 12.5 %collective-permute-start.9 = (bf16[8,224,128]{2,1,0:T(8,128)(2,1)S(1)}, bf16[8,224,128]{2,1,0:T(8,128)(2,1)S(1)}, u32[]{:S(2)}, u32[]{:S(2)}) collective-permute-start(bf16[8,224,128]{2,1,0:T(8,128)(2,1)S(1)} %slice.100), channel_id=1, source_target_pairs={{0,96},{32,0},{64,32},{96,64},{1,97},{33,1},{65,33},{97,65},{2,98}... | collective-permute-start | bytes 1376264 | tf_op jit(solution)/shard_map/ppermute | solution.py:284
  69.0 12.2 %collective-permute-start.10 = (bf16[16,224,128]{2,1,0:T(8,128)(2,1)}, bf16[16,224,128]{2,1,0:T(8,128)(2,1)}, u32[]{:S(2)}, u32[]{:S(2)}) collective-permute-start(bf16[16,224,128]{2,1,0:T(8,128)(2,1)} %copy-done.13), channel_id=1, source_target_pairs={{0,1},{1,0},{2,3},{3,2},{4,5},{5,4},{6,7},{7,6},{8,9},{9,8},{10,11... | collective-permute-start | bytes 2752520 | tf_op jit(solution)/shard_map/ppermute | solution.py:284
  69.0 12.2 %collective-permute-start.13 = (bf16[16,224,128]{2,1,0:T(8,128)(2,1)}, bf16[16,224,128]{2,1,0:T(8,128)(2,1)}, u32[]{:S(2)}, u32[]{:S(2)}) collective-permute-start(bf16[16,224,128]{2,1,0:T(8,128)(2,1)} %collective-permute-done.8.refs_8_), channel_id=1, source_target_pairs={{0,1},{1,0},{2,3},{3,2},{4,5},{5,4},{6,7},{7,6},{8,9},{9,8},{10,11... | collective-permute-start | bytes 2752520 | tf_op jit(solution)/shard_map/ppermute | solution.py:284
  69.5 11.7 %collective-permute-start.11 = (bf16[16,224,128]{2,1,0:T(8,128)(2,1)S(1)}, bf16[16,224,128]{2,1,0:T(8,128)(2,1)}, u32[]{:S(2)}, u32[]{:S(2)}) collective-permute-start(bf16[16,224,128]{2,1,0:T(8,128)(2,1)S(1)} %collective-permute-done.6.refs_6_), channel_id=1, source_target_pairs={{0,1},{1,0},{2,3},{3,2},{4,5},{5,4},{6,7},{7,6},{8,9},{9,8},{10,11... | collective-permute-start | bytes 2752520 | tf_op jit(solution)/shard_map/ppermute | solution.py:284
  79.4 2.8 %collective-permute-start.12 = (bf16[16,224,128]{2,1,0:T(8,128)(2,1)}, bf16[16,224,128]{2,1,0:T(8,128)(2,1)}, u32[]{:S(2)}, u32[]{:S(2)}) collective-permute-start(bf16[16,224,128]{2,1,0:T(8,128)(2,1)} %constant_dynamic-update-slice_fusion.7.refs_7_), channel_id=1, source_target_pairs={{0,1},{1,0},{2,3},{3,2},{4,5},{5,4},{6,7},{7,6},{8,9},{9,8},{10,11... | collective-permute-start | bytes 2752520 | tf_op jit(solution)/shard_map/ppermute | solution.py:284
  160.8 7.8 %copy-start.10 = (bf16[16,224,128]{2,1,0:T(8,128)(2,1)S(1)}, bf16[16,224,128]{2,1,0:T(8,128)(2,1)}, u32[]{:S(2)}) copy-start(bf16[16,224,128]{2,1,0:T(8,128)(2,1)} %get-tuple-element.35) | copy-start | bytes 2752516
  160.8 92.6 %all-to-all-start.1 = ((bf16[32,128,768]{2,1,0:T(8,128)(2,1)}), bf16[32,128,768]{2,1,0:T(8,128)(2,1)}, u32[]{:S(2)}, u32[]{:S(2)}) async-start(bf16[32,128,768]{2,1,0:T(8,128)(2,1)} %get-tuple-element.26), calls=%async_computation.1 | async-start | bytes 12582912 | tf_op jit(solution)/shard_map/all_to_all | solution.py:279
  165.8 2.8 %collective-permute-start.16 = (bf16[16,224,128]{2,1,0:T(8,128)(2,1)}, bf16[16,224,128]{2,1,0:T(8,128)(2,1)S(1)}, u32[]{:S(2)}, u32[]{:S(2)}) collective-permute-start(bf16[16,224,128]{2,1,0:T(8,128)(2,1)} %get-tuple-element.36), channel_id=1, source_target_pairs={{0,1},{1,0},{2,3},{3,2},{4,5},{5,4},{6,7},{7,6},{8,9},{9,8},{10,11... | collective-permute-start | bytes 2752520 | tf_op jit(solution)/shard_map/ppermute | solution.py:284
  166.0 6.1 %collective-permute-start.15 = (bf16[16,224,128]{2,1,0:T(8,128)(2,1)}, bf16[16,224,128]{2,1,0:T(8,128)(2,1)S(1)}, u32[]{:S(2)}, u32[]{:S(2)}) collective-permute-start(bf16[16,224,128]{2,1,0:T(8,128)(2,1)} %get-tuple-element.34), channel_id=1, source_target_pairs={{0,1},{1,0},{2,3},{3,2},{4,5},{5,4},{6,7},{7,6},{8,9},{9,8},{10,11... | collective-permute-start | bytes 2752520 | tf_op jit(solution)/shard_map/ppermute | solution.py:284
  166.4 5.9 %collective-permute-start.19 = (bf16[16,224,128]{2,1,0:T(8,128)(2,1)}, bf16[16,224,128]{2,1,0:T(8,128)(2,1)S(1)}, u32[]{:S(2)}, u32[]{:S(2)}) collective-permute-start(bf16[16,224,128]{2,1,0:T(8,128)(2,1)} %get-tuple-element.38), channel_id=1, source_target_pairs={{0,1},{1,0},{2,3},{3,2},{4,5},{5,4},{6,7},{7,6},{8,9},{9,8},{10,11... | collective-permute-start | bytes 2752520 | tf_op jit(solution)/shard_map/ppermute | solution.py:284
  166.5 19.9 %collective-permute-start.14 = (bf16[16,224,128]{2,1,0:T(8,128)(2,1)}, bf16[16,224,128]{2,1,0:T(8,128)(2,1)S(1)}, u32[]{:S(2)}, u32[]{:S(2)}) collective-permute-start(bf16[16,224,128]{2,1,0:T(8,128)(2,1)} %get-tuple-element.32), channel_id=1, source_target_pairs={{0,1},{1,0},{2,3},{3,2},{4,5},{5,4},{6,7},{7,6},{8,9},{9,8},{10,11... | collective-permute-start | bytes 2752520 | tf_op jit(solution)/shard_map/ppermute | solution.py:284
  168.6 3.5 %copy-start.9 = (bf16[16,224,128]{2,1,0:T(8,128)(2,1)S(1)}, bf16[16,224,128]{2,1,0:T(8,128)(2,1)}, u32[]{:S(2)}) copy-start(bf16[16,224,128]{2,1,0:T(8,128)(2,1)} %get-tuple-element.33) | copy-start | bytes 2752516
  169.0 3.4 %copy-start.8 = (bf16[16,224,128]{2,1,0:T(8,128)(2,1)S(1)}, bf16[16,224,128]{2,1,0:T(8,128)(2,1)}, u32[]{:S(2)}) copy-start(bf16[16,224,128]{2,1,0:T(8,128)(2,1)} %get-tuple-element.37) | copy-start | bytes 2752516
  169.0 13.2 %collective-permute-start.17 = (bf16[8,224,128]{2,1,0:T(8,128)(2,1)S(1)}, bf16[8,224,128]{2,1,0:T(8,128)(2,1)S(1)}, u32[]{:S(2)}, u32[]{:S(2)}) collective-permute-start(bf16[8,224,128]{2,1,0:T(8,128)(2,1)S(1)} %get-tuple-element.45), channel_id=1, source_target_pairs={{0,96},{32,0},{64,32},{96,64},{1,97},{33,1},{65,33},{97,65},{2,98}... | collective-permute-start | bytes 1376264 | tf_op jit(solution)/shard_map/ppermute | solution.py:284
  172.1 14.1 %collective-permute-start.20 = (bf16[8,224,128]{2,1,0:T(8,128)(2,1)S(1)}, bf16[8,224,128]{2,1,0:T(8,128)(2,1)S(1)}, u32[]{:S(2)}, u32[]{:S(2)}) collective-permute-start(bf16[8,224,128]{2,1,0:T(8,128)(2,1)S(1)} %get-tuple-element.46), channel_id=1, source_target_pairs={{0,32},{32,64},{64,96},{96,0},{1,33},{33,65},{65,97},{97,1},{2,34}... | collective-permute-start | bytes 1376264 | tf_op jit(solution)/shard_map/ppermute | solution.py:284
  182.4 26.7 %copy-start.7 = (bf16[16,224,128]{2,1,0:T(8,128)(2,1)S(1)}, bf16[16,224,128]{2,1,0:T(8,128)(2,1)}, u32[]{:S(2)}) copy-start(bf16[16,224,128]{2,1,0:T(8,128)(2,1)} %get-tuple-element.31) | copy-start | bytes 2752516
  182.4 22.9 %collective-permute-start.18 = (bf16[16,224,128]{2,1,0:T(8,128)(2,1)S(1)}, bf16[16,224,128]{2,1,0:T(8,128)(2,1)S(1)}, u32[]{:S(2)}, u32[]{:S(2)}) collective-permute-start(bf16[16,224,128]{2,1,0:T(8,128)(2,1)S(1)} %pad_maximum_fusion), channel_id=1, source_target_pairs={{0,96},{32,0},{64,32},{96,64},{1,97},{33,1},{65,33},{97,65},{2,98}... | collective-permute-start | bytes 2752520 | tf_op jit(solution)/shard_map/ppermute | solution.py:284
  186.4 22.7 %collective-permute-start.21 = (bf16[16,224,128]{2,1,0:T(8,128)(2,1)S(1)}, bf16[16,224,128]{2,1,0:T(8,128)(2,1)S(1)}, u32[]{:S(2)}, u32[]{:S(2)}) collective-permute-start(bf16[16,224,128]{2,1,0:T(8,128)(2,1)S(1)} %pad_maximum_fusion.1), channel_id=1, source_target_pairs={{0,32},{32,64},{64,96},{96,0},{1,33},{33,65},{65,97},{97,1},{2,34}... | collective-permute-start | bytes 2752520 | tf_op jit(solution)/shard_map/ppermute | solution.py:284
  209.6 33.7 %collective-permute-start.22 = (bf16[4,224,128]{2,1,0:T(8,128)(2,1)S(1)}, bf16[4,224,128]{2,1,0:T(8,128)(2,1)S(1)}, u32[]{:S(2)}, u32[]{:S(2)}) collective-permute-start(bf16[4,224,128]{2,1,0:T(8,128)(2,1)S(1)} %get-tuple-element.42), channel_id=1, source_target_pairs={{0,24},{8,0},{16,8},{24,16},{1,25},{9,1},{17,9},{25,17},{2,26},{10... | collective-permute-start | bytes 688136 | tf_op jit(solution)/shard_map/ppermute | solution.py:284
  212.6 30.6 %collective-permute-start.24 = (bf16[4,224,128]{2,1,0:T(8,128)(2,1)S(1)}, bf16[4,224,128]{2,1,0:T(8,128)(2,1)S(1)}, u32[]{:S(2)}, u32[]{:S(2)}) collective-permute-start(bf16[4,224,128]{2,1,0:T(8,128)(2,1)S(1)} %get-tuple-element.43), channel_id=1, source_target_pairs={{0,8},{8,16},{16,24},{24,0},{1,9},{9,17},{17,25},{25,1},{2,10},{10... | collective-permute-start | bytes 688136 | tf_op jit(solution)/shard_map/ppermute | solution.py:284
  212.6 35.9 %collective-permute-start.23 = (bf16[4,224,128]{2,1,0:T(8,128)(2,1)S(1)}, bf16[4,224,128]{2,1,0:T(8,128)(2,1)S(1)}, u32[]{:S(2)}, u32[]{:S(2)}) collective-permute-start(bf16[4,224,128]{2,1,0:T(8,128)(2,1)S(1)} %get-tuple-element.44), channel_id=1, source_target_pairs={{0,16},{8,24},{16,0},{24,8},{1,17},{9,25},{17,1},{25,9},{2,18},{10... | collective-permute-start | bytes 688136 | tf_op jit(solution)/shard_map/ppermute | solution.py:284
  248.7 18.6 %collective-permute-start.25 = (bf16[1,224,128]{2,1,0:T(8,128)(2,1)S(1)}, bf16[1,224,128]{2,1,0:T(8,128)(2,1)S(1)}, u32[]{:S(2)}, u32[]{:S(2)}) collective-permute-start(bf16[1,224,128]{2,1,0:T(8,128)(2,1)S(1)} %get-tuple-element.50), channel_id=1, source_target_pairs={{0,6},{2,0},{4,2},{6,4},{1,7},{3,1},{5,3},{7,5},{8,14},{10,8},{12,... | collective-permute-start | bytes 172040 | tf_op jit(solution)/shard_map/ppermute | solution.py:284
  251.8 17.7 %collective-permute-start.27 = (bf16[1,224,128]{2,1,0:T(8,128)(2,1)S(1)}, bf16[1,224,128]{2,1,0:T(8,128)(2,1)S(1)}, u32[]{:S(2)}, u32[]{:S(2)}) collective-permute-start(bf16[1,224,128]{2,1,0:T(8,128)(2,1)S(1)} %get-tuple-element.51), channel_id=1, source_target_pairs={{0,2},{2,4},{4,6},{6,0},{1,3},{3,5},{5,7},{7,1},{8,10},{10,12},{12... | collective-permute-start | bytes 172040 | tf_op jit(solution)/shard_map/ppermute | solution.py:284
  251.8 17.7 %collective-permute-start.26 = (bf16[1,224,128]{2,1,0:T(8,128)(2,1)S(1)}, bf16[1,224,128]{2,1,0:T(8,128)(2,1)S(1)}, u32[]{:S(2)}, u32[]{:S(2)}) collective-permute-start(bf16[1,224,128]{2,1,0:T(8,128)(2,1)S(1)} %get-tuple-element.52), channel_id=1, source_target_pairs={{0,4},{2,6},{4,0},{6,2},{1,5},{3,7},{5,1},{7,3},{8,12},{10,14},{12... | collective-permute-start | bytes 172040 | tf_op jit(solution)/shard_map/ppermute | solution.py:284
  253.3 20.8 %copy-start.1 = (f32[512]{0:T(512)S(1)}, f32[512]{0:T(512)}, u32[]{:S(2)}) copy-start(f32[512]{0:T(512)} %param.20) | copy-start | bytes 6148
  264.1 7.3 %collective-permute-start.28 = (bf16[256,128]{1,0:T(8,128)(2,1)S(1)}, bf16[256,128]{1,0:T(8,128)(2,1)S(1)}, u32[]{:S(2)}, u32[]{:S(2)}) collective-permute-start(bf16[256,128]{1,0:T(8,128)(2,1)S(1)} %get-tuple-element.47), channel_id=1, source_target_pairs={{0,96},{32,0},{64,32},{96,64},{1,97},{33,1},{65,33},{97,65},{2,98}... | collective-permute-start | bytes 196616 | tf_op jit(solution)/shard_map/ppermute | solution.py:284
  267.3 6.2 %collective-permute-start.30 = (bf16[256,128]{1,0:T(8,128)(2,1)S(1)}, bf16[256,128]{1,0:T(8,128)(2,1)S(1)}, u32[]{:S(2)}, u32[]{:S(2)}) collective-permute-start(bf16[256,128]{1,0:T(8,128)(2,1)S(1)} %get-tuple-element.48), channel_id=1, source_target_pairs={{0,32},{32,64},{64,96},{96,0},{1,33},{33,65},{65,97},{97,1},{2,34}... | collective-permute-start | bytes 196616 | tf_op jit(solution)/shard_map/ppermute | solution.py:284
  267.3 6.2 %collective-permute-start.29 = (bf16[256,128]{1,0:T(8,128)(2,1)S(1)}, bf16[256,128]{1,0:T(8,128)(2,1)S(1)}, u32[]{:S(2)}, u32[]{:S(2)}) collective-permute-start(bf16[256,128]{1,0:T(8,128)(2,1)S(1)} %get-tuple-element.49), channel_id=1, source_target_pairs={{0,64},{32,96},{64,0},{96,32},{1,65},{33,97},{65,1},{97,33},{2,66}... | collective-permute-start | bytes 196616 | tf_op jit(solution)/shard_map/ppermute | solution.py:284

commit v2 on v1

--- a/solution.py
+++ b/solution.py
@@ -13,24 +13,36 @@
 ROWS = 224
 GROUP = 8
 UNROLL = 8
+PARTS = (5, 3)
 
 
 def dot(a, b, dims=((1,), (0,))):
     return lax.dot_general(a, b, (dims, ((), ())), preferred_element_type=F32)
 
 
-def owner_forward_body(at_ref, bt_ref, c_ref, d_ref, wd_ref, u_ref):
+def owner_forward_body(at_ref, bt_ref, c_ref, d_ref, wd_ref, *u_refs):
     rows, width = c_ref.shape[0], wd_ref.shape[1]
     narrow = jnp.concatenate(
         [bt_ref[...], at_ref[...], jnp.zeros((32, rows), BF16)], axis=0
     )
-    u_ref[:, 0:width] = dot(d_ref[...], wd_ref[...]).astype(BF16)
-    u_ref[:, width : width + 128] = c_ref[...]
-    u_ref[:, width + 128 : width + 256] = narrow.T
-
-
-def owner_forward(at, bt, c, d, wd, rows=512):
+    group = u_refs[0].shape[0]
+
+    def place(value, start, stop):
+        value = value.reshape(group, rows // group, stop - start)
+        first = 0
+        for u_ref in u_refs:
+            part = u_ref.shape[1]
+            u_ref[:, :, start:stop] = value[:, first : first + part]
+            first += part
+
+    place(dot(d_ref[...], wd_ref[...]).astype(BF16), 0, width)
+    place(c_ref[...], width, width + 128)
+    place(narrow.T, width + 128, width + 256)
+
+
+def owner_forward(at, bt, c, d, wd, nb, rows=512):
     total, width = c.shape[0], wd.shape[1]
+    parts = [nb * n // sum(PARTS) for n in PARTS]
     return pl.pallas_call(
         owner_forward_body,
         grid=(total // rows,),
@@ -41,8 +53,8 @@
             pl.BlockSpec((rows, d.shape[1]), lambda i: (i, 0)),
             pl.BlockSpec(wd.shape, lambda i: (0, 0)),
         ],
-        out_specs=pl.BlockSpec((rows, width + 256), lambda i: (i, 0)),
-        out_shape=jax.ShapeDtypeStruct((total, width + 256), BF16),
+        out_specs=[pl.BlockSpec((rows // nb, n, width + 256), lambda i: (i, 0, 0)) for n in parts],
+        out_shape=[jax.ShapeDtypeStruct((total // nb, n, width + 256), BF16) for n in parts],
         compiler_params=pltpu.CompilerParams(vmem_limit_bytes=40 * MIB),
         cost_estimate=pl.CostEstimate(
             flops=2 * total * 256 * width, bytes_accessed=total * 2 * (480 + 768), transcendentals=0
@@ -60,9 +72,11 @@
 
 
 def middle_body(
-    steps, at_ref, table_ref, gain_ref, pd_ref, x_ref, w00, w01, w02, w03, w10, w11, w12, w13,
-    g_ref, gu_ref, v00, v01, v02, v03, v10, v11, v12, v13, scr, nrm, acc,
+    steps, later, at_ref, table_ref, gain_ref, pd_ref, x_ref, w00, w01, w02, w03, w10, w11, w12, w13,
+    g_ref, *refs,
 ):
+    before = (refs[0:4], refs[4:8])
+    gu_ref, v00, v01, v02, v03, v10, v11, v12, v13, scr, nrm, acc = refs[8 if later else 0 :]
     i = pl.program_id(0)
     nb = x_ref.shape[1]
     ns = nb + 1
@@ -148,17 +162,18 @@
             gu_ref[t, :, width + 128 : width + 256] = (
                 dot(ga, wa, last) + dot(gb, wb, last)
             ).astype(BF16)
-            vc = dot(xc, gc, first).astype(BF16)
-            vb = dot(xn, gb, first)[0:64].astype(BF16)
-            va = dot(xn, ga, first)[64:96].astype(BF16)
+            vc = dot(xc, gc, first)
+            vb = dot(xn, gb, first)[0:64]
+            va = dot(xn, ga, first)[64:96]
             for q in lanes:
-                part = slice(q * 128, (q + 1) * 128)
-                weight_grads[side][q][dx, 0:128, :] = vc[:, part]
-                weight_grads[side][q][dx, 128:192, :] = vb[:, part]
-                weight_grads[side][q][dx, 192:224, :] = va[:, part]
-
-
-def middle(at, table, gain, u, ws, g, per=16):
+                for value, rows in ((vc, slice(0, 128)), (vb, slice(128, 192)), (va, slice(192, 224))):
+                    piece = value[:, q * 128 : (q + 1) * 128]
+                    if later:
+                        piece = piece + before[side][q][dx, rows, :].astype(F32)
+                    weight_grads[side][q][dx, rows, :] = piece.astype(BF16)
+
+
+def middle(start, at, table, gain, u, ws, g, before, per=16):
     ntab, nb, full = u.shape
     width = gain.shape[1]
     steps = nb // per
@@ -181,7 +196,7 @@
     weight_in = pl.BlockSpec((4, ROWS, 128), lambda i, at, tb: (turn(i), 0, 0))
     weight_out = pl.BlockSpec((4, ROWS, 128), lambda i, at, tb: (late(i), 0, 0))
     return pl.pallas_call(
-        lambda *refs: middle_body(steps, *refs),
+        lambda *refs: middle_body(steps, len(before) > 0, *refs),
         grid_spec=pltpu.PrefetchScalarGridSpec(
             num_scalar_prefetch=2,
             grid=(8 + steps,),
@@ -195,9 +210,11 @@
             + [weight_in] * 8
             + [
                 pl.BlockSpec(
-                    (per, 128, 128), lambda i, at, tb: (jnp.clip(i - 4, 0, steps - 1), 0, 0)
+                    (per, 128, 128),
+                    lambda i, at, tb: (start // per + jnp.clip(i - 4, 0, steps - 1), 0, 0),
                 ),
-            ],
+            ]
+            + [weight_out] * len(before),
             out_specs=[
                 pl.BlockSpec((GROUP, nb, full), lambda i, at, tb: (backward_only(i, at), 0, 0)),
             ]
@@ -212,67 +229,99 @@
         + [jax.ShapeDtypeStruct((16, ROWS, 128), BF16)] * 8,
         compiler_params=pltpu.CompilerParams(vmem_limit_bytes=58 * MIB),
         cost_estimate=pl.CostEstimate(
-            flops=15 * 10**9, bytes_accessed=40 * 10**6, transcendentals=0
+            flops=nb * 10**8, bytes_accessed=35 * 10**6, transcendentals=0
         ),
         name="middle",
-    )(at, table, gain, u, u, *ws, g)
-
-
-def owner_backward_body(
-    gp_ref, gx_ref, d_ref, wd_ref, gat_ref, gbt_ref, gc_ref, gd_ref, gw_ref, acc
-):
+    )(at, table, gain, u, u, *ws, g, *before)
+
+
+def owner_backward_body(later, gp_ref, gx_ref, d_ref, wd_ref, *refs):
+    gd_ref, gc_ref, gw_ref, acc = refs[-4:]
     i = pl.program_id(0)
-    gc_ref[...] = gx_ref[:, 0:128]
-    narrow = gx_ref[:, 128:256].T
+    owners, part, wdim = d_ref.shape
+    gp = gp_ref[...].reshape(owners * part, -1)
+    gd = dot(gp, wd_ref[...], ((1,), (1,))).astype(BF16)
+    gd_ref[...] = gd.reshape(owners, part, wdim)
+    gc_ref[...] = gx_ref[...]
+
+    @pl.when(i == 0)
+    def _():
+        acc[...] = refs[2][...] if later else jnp.zeros_like(acc)
+
+    acc[...] += dot(d_ref[...].reshape(owners * part, wdim), gp, ((0,), (0,)))
+
+    @pl.when(i == pl.num_programs(0) - 1)
+    def _():
+        gw_ref[...] = acc[...].astype(gw_ref.dtype)
+
+
+def owner_backward(start, gu, d, wd, before=(), per=16):
+    owners, nb, wdim = d.shape
+    width = wd.shape[1]
+    part = gu.shape[1]
+    later = len(before) > 0
+    whole = pl.BlockSpec((wdim, width), lambda i: (0, 0))
+    d_spec = pl.BlockSpec((owners, per, wdim), lambda i: (0, start // per + i, 0))
+    c_spec = pl.BlockSpec((owners, per, 128), lambda i: (0, start // per + i, 0))
+    in_specs = [
+        pl.BlockSpec((owners, per, width), lambda i: (0, i, 0)),
+        pl.BlockSpec((owners, per, 128), lambda i: (0, i, width // 128)),
+        d_spec,
+        whole,
+    ]
+    if later:
+        in_specs += [pl.BlockSpec(memory_space=pl.ANY)] * 2 + [whole]
+    return pl.pallas_call(
+        lambda *refs: owner_backward_body(later, *refs),
+        grid=(part // per,),
+        in_specs=in_specs,
+        out_specs=[d_spec, c_spec, whole],
+        out_shape=[
+            jax.ShapeDtypeStruct(d.shape, BF16),
+            jax.ShapeDtypeStruct((owners, nb, 128), BF16),
+            jax.ShapeDtypeStruct((wdim, width), BF16 if later else F32),
+        ],
+        scratch_shapes=[pltpu.VMEM((wdim, width), F32)],
+        input_output_aliases={4: 0, 5: 1} if later else {},
+        compiler_params=pltpu.CompilerParams(vmem_limit_bytes=40 * MIB),
+        cost_estimate=pl.CostEstimate(
+            flops=4 * owners * part * wdim * width,
+            bytes_accessed=owners * part * 2 * 1024,
+            transcendentals=0,
+        ),
+        name="owner_backward",
+    )(gu, gu, d, wd, *before)
+
+
+def owner_split_body(*refs):
+    *gx_refs, gat_ref, gbt_ref = refs
+    narrow = jnp.concatenate([r[...] for r in gx_refs], axis=1).reshape(-1, 128).T
     gbt_ref[...] = narrow[0:64]
     gat_ref[...] = narrow[64:96]
-    gp = gp_ref[...]
-    gd_ref[...] = dot(gp, wd_ref[...], ((1,), (1,))).astype(BF16)
-
-    @pl.when(i == 0)
-    def _():
-        acc[...] = jnp.zeros_like(acc)
-
-    acc[...] += dot(d_ref[...], gp, ((0,), (0,)))
-
-    @pl.when(i == pl.num_programs(0) - 1)
-    def _():
-        gw_ref[...] = acc[...].astype(BF16)
-
-
-def owner_backward(gu, d, wd, rows=512):
-    total = gu.shape[0]
-    wdim, width = wd.shape
+
+
+def owner_split(gus, group=8):
+    owners, _, full = gus[0].shape
+    nb = sum(gu.shape[1] for gu in gus)
+    total, rows = owners * nb, group * nb
     return pl.pallas_call(
-        owner_backward_body,
-        grid=(total // rows,),
+        owner_split_body,
+        grid=(owners // group,),
         in_specs=[
-            pl.BlockSpec((rows, width), lambda i: (i, 0)),
-            pl.BlockSpec((rows, 256), lambda i: (i, width // 256)),
-            pl.BlockSpec((rows, wdim), lambda i: (i, 0)),
-            pl.BlockSpec(wd.shape, lambda i: (0, 0)),
+            pl.BlockSpec((group, gu.shape[1], 128), lambda i: (i, 0, full // 128 - 1)) for gu in gus
         ],
         out_specs=[
             pl.BlockSpec((32, rows), lambda i: (0, i)),
             pl.BlockSpec((64, rows), lambda i: (0, i)),
-            pl.BlockSpec((rows, 128), lambda i: (i, 0)),
-            pl.BlockSpec((rows, wdim), lambda i: (i, 0)),
-            pl.BlockSpec((wdim, width), lambda i: (0, 0)),
         ],
         out_shape=[
             jax.ShapeDtypeStruct((32, total), BF16),
             jax.ShapeDtypeStruct((64, total), BF16),
-            jax.ShapeDtypeStruct((total, 128), BF16),
-            jax.ShapeDtypeStruct((total, wdim), BF16),
-            jax.ShapeDtypeStruct((wdim, width), BF16),
         ],
-        scratch_shapes=[pltpu.VMEM((wdim, width), F32)],
         compiler_params=pltpu.CompilerParams(vmem_limit_bytes=40 * MIB),
-        cost_estimate=pl.CostEstimate(
-            flops=4 * total * wdim * width, bytes_accessed=total * 2 * 1500, transcendentals=0
-        ),
-        name="owner_backward",
-    )(gu, gu, d, wd)
+        cost_estimate=pl.CostEstimate(flops=0, bytes_accessed=total * 2 * 224, transcendentals=0),
+        name="owner_split",
+    )(*gus)
 
 
 def exchange(x):
@@ -297,10 +346,8 @@
     return jnp.take(blocks, order, axis=1).reshape(w.shape)
 
 
-def gather_plane(w, y):
-    part = lax.dynamic_slice_in_dim(w, y * 128, 128, axis=1)
-    part = jnp.stack([part, shift(part, "x", 1), shift(part, "x", 2), shift(part, "x", -1)])
-    return jnp.concatenate([part, shift(part, "z", 1), shift(part, "z", 2), shift(part, "z", -1)])
+def gather_axis(part, axis):
+    return jnp.concatenate([part, shift(part, axis, 1), shift(part, axis, 2), shift(part, axis, -1)])
 
 
 def gather_quarters(part):
@@ -310,21 +357,22 @@
     return own + tuple(shift(p, "c", 1) for p in own)
 
 
-def scatter_weight_grads(own, other):
-    s = [add(o, shift(p, "c", 1)).astype(BF16) for o, p in zip(own, other)]
-    from_above, from_below = shift(s[2][:8], "y", -1), shift(s[2][8:], "y", 1)
-    down = jnp.concatenate([add(s[1][:8], from_above).astype(BF16), s[1][8:]])
-    up = jnp.concatenate([s[3][:8], add(s[3][8:], from_below).astype(BF16)])
-    part = add(s[0], shift(down, "y", -1), shift(up, "y", 1)).astype(BF16)
-    for axis in ("z", "x"):
-        n = part.shape[0] // 4
-        part = add(
-            part[:n],
-            shift(part[n : 2 * n], axis, -1),
-            shift(part[2 * n : 3 * n], axis, -2),
-            shift(part[3 * n :], axis, -3),
-        ).astype(BF16)
-    return part[0]
+def scatter_far(own, other):
+    s = add(own[2], shift(other[2], "c", 1)).astype(BF16)
+    from_above, from_below = shift(s[:8], "y", -1), shift(s[8:], "y", 1)
+    s = [add(own[r], shift(other[r], "c", 1)) for r in (0, 1, 3)]
+    down = jnp.concatenate([add(s[1][:8], from_above), s[1][8:]]).astype(BF16)
+    up = jnp.concatenate([s[2][:8], add(s[2][8:], from_below)]).astype(BF16)
+    return s[0], down, up
+
+
+def scatter_near(own, down, up):
+    return add(own, shift(down, "y", -1), shift(up, "y", 1)).astype(BF16)
+
+
+def scatter_axis(part, axis):
+    n = part.shape[0] // 4
+    return (part[:n],) + tuple(shift(part[k * n : (k + 1) * n], axis, -k) for k in (1, 2, 3))
 
 
 def on_device(
@@ -339,20 +387,41 @@
     wd = turn_features(proj_d[0], y)
     gain = turn_features(norm_gain[None], y)
     d = pooled_d[:, 0]
-    part = gather_plane(jnp.concatenate([proj_c[0], proj_b[0], proj_a[0]], axis=0), y)
-    u = owner_forward(
-        pooled_a.transpose(1, 2, 0)[0], pooled_b.transpose(1, 2, 0)[0], pooled_c[:, 0], d, wd
+    part = jnp.concatenate([proj_c[0], proj_b[0], proj_a[0]], axis=0)
+    part = gather_axis(lax.dynamic_slice_in_dim(part, y * 128, 128, axis=1)[None], "x")
+    wd, part = lax.optimization_barrier((wd, part))
+    part = gather_axis(part, "z")
+    us = owner_forward(
+        pooled_a.transpose(1, 2, 0)[0], pooled_b.transpose(1, 2, 0)[0], pooled_c[:, 0], d, wd, nb
     )
-    u, part = lax.optimization_barrier((u, part))
+    u0, u1 = us
+    start = u0.shape[1]
+    u0, part = lax.optimization_barrier((u0, part))
     ws = gather_quarters(part)
-    u = exchange(u.reshape(owners, nb, -1))
-    gu, *gws = middle(at, slot_table, gain, u, ws, grad_gram)
-    gu = exchange(gu).reshape(total, -1)
-    gat, gbt, gc, gd, gwd = owner_backward(gu, d, wd)
+    u0 = exchange(u0)
+    u1, u0, ws = lax.optimization_barrier((u1, u0, ws))
+    u1 = exchange(u1)
+    gu0, *gws = middle(0, at, slot_table, gain, u0, ws, grad_gram, [])
+    gu0 = exchange(gu0)
+    gu1, *gws = middle(start, at, slot_table, gain, u1, ws, grad_gram, gws)
+    own, down, up = scatter_far(gws[:4], gws[4:])
+    gu1, down, up = lax.optimization_barrier((gu1, down, up))
+    gu1 = exchange(gu1)
+    d = d.reshape(owners, nb, -1)
+    gd, gc, gwd = owner_backward(0, gu0, d, wd)
+    part = scatter_near(own, down, up)
+    gd, gc, gwd, part = lax.optimization_barrier((gd, gc, gwd, part))
+    gd, gc, gwd = owner_backward(start, gu1, d, wd, (gd, gc, gwd))
+    gd, gc = gd.reshape(total, -1), gc.reshape(total, -1)
+    q = [gwd[:, r * 128 : (r + 1) * 128] for r in range(4)]
+    q = [q[0]] + [shift(q[r], "y", -r) for r in (1, 2, 3)]
+    pieces, _ = lax.optimization_barrier((scatter_axis(part, "z"), gwd))
+    pieces = scatter_axis(add(*pieces).astype(BF16), "x")
+    gat, gbt = owner_split((gu0, gu1))
+    pieces, q, gat, gbt = lax.optimization_barrier((pieces, q, gat, gbt))
     scale = 1.0 / np.sqrt(total * lax.axis_size("y")).astype(np.float32)
-    gw = scatter_weight_grads(gws[:4], gws[4:]).astype(F32) * scale
-    q = [gwd[:, r * 128 : (r + 1) * 128] for r in range(4)]
-    gwd = add(q[0], shift(q[1], "y", -1), shift(q[2], "y", -2), shift(q[3], "y", -3)) * scale
+    gw = add(*pieces)[0] * scale
+    gwd = add(*q) * scale
     return (
         gat.T[:, None],
         gbt.T[:, None],

time: 276 us -> 244 us (0.88)
  waiting for transfers between devices: 147 us -> 80.6 us
  Pallas kernels: 55.4 us -> 74.9 us
  starting transfers between devices: 52.3 us -> 59.3 us
  other arithmetic: 5.39 us -> 9.85 us
  local copies, waits for them, and re-layouts: 13.4 us -> 16.9 us
    ppermute x31, waiting for transfers between devices: 110 us -> 64.6 us  [shift(): return lax.ppermute(x, axis, [(i, (i + k) % n) for i in range(n)])]
    all_to_all x2 -> x4, waiting for transfers between devices: 36.3 us -> 16.1 us  [exchange(): return lax.all_to_all(x, PLANE, split_axis=0, concat_axis=0, tiled=True)]
    pallas_call x2 -> x5, Pallas kernels: 52.9 us -> 70.4 us  [the longest x2 56 us: middle(): pl.pallas_call(lambda *refs: middle_body(steps, len(before) > 0, *refs),...]
    all_to_all x2 -> x4, starting transfers between devices: 9.94 us -> 20 us  [exchange(): return lax.all_to_all(x, PLANE, split_axis=0, concat_axis=0, tiled=True)]
    unnamed x36 -> x43, local copies, waits for them, and re-layouts: 8 us -> 12.4 us
    ppermute x31, starting transfers between devices: 42.4 us -> 39.3 us  [shift(): return lax.ppermute(x, axis, [(i, (i + k) % n) for i in range(n)])]
    concatenate x2 -> x4, other arithmetic: 0.17 us -> 3.03 us  [the longest x1 1.03 us: scatter_far(): up = jnp.concatenate([s[2][:8], add(s[2][8:], from_below)]).astype(BF16)]
  transfers between devices with their start and end apart: 33 -> 35, of which waited for: 12 -> 15; matrix products, arithmetic and copies ran while one was open for 4% -> 4% of each run, Pallas kernels for 5% -> 31%
where the time goes in v2:
time: 244 us; the launch traced here: 243 us
  waiting for transfers between devices  80.6 us (33%)
  Pallas kernels  74.9 us (31%)
  starting transfers between devices  59.3 us (24%)
  local copies, waits for them, and re-layouts  16.9 us (7%)
  other arithmetic  9.85 us (4%)
    ppermute x31, waiting for transfers between devices, shift(): return lax.ppermute(x, axis, [(i, (i + k) % n) for i in range(n)])  64.6 us
    pallas_call x2, Pallas kernels, middle(): pl.pallas_call(lambda *refs: middle_body(steps, len(before) > 0, *refs),...  56 us
    ppermute x31, starting transfers between devices, shift(): return lax.ppermute(x, axis, [(i, (i + k) % n) for i in range(n)])  39.3 us
    all_to_all x4, starting transfers between devices, exchange(): return lax.all_to_all(x, PLANE, split_axis=0, concat_axis=0, tiled=True)  20 us
    all_to_all x4, waiting for transfers between devices, exchange(): return lax.all_to_all(x, PLANE, split_axis=0, concat_axis=0, tiled=True)  16.1 us
    unnamed x43, local copies, waits for them, and re-layouts  12.4 us
    pallas_call x2, Pallas kernels, owner_backward(): pl.pallas_call(lambda *refs: owner_backward_body(later, *refs), grid=(par...  11 us
  transfers between devices with their start and end apart: 35, of which 15 were waited for; matrix products, arithmetic and copies ran while one was open for 4% of the time, Pallas kernels for 31%

profile of v2, /device:TPU:0, one launch (start us, length us, event | category | flops | bytes accessed | tf_op | source)
XLA Modules:
  0.0 242.6 jit_solution(15020404269551536252)
XLA Ops:
  1.6 2.8 %collective-permute-start.2 = (bf16[1,224,128]{2,1,0:T(8,128)(2,1)S(1)}, bf16[1,224,128]{2,1,0:T(8,128)(2,1)S(1)}, u32[]{:S(2)}, u32[]{:S(2)}) collective-permute-start(bf16[1,224,128]{2,1,0:T(8,128)(2,1)S(1)} %fusion.4), channel_id=1, source_target_pairs={{0,6},{2,0},{4,2},{6,4},{1,7},{3,1},{5,3},{7,5},{8,14},{10,8},{12,... | collective-permute-start | bytes 172040 | tf_op jit(solution)/shard_map/ppermute | solution.py:333
  6.2 1.1 copy.22
  8.2 2.1 collective-permute-done.1
  11.7 4.1 %collective-permute-start.5 = (bf16[4,224,128]{2,1,0:T(8,128)(2,1)S(1)}, bf16[4,224,128]{2,1,0:T(8,128)(2,1)S(1)}, u32[]{:S(2)}, u32[]{:S(2)}) collective-permute-start(bf16[4,224,128]{2,1,0:T(8,128)(2,1)S(1)} %pad_maximum_fusion.3), channel_id=1, source_target_pairs={{0,24},{8,0},{16,8},{24,16},{1,25},{9,1},{17,9},{25,17},{2,26},{10... | collective-permute-start | bytes 688136 | tf_op jit(solution)/shard_map/ppermute | solution.py:333
  15.8 1.3 collective-permute-start.3
  17.1 1.2 copy-done.6
  18.3 4.5 %owner_forward.1 = (bf16[32,80,768]{2,1,0:T(8,128)(2,1)S(1)}, bf16[32,48,768]{2,1,0:T(8,128)(2,1)}) custom-call(bf16[32,4096]{1,0:T(8,128)(2,1)S(1)} %bitcast.51, bf16[64,4096]{1,0:T(8,128)(2,1)S(1)} %bitcast.50, bf16[4096,128]{1,0:T(8,128)(2,1)S(1)} %bitcast.49, bf16[4096,256]{1,0:T(8,128)(2,1)S(1)} %bitcast.46, ...), custom_call_target="tpu_custom_call" | custom-call | flops 1073741824 | bytes 10223616 | tf_op jit(solution)/shard_map/owner_forward/pallas_call | solution.py:46
  22.8 1.9 copy-done.5
  25.5 2.1 collective-permute-done.3
  27.7 4.8 %all-to-all-start = ((bf16[32,80,768]{2,1,0:T(8,128)(2,1)}), bf16[32,80,768]{2,1,0:T(8,128)(2,1)}, u32[]{:S(2)}, u32[]{:S(2)}) async-start(bf16[32,80,768]{2,1,0:T(8,128)(2,1)} %copy-done.5), calls=%async_computation | async-start | bytes 7864320 | tf_op jit(solution)/shard_map/all_to_all | solution.py:328
  32.6 1.6 collective-permute-start.6
  34.2 1.7 collective-permute-start.8
  35.9 20.4 %collective-permute-done.6.refs_6_ = bf16[16,224,128]{2,1,0:T(8,128)(2,1)S(1)} collective-permute-done((bf16[16,224,128]{2,1,0:T(8,128)(2,1)S(1)}, bf16[16,224,128]{2,1,0:T(8,128)(2,1)S(1)}, u32[]{:S(2)}, u32[]{:S(2)}) %collective-permute-start.6) | collective-permute-done | bytes 917536 | tf_op jit(solution)/shard_map/ppermute | solution.py:333
  56.7 3.0 %collective-permute-start.9 = (bf16[8,224,128]{2,1,0:T(8,128)(2,1)S(1)}, bf16[8,224,128]{2,1,0:T(8,128)(2,1)S(1)}, u32[]{:S(2)}, u32[]{:S(2)}) collective-permute-start(bf16[8,224,128]{2,1,0:T(8,128)(2,1)S(1)} %slice.102), channel_id=1, source_target_pairs={{0,96},{32,0},{64,32},{96,64},{1,97},{33,1},{65,33},{97,65},{2,98}... | collective-permute-start | bytes 1376264 | tf_op jit(solution)/shard_map/ppermute | solution.py:333
  60.3 9.2 %collective-permute-done.7 = bf16[8,224,128]{2,1,0:T(8,128)(2,1)S(1)} collective-permute-done((bf16[8,224,128]{2,1,0:T(8,128)(2,1)S(1)}, bf16[8,224,128]{2,1,0:T(8,128)(2,1)S(1)}, u32[]{:S(2)}, u32[]{:S(2)}) %collective-permute-start.7) | collective-permute-done | bytes 458784 | tf_op jit(solution)/shard_map/ppermute | solution.py:333
  72.3 10.9 %all-to-all-done.refs_3_.refs_4_ = bf16[32,80,768]{2,1,0:T(8,128)(2,1)} async-done(((bf16[32,80,768]{2,1,0:T(8,128)(2,1)}), bf16[32,80,768]{2,1,0:T(8,128)(2,1)}, u32[]{:S(2)}, u32[]{:S(2)}) %all-to-all-start) | async-done | bytes 3932192 | tf_op jit(solution)/shard_map/all_to_all | solution.py:328
  83.2 4.1 %all-to-all-start.2 = ((bf16[32,48,768]{2,1,0:T(8,128)(2,1)}), bf16[32,48,768]{2,1,0:T(8,128)(2,1)S(1)}, u32[]{:S(2)}, u32[]{:S(2)}) async-start(bf16[32,48,768]{2,1,0:T(8,128)(2,1)} %get-tuple-element.90), calls=%async_computation.2 | async-start | bytes 4718592 | tf_op jit(solution)/shard_map/all_to_all | solution.py:328
  89.1 30.5 %middle.2 = (bf16[32,80,768]{2,1,0:T(8,128)(2,1)}, bf16[16,224,128]{2,1,0:T(8,128)(2,1)}, bf16[16,224,128]{2,1,0:T(8,128)(2,1)}, bf16[16,224,128]{2,1,0:T(8,128)...) custom-call(s32[3]{0:T(128)} %pad_add_fusion.refs_0_, ...), custom_call_target="tpu_custom_call" | custom-call | flops 8000000000 | bytes 35000000 | tf_op jit(solution)/shard_map/middle/pallas_call | solution.py:198
  120.4 1.5 copy-done.9
  121.9 7.0 %all-to-all-start.1 = ((bf16[32,80,768]{2,1,0:T(8,128)(2,1)}), bf16[32,80,768]{2,1,0:T(8,128)(2,1)}, u32[]{:S(2)}, u32[]{:S(2)}) async-start(bf16[32,80,768]{2,1,0:T(8,128)(2,1)} %get-tuple-element.86), calls=%async_computation.1 | async-start | bytes 7864320 | tf_op jit(solution)/shard_map/all_to_all | solution.py:328
  128.9 25.5 %middle.3 = (bf16[32,48,768]{2,1,0:T(8,128)(2,1)}, bf16[16,224,128]{2,1,0:T(8,128)(2,1)}, bf16[16,224,128]{2,1,0:T(8,128)(2,1)}, bf16[16,224,128]{2,1,0:T(8,128)...) custom-call(s32[3]{0:T(128)} %pad_add_fusion.refs_0_, ...), custom_call_target="tpu_custom_call" | custom-call | flops 4800000000 | bytes 35000000 | tf_op jit(solution)/shard_map/middle/pallas_call | solution.py:198
  155.1 2.1 collective-permute-done.16
  157.2 1.5 add_convert_fusion.1
  158.8 1.6 collective-permute-start.19
  160.4 1.7 collective-permute-start.17
  163.6 9.1 %collective-permute-done.17 = bf16[8,224,128]{2,1,0:T(8,128)(2,1)S(1)} collective-permute-done((bf16[8,224,128]{2,1,0:T(8,128)(2,1)S(1)}, bf16[8,224,128]{2,1,0:T(8,128)(2,1)S(1)}, u32[]{:S(2)}, u32[]{:S(2)}) %collective-permute-start.17) | collective-permute-done | bytes 458784 | tf_op jit(solution)/shard_map/ppermute | solution.py:333
  172.8 1.0 pad_maximum_fusion.1
  173.9 1.0 pad_maximum_fusion.2
  174.9 4.4 %all-to-all-done.1.refs_0_.refs_1_ = bf16[32,80,768]{2,1,0:T(8,128)(2,1)} async-done(((bf16[32,80,768]{2,1,0:T(8,128)(2,1)}), bf16[32,80,768]{2,1,0:T(8,128)(2,1)}, u32[]{:S(2)}, u32[]{:S(2)}) %all-to-all-start.1) | async-done | bytes 3932192 | tf_op jit(solution)/shard_map/all_to_all | solution.py:328
  179.3 4.1 %all-to-all-start.3 = ((bf16[32,48,768]{2,1,0:T(8,128)(2,1)}), bf16[32,48,768]{2,1,0:T(8,128)(2,1)S(1)}, u32[]{:S(2)}, u32[]{:S(2)}) async-start(bf16[32,48,768]{2,1,0:T(8,128)(2,1)} %get-tuple-element.111), calls=%async_computation.3 | async-start | bytes 4718592 | tf_op jit(solution)/shard_map/all_to_all | solution.py:328
  183.6 3.0 %collective-permute-start.20 = (bf16[16,224,128]{2,1,0:T(8,128)(2,1)}, bf16[16,224,128]{2,1,0:T(8,128)(2,1)S(1)}, u32[]{:S(2)}, u32[]{:S(2)}) collective-permute-start(bf16[16,224,128]{2,1,0:T(8,128)(2,1)} %pad_maximum_fusion.1), channel_id=1, source_target_pairs={{0,96},{32,0},{64,32},{96,64},{1,97},{33,1},{65,33},{97,65},{2,98}... | collective-permute-start | bytes 2752520 | tf_op jit(solution)/shard_map/ppermute | solution.py:333
  186.6 1.6 copy-done.3
  188.2 7.2 %owner_backward.2 = (bf16[32,128,256]{2,1,0:T(8,128)(2,1)}, bf16[32,128,128]{2,1,0:T(8,128)(2,1)}, f32[256,512]{1,0:T(8,128)S(1)}) custom-call(bf16[32,80,768]{2,1,0:T(8,128)(2,1)} %all-to-all-done.1.refs_0_.refs_1_, bf16[32,80,768]{2,1,0:T(8,128)(2,1)} %all-to-all-done.1.refs_0_.refs_1_, bf16[32,128,256]{2,1,0:T(8,128)(2,1)S(1)} %bitcast.47, ...), custom_call_target="tpu_custom_call" | custom-call | flops 1342177280 | bytes 5242880 | tf_op jit(solution)/shard_map/owner_backward/pallas_call | solution.py:274
  195.4 11.7 %collective-permute-done.20 = bf16[16,224,128]{2,1,0:T(8,128)(2,1)S(1)} collective-permute-done((bf16[16,224,128]{2,1,0:T(8,128)(2,1)}, bf16[16,224,128]{2,1,0:T(8,128)(2,1)S(1)}, u32[]{:S(2)}, u32[]{:S(2)}) %collective-permute-start.20) | collective-permute-done | bytes 917536 | tf_op jit(solution)/shard_map/ppermute | solution.py:333
  207.1 3.3 %collective-permute-done.21 = bf16[16,224,128]{2,1,0:T(8,128)(2,1)S(1)} collective-permute-done((bf16[16,224,128]{2,1,0:T(8,128)(2,1)}, bf16[16,224,128]{2,1,0:T(8,128)(2,1)S(1)}, u32[]{:S(2)}, u32[]{:S(2)}) %collective-permute-start.21) | collective-permute-done | bytes 917536 | tf_op jit(solution)/shard_map/ppermute | solution.py:333
  211.7 1.7 collective-permute-start.24
  213.5 2.8 %collective-permute-start.23 = (bf16[4,224,128]{2,1,0:T(8,128)(2,1)}, bf16[4,224,128]{2,1,0:T(8,128)(2,1)}, u32[]{:S(2)}, u32[]{:S(2)}) collective-permute-start(bf16[4,224,128]{2,1,0:T(8,128)(2,1)} %get-tuple-element.135), channel_id=1, source_target_pairs={{0,16},{8,24},{16,0},{24,8},{1,17},{9,25},{17,1},{25,9},{2,18},{10... | collective-permute-start | bytes 688136 | tf_op jit(solution)/shard_map/ppermute | solution.py:333
  216.2 1.4 collective-permute-start.22
  217.7 1.6 copy-done.4
  219.2 3.8 %owner_backward.3 = (bf16[32,128,256]{2,1,0:T(8,128)(2,1)}, bf16[32,128,128]{2,1,0:T(8,128)(2,1)}, bf16[256,512]{1,0:T(8,128)(2,1)S(1)}) custom-call(bf16[32,48,768]{2,1,0:T(8,128)(2,1)S(1)} %all-to-all-done.3.refs_0_.refs_1_, bf16[32,48,768]{2,1,0:T(8,128)(2,1)S(1)} %all-to-all-done.3.refs_0_.refs_1_, ...), custom_call_target="tpu_custom_call", output_to_operand_aliasing={{0}: (4, {}), {1}: (5, {})} | custom-call | flops 805306368 | bytes 3145728 | tf_op jit(solution)/shard_map/owner_backward/pallas_call | solution.py:274
  223.1 3.1 %collective-permute-done.23 = bf16[4,224,128]{2,1,0:T(8,128)(2,1)} collective-permute-done((bf16[4,224,128]{2,1,0:T(8,128)(2,1)}, bf16[4,224,128]{2,1,0:T(8,128)(2,1)}, u32[]{:S(2)}, u32[]{:S(2)}) %collective-permute-start.23) | collective-permute-done | bytes 229408 | tf_op jit(solution)/shard_map/ppermute | solution.py:333
  226.2 1.3 add_convert_fusion.2
  227.5 1.5 collective-permute-start.27
  229.2 2.4 %collective-permute-start.29 = (bf16[256,128]{1,0:T(8,128)(2,1)S(1)}, bf16[256,128]{1,0:T(8,128)(2,1)S(1)}, u32[]{:S(2)}, u32[]{:S(2)}) collective-permute-start(bf16[256,128]{1,0:T(8,128)(2,1)S(1)} %get-tuple-element.141), channel_id=1, source_target_pairs={{0,64},{32,96},{64,0},{96,32},{1,65},{33,97},{65,1},{97,33},{2,66}... | collective-permute-start | bytes 196616 | tf_op jit(solution)/shard_map/ppermute | solution.py:333
  231.6 1.1 collective-permute-start.28
  232.8 2.3 collective-permute-start.26
  235.1 1.4 collective-permute-start.25
  236.6 3.4 %owner_split.1 = (bf16[32,4096]{1,0:T(8,128)(2,1)}, bf16[64,4096]{1,0:T(8,128)(2,1)}) custom-call(bf16[32,80,768]{2,1,0:T(8,128)(2,1)} %all-to-all-done.1.refs_0_.refs_1_, bf16[32,48,768]{2,1,0:T(8,128)(2,1)S(1)} %all-to-all-done.3.refs_0_.refs_1_), custom_call_target="tpu_custom_call" | custom-call | bytes 1835008 | tf_op jit(solution)/shard_map/owner_split/pallas_call | solution.py:307
  (107 shorter events, 19.0 us)
Async XLA Ops:
  0.6 86.6 %copy-start = (f32[512]{0:T(512)S(1)}, f32[512]{0:T(512)}, u32[]{:S(2)}) copy-start(f32[512]{0:T(512)} %param.20) | copy-start | bytes 6148
  0.7 16.5 %copy-start.2 = (bf16[4096,1,256]{2,0,1:T(8,128)(2,1)S(1)}, bf16[4096,1,256]{2,0,1:T(8,128)(2,1)}, u32[]{:S(2)}) copy-start(bf16[4096,1,256]{2,0,1:T(8,128)(2,1)} %param.14) | copy-start | bytes 6291460
  0.7 16.4 %copy-start.7 = (bf16[4096,1,64]{0,2,1:T(8,128)(2,1)S(1)}, bf16[4096,1,64]{0,2,1:T(8,128)(2,1)}, u32[]{:S(2)}) copy-start(bf16[4096,1,64]{0,2,1:T(8,128)(2,1)} %param.12) | copy-start | bytes 1572868
  0.7 16.4 %copy-start.8 = (bf16[4096,1,32]{0,2,1:T(8,128)(2,1)S(1)}, bf16[4096,1,32]{0,2,1:T(8,128)(2,1)}, u32[]{:S(2)}) copy-start(bf16[4096,1,32]{0,2,1:T(8,128)(2,1)} %param.11) | copy-start | bytes 786436
  1.6 6.6 %collective-permute-start.2 = (bf16[1,224,128]{2,1,0:T(8,128)(2,1)S(1)}, bf16[1,224,128]{2,1,0:T(8,128)(2,1)S(1)}, u32[]{:S(2)}, u32[]{:S(2)}) collective-permute-start(bf16[1,224,128]{2,1,0:T(8,128)(2,1)S(1)} %fusion.4), channel_id=1, source_target_pairs={{0,6},{2,0},{4,2},{6,4},{1,7},{3,1},{5,3},{7,5},{8,14},{10,8},{12,... | collective-permute-start | bytes 172040 | tf_op jit(solution)/shard_map/ppermute | solution.py:333
  4.5 5.8 %collective-permute-start.1 = (bf16[1,224,128]{2,1,0:T(8,128)(2,1)S(1)}, bf16[1,224,128]{2,1,0:T(8,128)(2,1)}, u32[]{:S(2)}, u32[]{:S(2)}) collective-permute-start(bf16[1,224,128]{2,1,0:T(8,128)(2,1)S(1)} %fusion.4), channel_id=1, source_target_pairs={{0,4},{2,6},{4,0},{6,2},{1,5},{3,7},{5,1},{7,3},{8,12},{10,14},{12... | collective-permute-start | bytes 172040 | tf_op jit(solution)/shard_map/ppermute | solution.py:333
  5.3 5.6 %collective-permute-start = (bf16[1,224,128]{2,1,0:T(8,128)(2,1)S(1)}, bf16[1,224,128]{2,1,0:T(8,128)(2,1)}, u32[]{:S(2)}, u32[]{:S(2)}) collective-permute-start(bf16[1,224,128]{2,1,0:T(8,128)(2,1)S(1)} %fusion.4), channel_id=1, source_target_pairs={{0,2},{2,4},{4,6},{6,0},{1,3},{3,5},{5,7},{7,1},{8,10},{10,12},{12... | collective-permute-start | bytes 172040 | tf_op jit(solution)/shard_map/ppermute | solution.py:333
  11.7 13.1 %collective-permute-start.5 = (bf16[4,224,128]{2,1,0:T(8,128)(2,1)S(1)}, bf16[4,224,128]{2,1,0:T(8,128)(2,1)S(1)}, u32[]{:S(2)}, u32[]{:S(2)}) collective-permute-start(bf16[4,224,128]{2,1,0:T(8,128)(2,1)S(1)} %pad_maximum_fusion.3), channel_id=1, source_target_pairs={{0,24},{8,0},{16,8},{24,16},{1,25},{9,1},{17,9},{25,17},{2,26},{10... | collective-permute-start | bytes 688136 | tf_op jit(solution)/shard_map/ppermute | solution.py:333
  15.8 9.7 %collective-permute-start.4 = (bf16[4,224,128]{2,1,0:T(8,128)(2,1)S(1)}, bf16[4,224,128]{2,1,0:T(8,128)(2,1)S(1)}, u32[]{:S(2)}, u32[]{:S(2)}) collective-permute-start(bf16[4,224,128]{2,1,0:T(8,128)(2,1)S(1)} %pad_maximum_fusion.3), channel_id=1, source_target_pairs={{0,16},{8,24},{16,0},{24,8},{1,17},{9,25},{17,1},{25,9},{2,18},{10... | collective-permute-start | bytes 688136 | tf_op jit(solution)/shard_map/ppermute | solution.py:333
  15.8 11.8 %collective-permute-start.3 = (bf16[4,224,128]{2,1,0:T(8,128)(2,1)S(1)}, bf16[4,224,128]{2,1,0:T(8,128)(2,1)S(1)}, u32[]{:S(2)}, u32[]{:S(2)}) collective-permute-start(bf16[4,224,128]{2,1,0:T(8,128)(2,1)S(1)} %pad_maximum_fusion.3), channel_id=1, source_target_pairs={{0,8},{8,16},{16,24},{24,0},{1,9},{9,17},{17,25},{25,1},{2,10},{10... | collective-permute-start | bytes 688136 | tf_op jit(solution)/shard_map/ppermute | solution.py:333
  22.8 1.9 copy-start.5
  27.7 32.0 %copy-start.10 = (bf16[16,224,128]{2,1,0:T(8,128)(2,1)}, bf16[16,224,128]{2,1,0:T(8,128)(2,1)S(1)}, u32[]{:S(2)}) copy-start(bf16[16,224,128]{2,1,0:T(8,128)(2,1)S(1)} %pad_maximum_fusion.refs_5_) | copy-start | bytes 2752516
  27.7 55.5 %all-to-all-start = ((bf16[32,80,768]{2,1,0:T(8,128)(2,1)}), bf16[32,80,768]{2,1,0:T(8,128)(2,1)}, u32[]{:S(2)}, u32[]{:S(2)}) async-start(bf16[32,80,768]{2,1,0:T(8,128)(2,1)} %copy-done.5), calls=%async_computation | async-start | bytes 7864320 | tf_op jit(solution)/shard_map/all_to_all | solution.py:328
  32.6 23.7 %collective-permute-start.6 = (bf16[16,224,128]{2,1,0:T(8,128)(2,1)S(1)}, bf16[16,224,128]{2,1,0:T(8,128)(2,1)S(1)}, u32[]{:S(2)}, u32[]{:S(2)}) collective-permute-start(bf16[16,224,128]{2,1,0:T(8,128)(2,1)S(1)} %pad_maximum_fusion.refs_5_), channel_id=1, source_target_pairs={{0,32},{32,64},{64,96},{96,0},{1,33},{33,65},{65,97},{97,1},{2,34}... | collective-permute-start | bytes 2752520 | tf_op jit(solution)/shard_map/ppermute | solution.py:333
  34.2 22.5 %collective-permute-start.8 = (bf16[16,224,128]{2,1,0:T(8,128)(2,1)S(1)}, bf16[16,224,128]{2,1,0:T(8,128)(2,1)S(1)}, u32[]{:S(2)}, u32[]{:S(2)}) collective-permute-start(bf16[16,224,128]{2,1,0:T(8,128)(2,1)S(1)} %pad_maximum_fusion.refs_5_), channel_id=1, source_target_pairs={{0,96},{32,0},{64,32},{96,64},{1,97},{33,1},{65,33},{97,65},{2,98}... | collective-permute-start | bytes 2752520 | tf_op jit(solution)/shard_map/ppermute | solution.py:333
  56.3 13.3 %copy-start.11 = (bf16[16,224,128]{2,1,0:T(8,128)(2,1)}, bf16[16,224,128]{2,1,0:T(8,128)(2,1)S(1)}, u32[]{:S(2)}) copy-start(bf16[16,224,128]{2,1,0:T(8,128)(2,1)S(1)} %collective-permute-done.6.refs_6_) | copy-start | bytes 2752516
  56.3 13.1 %collective-permute-start.7 = (bf16[8,224,128]{2,1,0:T(8,128)(2,1)S(1)}, bf16[8,224,128]{2,1,0:T(8,128)(2,1)S(1)}, u32[]{:S(2)}, u32[]{:S(2)}) collective-permute-start(bf16[8,224,128]{2,1,0:T(8,128)(2,1)S(1)} %slice.101), channel_id=1, source_target_pairs={{0,32},{32,64},{64,96},{96,0},{1,33},{33,65},{65,97},{97,1},{2,34}... | collective-permute-start | bytes 1376264 | tf_op jit(solution)/shard_map/ppermute | solution.py:333
  56.7 26.5 %copy-start.12 = (bf16[16,224,128]{2,1,0:T(8,128)(2,1)}, bf16[16,224,128]{2,1,0:T(8,128)(2,1)S(1)}, u32[]{:S(2)}) copy-start(bf16[16,224,128]{2,1,0:T(8,128)(2,1)S(1)} %collective-permute-done.8.refs_8_) | copy-start | bytes 2752516
  56.7 12.8 %collective-permute-start.9 = (bf16[8,224,128]{2,1,0:T(8,128)(2,1)S(1)}, bf16[8,224,128]{2,1,0:T(8,128)(2,1)S(1)}, u32[]{:S(2)}, u32[]{:S(2)}) collective-permute-start(bf16[8,224,128]{2,1,0:T(8,128)(2,1)S(1)} %slice.102), channel_id=1, source_target_pairs={{0,96},{32,0},{64,32},{96,64},{1,97},{33,1},{65,33},{97,65},{2,98}... | collective-permute-start | bytes 1376264 | tf_op jit(solution)/shard_map/ppermute | solution.py:333
  59.7 10.0 %collective-permute-start.10 = (bf16[16,224,128]{2,1,0:T(8,128)(2,1)S(1)}, bf16[16,224,128]{2,1,0:T(8,128)(2,1)S(1)}, u32[]{:S(2)}, u32[]{:S(2)}) collective-permute-start(bf16[16,224,128]{2,1,0:T(8,128)(2,1)S(1)} %pad_maximum_fusion.refs_5_), channel_id=1, source_target_pairs={{0,1},{1,0},{2,3},{3,2},{4,5},{5,4},{6,7},{7,6},{8,9},{9,8},{10,11... | collective-permute-start | bytes 2752520 | tf_op jit(solution)/shard_map/ppermute | solution.py:333
  59.7 10.0 %collective-permute-start.13 = (bf16[16,224,128]{2,1,0:T(8,128)(2,1)S(1)}, bf16[16,224,128]{2,1,0:T(8,128)(2,1)S(1)}, u32[]{:S(2)}, u32[]{:S(2)}) collective-permute-start(bf16[16,224,128]{2,1,0:T(8,128)(2,1)S(1)} %collective-permute-done.8.refs_8_), channel_id=1, source_target_pairs={{0,1},{1,0},{2,3},{3,2},{4,5},{5,4},{6,7},{7,6},{8,9},{9,8},{10,11... | collective-permute-start | bytes 2752520 | tf_op jit(solution)/shard_map/ppermute | solution.py:333
  60.3 9.5 %collective-permute-start.11 = (bf16[16,224,128]{2,1,0:T(8,128)(2,1)S(1)}, bf16[16,224,128]{2,1,0:T(8,128)(2,1)S(1)}, u32[]{:S(2)}, u32[]{:S(2)}) collective-permute-start(bf16[16,224,128]{2,1,0:T(8,128)(2,1)S(1)} %collective-permute-done.6.refs_6_), channel_id=1, source_target_pairs={{0,1},{1,0},{2,3},{3,2},{4,5},{5,4},{6,7},{7,6},{8,9},{9,8},{10,11... | collective-permute-start | bytes 2752520 | tf_op jit(solution)/shard_map/ppermute | solution.py:333
  69.6 2.7 %collective-permute-start.12 = (bf16[16,224,128]{2,1,0:T(8,128)(2,1)S(1)}, bf16[16,224,128]{2,1,0:T(8,128)(2,1)}, u32[]{:S(2)}, u32[]{:S(2)}) collective-permute-start(bf16[16,224,128]{2,1,0:T(8,128)(2,1)S(1)} %constant_dynamic-update-slice_fusion.refs_7_), channel_id=1, source_target_pairs={{0,1},{1,0},{2,3},{3,2},{4,5},{5,4},{6,7},{7,6},{8,9},{9,8},{10,11... | collective-permute-start | bytes 2752520 | tf_op jit(solution)/shard_map/ppermute | solution.py:333
  83.2 37.2 %all-to-all-start.2 = ((bf16[32,48,768]{2,1,0:T(8,128)(2,1)}), bf16[32,48,768]{2,1,0:T(8,128)(2,1)S(1)}, u32[]{:S(2)}, u32[]{:S(2)}) async-start(bf16[32,48,768]{2,1,0:T(8,128)(2,1)} %get-tuple-element.90), calls=%async_computation.2 | async-start | bytes 4718592 | tf_op jit(solution)/shard_map/all_to_all | solution.py:328
  121.9 57.5 %all-to-all-start.1 = ((bf16[32,80,768]{2,1,0:T(8,128)(2,1)}), bf16[32,80,768]{2,1,0:T(8,128)(2,1)}, u32[]{:S(2)}, u32[]{:S(2)}) async-start(bf16[32,80,768]{2,1,0:T(8,128)(2,1)} %get-tuple-element.86), calls=%async_computation.1 | async-start | bytes 7864320 | tf_op jit(solution)/shard_map/all_to_all | solution.py:328
  154.4 2.8 %collective-permute-start.16 = (bf16[16,224,128]{2,1,0:T(8,128)(2,1)}, bf16[16,224,128]{2,1,0:T(8,128)(2,1)S(1)}, u32[]{:S(2)}, u32[]{:S(2)}) collective-permute-start(bf16[16,224,128]{2,1,0:T(8,128)(2,1)} %get-tuple-element.105), channel_id=1, source_target_pairs={{0,1},{1,0},{2,3},{3,2},{4,5},{5,4},{6,7},{7,6},{8,9},{9,8},{10,11... | collective-permute-start | bytes 2752520 | tf_op jit(solution)/shard_map/ppermute | solution.py:333
  154.6 7.5 %collective-permute-start.15 = (bf16[16,224,128]{2,1,0:T(8,128)(2,1)}, bf16[16,224,128]{2,1,0:T(8,128)(2,1)S(1)}, u32[]{:S(2)}, u32[]{:S(2)}) collective-permute-start(bf16[16,224,128]{2,1,0:T(8,128)(2,1)} %get-tuple-element.103), channel_id=1, source_target_pairs={{0,1},{1,0},{2,3},{3,2},{4,5},{5,4},{6,7},{7,6},{8,9},{9,8},{10,11... | collective-permute-start | bytes 2752520 | tf_op jit(solution)/shard_map/ppermute | solution.py:333
  155.0 7.3 %collective-permute-start.18 = (bf16[16,224,128]{2,1,0:T(8,128)(2,1)}, bf16[16,224,128]{2,1,0:T(8,128)(2,1)S(1)}, u32[]{:S(2)}, u32[]{:S(2)}) collective-permute-start(bf16[16,224,128]{2,1,0:T(8,128)(2,1)} %get-tuple-element.107), channel_id=1, source_target_pairs={{0,1},{1,0},{2,3},{3,2},{4,5},{5,4},{6,7},{7,6},{8,9},{9,8},{10,11... | collective-permute-start | bytes 2752520 | tf_op jit(solution)/shard_map/ppermute | solution.py:333
  157.2 4.9 %copy-start.15 = (bf16[16,224,128]{2,1,0:T(8,128)(2,1)S(1)}, bf16[16,224,128]{2,1,0:T(8,128)(2,1)}, u32[]{:S(2)}) copy-start(bf16[16,224,128]{2,1,0:T(8,128)(2,1)} %get-tuple-element.102) | copy-start | bytes 2752516
  158.8 15.0 %collective-permute-start.19 = (bf16[8,224,128]{2,1,0:T(8,128)(2,1)S(1)}, bf16[8,224,128]{2,1,0:T(8,128)(2,1)S(1)}, u32[]{:S(2)}, u32[]{:S(2)}) collective-permute-start(bf16[8,224,128]{2,1,0:T(8,128)(2,1)S(1)} %get-tuple-element.138), channel_id=1, source_target_pairs={{0,32},{32,64},{64,96},{96,0},{1,33},{33,65},{65,97},{97,1},{2,34}... | collective-permute-start | bytes 1376264 | tf_op jit(solution)/shard_map/ppermute | solution.py:333
  160.4 12.3 %collective-permute-start.17 = (bf16[8,224,128]{2,1,0:T(8,128)(2,1)S(1)}, bf16[8,224,128]{2,1,0:T(8,128)(2,1)S(1)}, u32[]{:S(2)}, u32[]{:S(2)}) collective-permute-start(bf16[8,224,128]{2,1,0:T(8,128)(2,1)S(1)} %get-tuple-element.139), channel_id=1, source_target_pairs={{0,96},{32,0},{64,32},{96,64},{1,97},{33,1},{65,33},{97,65},{2,98}... | collective-permute-start | bytes 1376264 | tf_op jit(solution)/shard_map/ppermute | solution.py:333
  179.3 38.3 %all-to-all-start.3 = ((bf16[32,48,768]{2,1,0:T(8,128)(2,1)}), bf16[32,48,768]{2,1,0:T(8,128)(2,1)S(1)}, u32[]{:S(2)}, u32[]{:S(2)}) async-start(bf16[32,48,768]{2,1,0:T(8,128)(2,1)} %get-tuple-element.111), calls=%async_computation.3 | async-start | bytes 4718592 | tf_op jit(solution)/shard_map/all_to_all | solution.py:328
  183.4 12.0 %collective-permute-start.14 = (bf16[16,224,128]{2,1,0:T(8,128)(2,1)}, bf16[16,224,128]{2,1,0:T(8,128)(2,1)S(1)}, u32[]{:S(2)}, u32[]{:S(2)}) collective-permute-start(bf16[16,224,128]{2,1,0:T(8,128)(2,1)} %get-tuple-element.100), channel_id=1, source_target_pairs={{0,1},{1,0},{2,3},{3,2},{4,5},{5,4},{6,7},{7,6},{8,9},{9,8},{10,11... | collective-permute-start | bytes 2752520 | tf_op jit(solution)/shard_map/ppermute | solution.py:333
  183.6 23.4 %collective-permute-start.20 = (bf16[16,224,128]{2,1,0:T(8,128)(2,1)}, bf16[16,224,128]{2,1,0:T(8,128)(2,1)S(1)}, u32[]{:S(2)}, u32[]{:S(2)}) collective-permute-start(bf16[16,224,128]{2,1,0:T(8,128)(2,1)} %pad_maximum_fusion.1), channel_id=1, source_target_pairs={{0,96},{32,0},{64,32},{96,64},{1,97},{33,1},{65,33},{97,65},{2,98}... | collective-permute-start | bytes 2752520 | tf_op jit(solution)/shard_map/ppermute | solution.py:333
  186.6 23.7 %collective-permute-start.21 = (bf16[16,224,128]{2,1,0:T(8,128)(2,1)}, bf16[16,224,128]{2,1,0:T(8,128)(2,1)S(1)}, u32[]{:S(2)}, u32[]{:S(2)}) collective-permute-start(bf16[16,224,128]{2,1,0:T(8,128)(2,1)} %pad_maximum_fusion.2), channel_id=1, source_target_pairs={{0,32},{32,64},{64,96},{96,0},{1,33},{33,65},{65,97},{97,1},{2,34}... | collective-permute-start | bytes 2752520 | tf_op jit(solution)/shard_map/ppermute | solution.py:333
  186.6 1.6 copy-start.3
  188.2 22.2 %copy-start.16 = (bf16[16,224,128]{2,1,0:T(8,128)(2,1)S(1)}, bf16[16,224,128]{2,1,0:T(8,128)(2,1)}, u32[]{:S(2)}) copy-start(bf16[16,224,128]{2,1,0:T(8,128)(2,1)} %get-tuple-element.99) | copy-start | bytes 2752516
  211.7 11.3 %collective-permute-start.24 = (bf16[4,224,128]{2,1,0:T(8,128)(2,1)}, bf16[4,224,128]{2,1,0:T(8,128)(2,1)}, u32[]{:S(2)}, u32[]{:S(2)}) collective-permute-start(bf16[4,224,128]{2,1,0:T(8,128)(2,1)} %get-tuple-element.134), channel_id=1, source_target_pairs={{0,8},{8,16},{16,24},{24,0},{1,9},{9,17},{17,25},{25,1},{2,10},{10... | collective-permute-start | bytes 688136 | tf_op jit(solution)/shard_map/ppermute | solution.py:333
  213.5 12.7 %collective-permute-start.23 = (bf16[4,224,128]{2,1,0:T(8,128)(2,1)}, bf16[4,224,128]{2,1,0:T(8,128)(2,1)}, u32[]{:S(2)}, u32[]{:S(2)}) collective-permute-start(bf16[4,224,128]{2,1,0:T(8,128)(2,1)} %get-tuple-element.135), channel_id=1, source_target_pairs={{0,16},{8,24},{16,0},{24,8},{1,17},{9,25},{17,1},{25,9},{2,18},{10... | collective-permute-start | bytes 688136 | tf_op jit(solution)/shard_map/ppermute | solution.py:333
  216.2 9.9 %collective-permute-start.22 = (bf16[4,224,128]{2,1,0:T(8,128)(2,1)}, bf16[4,224,128]{2,1,0:T(8,128)(2,1)}, u32[]{:S(2)}, u32[]{:S(2)}) collective-permute-start(bf16[4,224,128]{2,1,0:T(8,128)(2,1)} %get-tuple-element.136), channel_id=1, source_target_pairs={{0,24},{8,0},{16,8},{24,16},{1,25},{9,1},{17,9},{25,17},{2,26},{10... | collective-permute-start | bytes 688136 | tf_op jit(solution)/shard_map/ppermute | solution.py:333
  217.7 1.6 copy-start.4
  227.5 7.6 %collective-permute-start.27 = (bf16[1,224,128]{2,1,0:T(8,128)(2,1)S(1)}, bf16[1,224,128]{2,1,0:T(8,128)(2,1)S(1)}, u32[]{:S(2)}, u32[]{:S(2)}) collective-permute-start(bf16[1,224,128]{2,1,0:T(8,128)(2,1)S(1)} %get-tuple-element.144), channel_id=1, source_target_pairs={{0,2},{2,4},{4,6},{6,0},{1,3},{3,5},{5,7},{7,1},{8,10},{10,12},{12... | collective-permute-start | bytes 172040 | tf_op jit(solution)/shard_map/ppermute | solution.py:333
  229.1 10.9 %collective-permute-start.30 = (bf16[256,128]{1,0:T(8,128)(2,1)S(1)}, bf16[256,128]{1,0:T(8,128)(2,1)S(1)}, u32[]{:S(2)}, u32[]{:S(2)}) collective-permute-start(bf16[256,128]{1,0:T(8,128)(2,1)S(1)} %get-tuple-element.140), channel_id=1, source_target_pairs={{0,32},{32,64},{64,96},{96,0},{1,33},{33,65},{65,97},{97,1},{2,34}... | collective-permute-start | bytes 196616 | tf_op jit(solution)/shard_map/ppermute | solution.py:333
  229.2 10.8 %collective-permute-start.29 = (bf16[256,128]{1,0:T(8,128)(2,1)S(1)}, bf16[256,128]{1,0:T(8,128)(2,1)S(1)}, u32[]{:S(2)}, u32[]{:S(2)}) collective-permute-start(bf16[256,128]{1,0:T(8,128)(2,1)S(1)} %get-tuple-element.141), channel_id=1, source_target_pairs={{0,64},{32,96},{64,0},{96,32},{1,65},{33,97},{65,1},{97,33},{2,66}... | collective-permute-start | bytes 196616 | tf_op jit(solution)/shard_map/ppermute | solution.py:333
  231.6 8.4 %collective-permute-start.28 = (bf16[256,128]{1,0:T(8,128)(2,1)S(1)}, bf16[256,128]{1,0:T(8,128)(2,1)S(1)}, u32[]{:S(2)}, u32[]{:S(2)}) collective-permute-start(bf16[256,128]{1,0:T(8,128)(2,1)S(1)} %get-tuple-element.142), channel_id=1, source_target_pairs={{0,96},{32,0},{64,32},{96,64},{1,97},{33,1},{65,33},{97,65},{2,98}... | collective-permute-start | bytes 196616 | tf_op jit(solution)/shard_map/ppermute | solution.py:333
  232.8 7.2 %collective-permute-start.26 = (bf16[1,224,128]{2,1,0:T(8,128)(2,1)S(1)}, bf16[1,224,128]{2,1,0:T(8,128)(2,1)S(1)}, u32[]{:S(2)}, u32[]{:S(2)}) collective-permute-start(bf16[1,224,128]{2,1,0:T(8,128)(2,1)S(1)} %get-tuple-element.145), channel_id=1, source_target_pairs={{0,4},{2,6},{4,0},{6,2},{1,5},{3,7},{5,1},{7,3},{8,12},{10,14},{12... | collective-permute-start | bytes 172040 | tf_op jit(solution)/shard_map/ppermute | solution.py:333
  235.1 4.9 %collective-permute-start.25 = (bf16[1,224,128]{2,1,0:T(8,128)(2,1)S(1)}, bf16[1,224,128]{2,1,0:T(8,128)(2,1)S(1)}, u32[]{:S(2)}, u32[]{:S(2)}) collective-permute-start(bf16[1,224,128]{2,1,0:T(8,128)(2,1)S(1)} %get-tuple-element.146), channel_id=1, source_target_pairs={{0,6},{2,0},{4,2},{6,4},{1,7},{3,1},{5,3},{7,5},{8,14},{10,8},{12,... | collective-permute-start | bytes 172040 | tf_op jit(solution)/shard_map/ppermute | solution.py:333
  236.6 6.1 %copy-start.1 = (f32[512]{0:T(512)S(1)}, f32[512]{0:T(512)}, u32[]{:S(2)}) copy-start(f32[512]{0:T(512)} %param.20) | copy-start | bytes 6148
  (7 other events, 8.4 us)

commit v3 on v2

--- a/solution.py
+++ b/solution.py
@@ -54,7 +54,7 @@
             pl.BlockSpec(wd.shape, lambda i: (0, 0)),
         ],
         out_specs=[pl.BlockSpec((rows // nb, n, width + 256), lambda i: (i, 0, 0)) for n in parts],
-        out_shape=[jax.ShapeDtypeStruct((total // nb, n, width + 256), BF16) for n in parts],
+        out_shape=[pltpu.HBM((total // nb, n, width + 256), BF16) for n in parts],
         compiler_params=pltpu.CompilerParams(vmem_limit_bytes=40 * MIB),
         cost_estimate=pl.CostEstimate(
             flops=2 * total * 256 * width, bytes_accessed=total * 2 * (480 + 768), transcendentals=0
@@ -225,7 +225,7 @@
                 pltpu.VMEM((UNROLL, 128, width), F32),
             ],
         ),
-        out_shape=[jax.ShapeDtypeStruct((ntab, nb, full), BF16)]
+        out_shape=[pltpu.HBM((ntab, nb, full), BF16)]
         + [jax.ShapeDtypeStruct((16, ROWS, 128), BF16)] * 8,
         compiler_params=pltpu.CompilerParams(vmem_limit_bytes=58 * MIB),
         cost_estimate=pl.CostEstimate(
@@ -346,8 +346,33 @@
     return jnp.take(blocks, order, axis=1).reshape(w.shape)
 
 
-def gather_axis(part, axis):
-    return jnp.concatenate([part, shift(part, axis, 1), shift(part, axis, 2), shift(part, axis, -1)])
+def cross_shift(x, k, swap):
+    moves = []
+    for z in range(4):
+        for xx in range(4):
+            for c in range(2):
+                along_x = (c == 0) != swap
+                to = (z, (xx + k) % 4) if along_x else ((z + k) % 4, xx)
+                moves.append((z * 8 + xx * 2 + c, to[0] * 8 + to[1] * 2 + c))
+    return lax.ppermute(x, PLANE, moves)
+
+
+def gather_plane(part):
+    part = jnp.concatenate([part] + [cross_shift(part, k, False) for k in (1, 2, 3)])
+    pieces = [part] + [cross_shift(part, k, True) for k in (1, 2, 3)]
+    first = lax.axis_index("c") == 0
+    pieces = jnp.where(first, jnp.stack(pieces), jnp.stack(pieces, axis=1))
+    return pieces.reshape((16,) + part.shape[1:])
+
+
+def scatter_outer(part):
+    part = part.reshape((4, 4) + part.shape[1:])
+    part = jnp.where(lax.axis_index("c") == 0, part, part.swapaxes(0, 1))
+    return [part[0]] + [cross_shift(part[k], -k, True) for k in (1, 2, 3)]
+
+
+def scatter_inner(part):
+    return [part[0]] + [cross_shift(part[k], -k, False) for k in (1, 2, 3)]
 
 
 def gather_quarters(part):
@@ -368,11 +393,6 @@
 
 def scatter_near(own, down, up):
     return add(own, shift(down, "y", -1), shift(up, "y", 1)).astype(BF16)
-
-
-def scatter_axis(part, axis):
-    n = part.shape[0] // 4
-    return (part[:n],) + tuple(shift(part[k * n : (k + 1) * n], axis, -k) for k in (1, 2, 3))
 
 
 def on_device(
@@ -388,9 +408,7 @@
     gain = turn_features(norm_gain[None], y)
     d = pooled_d[:, 0]
     part = jnp.concatenate([proj_c[0], proj_b[0], proj_a[0]], axis=0)
-    part = gather_axis(lax.dynamic_slice_in_dim(part, y * 128, 128, axis=1)[None], "x")
-    wd, part = lax.optimization_barrier((wd, part))
-    part = gather_axis(part, "z")
+    part = gather_plane(lax.dynamic_slice_in_dim(part, y * 128, 128, axis=1)[None])
     us = owner_forward(
         pooled_a.transpose(1, 2, 0)[0], pooled_b.transpose(1, 2, 0)[0], pooled_c[:, 0], d, wd, nb
     )
@@ -415,21 +433,21 @@
     gd, gc = gd.reshape(total, -1), gc.reshape(total, -1)
     q = [gwd[:, r * 128 : (r + 1) * 128] for r in range(4)]
     q = [q[0]] + [shift(q[r], "y", -r) for r in (1, 2, 3)]
-    pieces, _ = lax.optimization_barrier((scatter_axis(part, "z"), gwd))
-    pieces = scatter_axis(add(*pieces).astype(BF16), "x")
+    pieces, _ = lax.optimization_barrier((scatter_outer(part), gwd))
+    pieces = scatter_inner(add(*pieces).astype(BF16))
     gat, gbt = owner_split((gu0, gu1))
     pieces, q, gat, gbt = lax.optimization_barrier((pieces, q, gat, gbt))
     scale = 1.0 / np.sqrt(total * lax.axis_size("y")).astype(np.float32)
-    gw = add(*pieces)[0] * scale
+    gw = lambda start, stop: add(*[p[None, start:stop] for p in pieces]) * scale
     gwd = add(*q) * scale
     return (
         gat.T[:, None],
         gbt.T[:, None],
         gc[:, None],
         gd[:, None],
-        gw[192:224][None],
-        gw[128:192][None],
-        gw[0:128][None],
+        gw(192, 224),
+        gw(128, 192),
+        gw(0, 128),
         gwd[None],
     )
 

time: 244 us -> 239 us (0.980)
  waiting for transfers between devices: 80.6 us -> 74.8 us
  local copies, waits for them, and re-layouts: 16.9 us -> 13.1 us
    ppermute x0 -> x12, starting transfers between devices: none -> 23.3 us  [cross_shift(): return lax.ppermute(x, PLANE, moves)]
    ppermute x31 -> x19, starting transfers between devices: 39.3 us -> 17.8 us  [shift(): return lax.ppermute(x, axis, [(i, (i + k) % n) for i in range(n)])]
    ppermute x31 -> x19, waiting for transfers between devices: 64.6 us -> 56 us  [shift(): return lax.ppermute(x, axis, [(i, (i + k) % n) for i in range(n)])]
    ppermute x0 -> x12, waiting for transfers between devices: none -> 2.74 us  [cross_shift(): return lax.ppermute(x, PLANE, moves)]
    slice x5 -> x0, local copies, waits for them, and re-layouts: 2.74 us -> none  [the longest x2 0.88 us: scatter_axis(): part[k * n:(k + 1) * n]]
    unnamed x43 -> x41, local copies, waits for them, and re-layouts: 12.4 us -> 10.4 us
  transfers between devices with their start and end apart: 35 -> 35, of which waited for: 15 -> 12; matrix products, arithmetic and copies ran while one was open for 4% -> 4% of each run, Pallas kernels for 31% -> 32%
where the time goes in v3:
time: 239 us; the launch traced here: 238 us
  Pallas kernels  75.6 us (32%)
  waiting for transfers between devices  74.8 us (31%)
  starting transfers between devices  61.2 us (26%)
  local copies, waits for them, and re-layouts  13.1 us (5%)
  other arithmetic  11.9 us (5%)
    pallas_call x2, Pallas kernels, middle(): pl.pallas_call(lambda *refs: middle_body(steps, len(before) > 0, *refs),...  56 us
    ppermute x19, waiting for transfers between devices, shift(): return lax.ppermute(x, axis, [(i, (i + k) % n) for i in range(n)])  56 us
    ppermute x12, starting transfers between devices, cross_shift(): return lax.ppermute(x, PLANE, moves)  23.3 us
    all_to_all x4, starting transfers between devices, exchange(): return lax.all_to_all(x, PLANE, split_axis=0, concat_axis=0, tiled=True)  20 us
    ppermute x19, starting transfers between devices, shift(): return lax.ppermute(x, axis, [(i, (i + k) % n) for i in range(n)])  17.8 us
    all_to_all x4, waiting for transfers between devices, exchange(): return lax.all_to_all(x, PLANE, split_axis=0, concat_axis=0, tiled=True)  16 us
    pallas_call x2, Pallas kernels, owner_backward(): pl.pallas_call(lambda *refs: owner_backward_body(later, *refs), grid=(par...  11 us
    unnamed x41, local copies, waits for them, and re-layouts  10.4 us
  transfers between devices with their start and end apart: 35, of which 12 were waited for; matrix products, arithmetic and copies ran while one was open for 4% of the time, Pallas kernels for 32%

profile of v3, /device:TPU:0, one launch (start us, length us, event | category | flops | bytes accessed | tf_op | source)
XLA Modules:
  0.0 237.5 jit_solution(15201819412280312659)
XLA Ops:
  1.6 2.8 %collective-permute-start.2 = (bf16[1,224,128]{2,1,0:T(8,128)(2,1)S(1)}, bf16[1,224,128]{2,1,0:T(8,128)(2,1)S(1)}, u32[]{:S(2)}, u32[]{:S(2)}) collective-permute-start(bf16[1,224,128]{2,1,0:T(8,128)(2,1)S(1)} %fusion.4), channel_id=1, source_target_pairs={{0,6},{1,25},{2,0},{3,27},{4,2},{5,29},{6,4},{7,31},{8,14},{9,1},{... | collective-permute-start | bytes 172040 | tf_op jit(solution)/shard_map/ppermute | solution.py:357
  6.2 1.1 copy.30
  8.1 2.1 collective-permute-done.1
  11.8 4.0 %collective-permute-start.4 = (bf16[4,224,128]{2,1,0:T(8,128)(2,1)S(1)}, bf16[4,224,128]{2,1,0:T(8,128)(2,1)S(1)}, u32[]{:S(2)}, u32[]{:S(2)}) collective-permute-start(bf16[4,224,128]{2,1,0:T(8,128)(2,1)S(1)} %get-tuple-element.146), channel_id=1, source_target_pairs={{0,16},{1,5},{2,18},{3,7},{4,20},{5,1},{6,22},{7,3},{8,24},{9,13},... | collective-permute-start | bytes 688136 | tf_op jit(solution)/shard_map/ppermute | solution.py:357
  15.7 1.0 collective-permute-start.3
  16.7 2.2 collective-permute-start.5
  19.0 1.2 copy-done.5
  20.3 5.2 %owner_forward.1 = (bf16[32,80,768]{2,1,0:T(8,128)(2,1)}, bf16[32,48,768]{2,1,0:T(8,128)(2,1)}) custom-call(bf16[32,4096]{1,0:T(8,128)(2,1)S(1)} %bitcast.93, bf16[64,4096]{1,0:T(8,128)(2,1)S(1)} %bitcast.92, bf16[4096,128]{1,0:T(8,128)(2,1)S(1)} %bitcast.91, bf16[4096,256]{1,0:T(8,128)(2,1)S(1)} %bitcast.88, ...), custom_call_target="tpu_custom_call" | custom-call | flops 1073741824 | bytes 10223616 | tf_op jit(solution)/shard_map/owner_forward/pallas_call | solution.py:46
  25.7 4.8 %all-to-all-start = ((bf16[32,80,768]{2,1,0:T(8,128)(2,1)}), bf16[32,80,768]{2,1,0:T(8,128)(2,1)}, u32[]{:S(2)}, u32[]{:S(2)}) async-start(bf16[32,80,768]{2,1,0:T(8,128)(2,1)} %get-tuple-element.71), calls=%async_computation | async-start | bytes 7864320 | tf_op jit(solution)/shard_map/all_to_all | solution.py:328
  30.5 1.7 collective-permute-start.6
  32.2 1.6 collective-permute-start.8
  33.8 20.4 %collective-permute-done.6.refs_6_ = bf16[16,224,128]{2,1,0:T(8,128)(2,1)S(1)} collective-permute-done((bf16[16,224,128]{2,1,0:T(8,128)(2,1)S(1)}, bf16[16,224,128]{2,1,0:T(8,128)(2,1)S(1)}, u32[]{:S(2)}, u32[]{:S(2)}) %collective-permute-start.6) | collective-permute-done | bytes 917536 | tf_op jit(solution)/shard_map/ppermute | solution.py:333
  54.7 3.0 %collective-permute-start.9 = (bf16[8,224,128]{2,1,0:T(8,128)(2,1)S(1)}, bf16[8,224,128]{2,1,0:T(8,128)(2,1)S(1)}, u32[]{:S(2)}, u32[]{:S(2)}) collective-permute-start(bf16[8,224,128]{2,1,0:T(8,128)(2,1)S(1)} %slice.135), channel_id=1, source_target_pairs={{0,96},{32,0},{64,32},{96,64},{1,97},{33,1},{65,33},{97,65},{2,98}... | collective-permute-start | bytes 1376264 | tf_op jit(solution)/shard_map/ppermute | solution.py:333
  58.2 9.2 %collective-permute-done.7 = bf16[8,224,128]{2,1,0:T(8,128)(2,1)S(1)} collective-permute-done((bf16[8,224,128]{2,1,0:T(8,128)(2,1)S(1)}, bf16[8,224,128]{2,1,0:T(8,128)(2,1)S(1)}, u32[]{:S(2)}, u32[]{:S(2)}) %collective-permute-start.7) | collective-permute-done | bytes 458784 | tf_op jit(solution)/shard_map/ppermute | solution.py:333
  69.1 0.9 copy-done.18
  70.2 10.9 %all-to-all-done.refs_3_.refs_4_ = bf16[32,80,768]{2,1,0:T(8,128)(2,1)} async-done(((bf16[32,80,768]{2,1,0:T(8,128)(2,1)}), bf16[32,80,768]{2,1,0:T(8,128)(2,1)}, u32[]{:S(2)}, u32[]{:S(2)}) %all-to-all-start) | async-done | bytes 3932192 | tf_op jit(solution)/shard_map/all_to_all | solution.py:328
  81.1 4.1 %all-to-all-start.2 = ((bf16[32,48,768]{2,1,0:T(8,128)(2,1)}), bf16[32,48,768]{2,1,0:T(8,128)(2,1)S(1)}, u32[]{:S(2)}, u32[]{:S(2)}) async-start(bf16[32,48,768]{2,1,0:T(8,128)(2,1)} %get-tuple-element.86), calls=%async_computation.2 | async-start | bytes 4718592 | tf_op jit(solution)/shard_map/all_to_all | solution.py:328
  87.0 30.5 %middle.2 = (bf16[32,80,768]{2,1,0:T(8,128)(2,1)}, bf16[16,224,128]{2,1,0:T(8,128)(2,1)}, bf16[16,224,128]{2,1,0:T(8,128)(2,1)}, bf16[16,224,128]{2,1,0:T(8,128)...) custom-call(s32[3]{0:T(128)} %pad_add_fusion.refs_0_, ...), custom_call_target="tpu_custom_call" | custom-call | flops 8000000000 | bytes 35000000 | tf_op jit(solution)/shard_map/middle/pallas_call | solution.py:198
  118.3 1.5 copy-done.8
  119.8 7.0 %all-to-all-start.1 = ((bf16[32,80,768]{2,1,0:T(8,128)(2,1)}), bf16[32,80,768]{2,1,0:T(8,128)(2,1)}, u32[]{:S(2)}, u32[]{:S(2)}) async-start(bf16[32,80,768]{2,1,0:T(8,128)(2,1)} %get-tuple-element.82), calls=%async_computation.1 | async-start | bytes 7864320 | tf_op jit(solution)/shard_map/all_to_all | solution.py:328
  126.8 25.5 %middle.3 = (bf16[32,48,768]{2,1,0:T(8,128)(2,1)}, bf16[16,224,128]{2,1,0:T(8,128)(2,1)}, bf16[16,224,128]{2,1,0:T(8,128)(2,1)}, bf16[16,224,128]{2,1,0:T(8,128)...) custom-call(s32[3]{0:T(128)} %pad_add_fusion.refs_0_, ...), custom_call_target="tpu_custom_call" | custom-call | flops 4800000000 | bytes 35000000 | tf_op jit(solution)/shard_map/middle/pallas_call | solution.py:198
  153.0 2.1 collective-permute-done.16
  155.1 1.5 add_convert_fusion.1
  156.7 1.7 collective-permute-start.19
  158.3 1.6 collective-permute-start.17
  160.2 0.9 copy-done.13
  161.5 9.1 %collective-permute-done.17 = bf16[8,224,128]{2,1,0:T(8,128)(2,1)S(1)} collective-permute-done((bf16[8,224,128]{2,1,0:T(8,128)(2,1)S(1)}, bf16[8,224,128]{2,1,0:T(8,128)(2,1)S(1)}, u32[]{:S(2)}, u32[]{:S(2)}) %collective-permute-start.17) | collective-permute-done | bytes 458784 | tf_op jit(solution)/shard_map/ppermute | solution.py:333
  170.7 1.0 pad_maximum_fusion
  171.8 1.0 pad_maximum_fusion.1
  172.9 4.4 %all-to-all-done.1.refs_0_.refs_1_ = bf16[32,80,768]{2,1,0:T(8,128)(2,1)} async-done(((bf16[32,80,768]{2,1,0:T(8,128)(2,1)}), bf16[32,80,768]{2,1,0:T(8,128)(2,1)}, u32[]{:S(2)}, u32[]{:S(2)}) %all-to-all-start.1) | async-done | bytes 3932192 | tf_op jit(solution)/shard_map/all_to_all | solution.py:328
  177.2 4.1 %all-to-all-start.3 = ((bf16[32,48,768]{2,1,0:T(8,128)(2,1)}), bf16[32,48,768]{2,1,0:T(8,128)(2,1)S(1)}, u32[]{:S(2)}, u32[]{:S(2)}) async-start(bf16[32,48,768]{2,1,0:T(8,128)(2,1)} %get-tuple-element.107), calls=%async_computation.3 | async-start | bytes 4718592 | tf_op jit(solution)/shard_map/all_to_all | solution.py:328
  181.5 3.0 %collective-permute-start.20 = (bf16[16,224,128]{2,1,0:T(8,128)(2,1)}, bf16[16,224,128]{2,1,0:T(8,128)(2,1)S(1)}, u32[]{:S(2)}, u32[]{:S(2)}) collective-permute-start(bf16[16,224,128]{2,1,0:T(8,128)(2,1)} %pad_maximum_fusion), channel_id=1, source_target_pairs={{0,96},{32,0},{64,32},{96,64},{1,97},{33,1},{65,33},{97,65},{2,98}... | collective-permute-start | bytes 2752520 | tf_op jit(solution)/shard_map/ppermute | solution.py:333
  184.6 1.6 copy-done.3
  186.2 7.2 %owner_backward.2 = (bf16[32,128,256]{2,1,0:T(8,128)(2,1)}, bf16[32,128,128]{2,1,0:T(8,128)(2,1)}, f32[256,512]{1,0:T(8,128)S(1)}) custom-call(bf16[32,80,768]{2,1,0:T(8,128)(2,1)} %all-to-all-done.1.refs_0_.refs_1_, bf16[32,80,768]{2,1,0:T(8,128)(2,1)} %all-to-all-done.1.refs_0_.refs_1_, bf16[32,128,256]{2,1,0:T(8,128)(2,1)S(1)} %bitcast.89, ...), custom_call_target="tpu_custom_call" | custom-call | flops 1342177280 | bytes 5242880 | tf_op jit(solution)/shard_map/owner_backward/pallas_call | solution.py:274
  193.3 11.7 %collective-permute-done.20 = bf16[16,224,128]{2,1,0:T(8,128)(2,1)S(1)} collective-permute-done((bf16[16,224,128]{2,1,0:T(8,128)(2,1)}, bf16[16,224,128]{2,1,0:T(8,128)(2,1)S(1)}, u32[]{:S(2)}, u32[]{:S(2)}) %collective-permute-start.20) | collective-permute-done | bytes 917536 | tf_op jit(solution)/shard_map/ppermute | solution.py:333
  205.0 3.3 %collective-permute-done.21 = bf16[16,224,128]{2,1,0:T(8,128)(2,1)S(1)} collective-permute-done((bf16[16,224,128]{2,1,0:T(8,128)(2,1)}, bf16[16,224,128]{2,1,0:T(8,128)(2,1)S(1)}, u32[]{:S(2)}, u32[]{:S(2)}) %collective-permute-start.21) | collective-permute-done | bytes 917536 | tf_op jit(solution)/shard_map/ppermute | solution.py:333
  209.7 1.7 collective-permute-start.24
  211.5 2.8 %collective-permute-start.23 = (bf16[4,224,128]{2,1,0:T(8,128)(2,1)}, bf16[4,224,128]{2,1,0:T(8,128)(2,1)}, u32[]{:S(2)}, u32[]{:S(2)}) collective-permute-start(bf16[4,224,128]{2,1,0:T(8,128)(2,1)} %get-tuple-element.131), channel_id=1, source_target_pairs={{0,16},{1,5},{2,18},{3,7},{4,20},{5,1},{6,22},{7,3},{8,24},{9,13},... | collective-permute-start | bytes 688136 | tf_op jit(solution)/shard_map/ppermute | solution.py:357
  214.3 1.4 collective-permute-start.22
  215.7 1.6 copy-done.4
  217.3 3.8 %owner_backward.3 = (bf16[32,128,256]{2,1,0:T(8,128)(2,1)}, bf16[32,128,128]{2,1,0:T(8,128)(2,1)}, bf16[256,512]{1,0:T(8,128)(2,1)S(1)}) custom-call(bf16[32,48,768]{2,1,0:T(8,128)(2,1)S(1)} %all-to-all-done.3.refs_0_.refs_1_, bf16[32,48,768]{2,1,0:T(8,128)(2,1)S(1)} %all-to-all-done.3.refs_0_.refs_1_, ...), custom_call_target="tpu_custom_call", output_to_operand_aliasing={{0}: (4, {}), {1}: (5, {})} | custom-call | flops 805306368 | bytes 3145728 | tf_op jit(solution)/shard_map/owner_backward/pallas_call | solution.py:274
  221.1 1.3 add_convert_fusion.2
  222.4 1.5 collective-permute-start.27
  224.1 1.7 collective-permute-start.29
  225.8 1.5 collective-permute-start.28
  227.3 2.7 %collective-permute-start.26 = (bf16[224,128]{1,0:T(8,128)(2,1)S(1)}, bf16[224,128]{1,0:T(8,128)(2,1)S(1)}, u32[]{:S(2)}, u32[]{:S(2)}) collective-permute-start(bf16[224,128]{1,0:T(8,128)(2,1)S(1)} %get-tuple-element.141), channel_id=1, source_target_pairs={{0,4},{1,17},{2,6},{3,19},{4,0},{5,21},{6,2},{7,23},{8,12},{9,25},... | collective-permute-start | bytes 172040 | tf_op jit(solution)/shard_map/ppermute | solution.py:357
  230.0 1.5 collective-permute-start.25
  231.5 3.4 %owner_split.1 = (bf16[32,4096]{1,0:T(8,128)(2,1)}, bf16[64,4096]{1,0:T(8,128)(2,1)}) custom-call(bf16[32,80,768]{2,1,0:T(8,128)(2,1)} %all-to-all-done.1.refs_0_.refs_1_, bf16[32,48,768]{2,1,0:T(8,128)(2,1)S(1)} %all-to-all-done.3.refs_0_.refs_1_), custom_call_target="tpu_custom_call" | custom-call | bytes 1835008 | tf_op jit(solution)/shard_map/owner_split/pallas_call | solution.py:307
  (105 shorter events, 16.6 us)
Async XLA Ops:
  0.6 84.6 %copy-start = (f32[512]{0:T(512)S(1)}, f32[512]{0:T(512)}, u32[]{:S(2)}) copy-start(f32[512]{0:T(512)} %param.20) | copy-start | bytes 6148
  0.7 18.3 %copy-start.2 = (bf16[4096,1,256]{2,0,1:T(8,128)(2,1)S(1)}, bf16[4096,1,256]{2,0,1:T(8,128)(2,1)}, u32[]{:S(2)}) copy-start(bf16[4096,1,256]{2,0,1:T(8,128)(2,1)} %param.14) | copy-start | bytes 6291460
  0.7 18.3 %copy-start.6 = (bf16[4096,1,64]{0,2,1:T(8,128)(2,1)S(1)}, bf16[4096,1,64]{0,2,1:T(8,128)(2,1)}, u32[]{:S(2)}) copy-start(bf16[4096,1,64]{0,2,1:T(8,128)(2,1)} %param.12) | copy-start | bytes 1572868
  0.7 18.3 %copy-start.7 = (bf16[4096,1,32]{0,2,1:T(8,128)(2,1)S(1)}, bf16[4096,1,32]{0,2,1:T(8,128)(2,1)}, u32[]{:S(2)}) copy-start(bf16[4096,1,32]{0,2,1:T(8,128)(2,1)} %param.11) | copy-start | bytes 786436
  1.6 6.5 %collective-permute-start.2 = (bf16[1,224,128]{2,1,0:T(8,128)(2,1)S(1)}, bf16[1,224,128]{2,1,0:T(8,128)(2,1)S(1)}, u32[]{:S(2)}, u32[]{:S(2)}) collective-permute-start(bf16[1,224,128]{2,1,0:T(8,128)(2,1)S(1)} %fusion.4), channel_id=1, source_target_pairs={{0,6},{1,25},{2,0},{3,27},{4,2},{5,29},{6,4},{7,31},{8,14},{9,1},{... | collective-permute-start | bytes 172040 | tf_op jit(solution)/shard_map/ppermute | solution.py:357
  4.5 5.8 %collective-permute-start.1 = (bf16[1,224,128]{2,1,0:T(8,128)(2,1)S(1)}, bf16[1,224,128]{2,1,0:T(8,128)(2,1)}, u32[]{:S(2)}, u32[]{:S(2)}) collective-permute-start(bf16[1,224,128]{2,1,0:T(8,128)(2,1)S(1)} %fusion.4), channel_id=1, source_target_pairs={{0,4},{1,17},{2,6},{3,19},{4,0},{5,21},{6,2},{7,23},{8,12},{9,25},... | collective-permute-start | bytes 172040 | tf_op jit(solution)/shard_map/ppermute | solution.py:357
  5.3 5.6 %collective-permute-start = (bf16[1,224,128]{2,1,0:T(8,128)(2,1)S(1)}, bf16[1,224,128]{2,1,0:T(8,128)(2,1)}, u32[]{:S(2)}, u32[]{:S(2)}) collective-permute-start(bf16[1,224,128]{2,1,0:T(8,128)(2,1)S(1)} %fusion.4), channel_id=1, source_target_pairs={{0,2},{1,9},{2,4},{3,11},{4,6},{5,13},{6,0},{7,15},{8,10},{9,17},{... | collective-permute-start | bytes 172040 | tf_op jit(solution)/shard_map/ppermute | solution.py:357
  11.8 13.7 %collective-permute-start.4 = (bf16[4,224,128]{2,1,0:T(8,128)(2,1)S(1)}, bf16[4,224,128]{2,1,0:T(8,128)(2,1)S(1)}, u32[]{:S(2)}, u32[]{:S(2)}) collective-permute-start(bf16[4,224,128]{2,1,0:T(8,128)(2,1)S(1)} %get-tuple-element.146), channel_id=1, source_target_pairs={{0,16},{1,5},{2,18},{3,7},{4,20},{5,1},{6,22},{7,3},{8,24},{9,13},... | collective-permute-start | bytes 688136 | tf_op jit(solution)/shard_map/ppermute | solution.py:357
  15.7 9.7 %collective-permute-start.3 = (bf16[4,224,128]{2,1,0:T(8,128)(2,1)S(1)}, bf16[4,224,128]{2,1,0:T(8,128)(2,1)S(1)}, u32[]{:S(2)}, u32[]{:S(2)}) collective-permute-start(bf16[4,224,128]{2,1,0:T(8,128)(2,1)S(1)} %get-tuple-element.146), channel_id=1, source_target_pairs={{0,8},{1,3},{2,10},{3,5},{4,12},{5,7},{6,14},{7,1},{8,16},{9,11},{... | collective-permute-start | bytes 688136 | tf_op jit(solution)/shard_map/ppermute | solution.py:357
  16.7 8.7 %collective-permute-start.5 = (bf16[4,224,128]{2,1,0:T(8,128)(2,1)S(1)}, bf16[4,224,128]{2,1,0:T(8,128)(2,1)S(1)}, u32[]{:S(2)}, u32[]{:S(2)}) collective-permute-start(bf16[4,224,128]{2,1,0:T(8,128)(2,1)S(1)} %get-tuple-element.146), channel_id=1, source_target_pairs={{0,24},{1,7},{2,26},{3,1},{4,28},{5,3},{6,30},{7,5},{8,0},{9,15},{... | collective-permute-start | bytes 688136 | tf_op jit(solution)/shard_map/ppermute | solution.py:357
  25.7 32.0 %copy-start.9 = (bf16[4,4,224,128]{3,2,1,0:T(8,128)(2,1)}, bf16[4,4,224,128]{3,2,1,0:T(8,128)(2,1)S(1)}, u32[]{:S(2)}) copy-start(bf16[4,4,224,128]{3,2,1,0:T(8,128)(2,1)S(1)} %maximum_select_fusion) | copy-start | bytes 2752516
  25.7 55.5 %all-to-all-start = ((bf16[32,80,768]{2,1,0:T(8,128)(2,1)}), bf16[32,80,768]{2,1,0:T(8,128)(2,1)}, u32[]{:S(2)}, u32[]{:S(2)}) async-start(bf16[32,80,768]{2,1,0:T(8,128)(2,1)} %get-tuple-element.71), calls=%async_computation | async-start | bytes 7864320 | tf_op jit(solution)/shard_map/all_to_all | solution.py:328
  30.5 23.7 %collective-permute-start.6 = (bf16[16,224,128]{2,1,0:T(8,128)(2,1)S(1)}, bf16[16,224,128]{2,1,0:T(8,128)(2,1)S(1)}, u32[]{:S(2)}, u32[]{:S(2)}) collective-permute-start(bf16[16,224,128]{2,1,0:T(8,128)(2,1)S(1)} %bitcast.94), channel_id=1, source_target_pairs={{0,32},{32,64},{64,96},{96,0},{1,33},{33,65},{65,97},{97,1},{2,34}... | collective-permute-start | bytes 2752520 | tf_op jit(solution)/shard_map/ppermute | solution.py:333
  32.2 22.5 %collective-permute-start.8 = (bf16[16,224,128]{2,1,0:T(8,128)(2,1)S(1)}, bf16[16,224,128]{2,1,0:T(8,128)(2,1)S(1)}, u32[]{:S(2)}, u32[]{:S(2)}) collective-permute-start(bf16[16,224,128]{2,1,0:T(8,128)(2,1)S(1)} %bitcast.95), channel_id=1, source_target_pairs={{0,96},{32,0},{64,32},{96,64},{1,97},{33,1},{65,33},{97,65},{2,98}... | collective-permute-start | bytes 2752520 | tf_op jit(solution)/shard_map/ppermute | solution.py:333
  54.2 13.3 %copy-start.10 = (bf16[16,224,128]{2,1,0:T(8,128)(2,1)}, bf16[16,224,128]{2,1,0:T(8,128)(2,1)S(1)}, u32[]{:S(2)}) copy-start(bf16[16,224,128]{2,1,0:T(8,128)(2,1)S(1)} %collective-permute-done.6.refs_6_) | copy-start | bytes 2752516
  54.3 13.2 %collective-permute-start.7 = (bf16[8,224,128]{2,1,0:T(8,128)(2,1)S(1)}, bf16[8,224,128]{2,1,0:T(8,128)(2,1)S(1)}, u32[]{:S(2)}, u32[]{:S(2)}) collective-permute-start(bf16[8,224,128]{2,1,0:T(8,128)(2,1)S(1)} %slice.134), channel_id=1, source_target_pairs={{0,32},{32,64},{64,96},{96,0},{1,33},{33,65},{65,97},{97,1},{2,34}... | collective-permute-start | bytes 1376264 | tf_op jit(solution)/shard_map/ppermute | solution.py:333
  54.7 26.5 %copy-start.11 = (bf16[16,224,128]{2,1,0:T(8,128)(2,1)}, bf16[16,224,128]{2,1,0:T(8,128)(2,1)S(1)}, u32[]{:S(2)}) copy-start(bf16[16,224,128]{2,1,0:T(8,128)(2,1)S(1)} %collective-permute-done.8.refs_8_) | copy-start | bytes 2752516
  54.7 12.8 %collective-permute-start.9 = (bf16[8,224,128]{2,1,0:T(8,128)(2,1)S(1)}, bf16[8,224,128]{2,1,0:T(8,128)(2,1)S(1)}, u32[]{:S(2)}, u32[]{:S(2)}) collective-permute-start(bf16[8,224,128]{2,1,0:T(8,128)(2,1)S(1)} %slice.135), channel_id=1, source_target_pairs={{0,96},{32,0},{64,32},{96,64},{1,97},{33,1},{65,33},{97,65},{2,98}... | collective-permute-start | bytes 1376264 | tf_op jit(solution)/shard_map/ppermute | solution.py:333
  57.7 10.0 %collective-permute-start.10 = (bf16[16,224,128]{2,1,0:T(8,128)(2,1)S(1)}, bf16[16,224,128]{2,1,0:T(8,128)(2,1)S(1)}, u32[]{:S(2)}, u32[]{:S(2)}) collective-permute-start(bf16[16,224,128]{2,1,0:T(8,128)(2,1)S(1)} %bitcast.96), channel_id=1, source_target_pairs={{0,1},{1,0},{2,3},{3,2},{4,5},{5,4},{6,7},{7,6},{8,9},{9,8},{10,11... | collective-permute-start | bytes 2752520 | tf_op jit(solution)/shard_map/ppermute | solution.py:333
  57.7 10.0 %collective-permute-start.13 = (bf16[16,224,128]{2,1,0:T(8,128)(2,1)S(1)}, bf16[16,224,128]{2,1,0:T(8,128)(2,1)S(1)}, u32[]{:S(2)}, u32[]{:S(2)}) collective-permute-start(bf16[16,224,128]{2,1,0:T(8,128)(2,1)S(1)} %collective-permute-done.8.refs_8_), channel_id=1, source_target_pairs={{0,1},{1,0},{2,3},{3,2},{4,5},{5,4},{6,7},{7,6},{8,9},{9,8},{10,11... | collective-permute-start | bytes 2752520 | tf_op jit(solution)/shard_map/ppermute | solution.py:333
  58.2 9.5 %collective-permute-start.11 = (bf16[16,224,128]{2,1,0:T(8,128)(2,1)S(1)}, bf16[16,224,128]{2,1,0:T(8,128)(2,1)S(1)}, u32[]{:S(2)}, u32[]{:S(2)}) collective-permute-start(bf16[16,224,128]{2,1,0:T(8,128)(2,1)S(1)} %collective-permute-done.6.refs_6_), channel_id=1, source_target_pairs={{0,1},{1,0},{2,3},{3,2},{4,5},{5,4},{6,7},{7,6},{8,9},{9,8},{10,11... | collective-permute-start | bytes 2752520 | tf_op jit(solution)/shard_map/ppermute | solution.py:333
  67.6 2.7 %collective-permute-start.12 = (bf16[16,224,128]{2,1,0:T(8,128)(2,1)S(1)}, bf16[16,224,128]{2,1,0:T(8,128)(2,1)}, u32[]{:S(2)}, u32[]{:S(2)}) collective-permute-start(bf16[16,224,128]{2,1,0:T(8,128)(2,1)S(1)} %constant_dynamic-update-slice_fusion.refs_7_), channel_id=1, source_target_pairs={{0,1},{1,0},{2,3},{3,2},{4,5},{5,4},{6,7},{7,6},{8,9},{9,8},{10,11... | collective-permute-start | bytes 2752520 | tf_op jit(solution)/shard_map/ppermute | solution.py:333
  81.1 37.2 %all-to-all-start.2 = ((bf16[32,48,768]{2,1,0:T(8,128)(2,1)}), bf16[32,48,768]{2,1,0:T(8,128)(2,1)S(1)}, u32[]{:S(2)}, u32[]{:S(2)}) async-start(bf16[32,48,768]{2,1,0:T(8,128)(2,1)} %get-tuple-element.86), calls=%async_computation.2 | async-start | bytes 4718592 | tf_op jit(solution)/shard_map/all_to_all | solution.py:328
  118.3 1.5 copy-start.8
  119.8 57.5 %all-to-all-start.1 = ((bf16[32,80,768]{2,1,0:T(8,128)(2,1)}), bf16[32,80,768]{2,1,0:T(8,128)(2,1)}, u32[]{:S(2)}, u32[]{:S(2)}) async-start(bf16[32,80,768]{2,1,0:T(8,128)(2,1)} %get-tuple-element.82), calls=%async_computation.1 | async-start | bytes 7864320 | tf_op jit(solution)/shard_map/all_to_all | solution.py:328
  152.3 2.8 %collective-permute-start.16 = (bf16[16,224,128]{2,1,0:T(8,128)(2,1)}, bf16[16,224,128]{2,1,0:T(8,128)(2,1)S(1)}, u32[]{:S(2)}, u32[]{:S(2)}) collective-permute-start(bf16[16,224,128]{2,1,0:T(8,128)(2,1)} %get-tuple-element.101), channel_id=1, source_target_pairs={{0,1},{1,0},{2,3},{3,2},{4,5},{5,4},{6,7},{7,6},{8,9},{9,8},{10,11... | collective-permute-start | bytes 2752520 | tf_op jit(solution)/shard_map/ppermute | solution.py:333
  152.5 7.5 %collective-permute-start.15 = (bf16[16,224,128]{2,1,0:T(8,128)(2,1)}, bf16[16,224,128]{2,1,0:T(8,128)(2,1)S(1)}, u32[]{:S(2)}, u32[]{:S(2)}) collective-permute-start(bf16[16,224,128]{2,1,0:T(8,128)(2,1)} %get-tuple-element.99), channel_id=1, source_target_pairs={{0,1},{1,0},{2,3},{3,2},{4,5},{5,4},{6,7},{7,6},{8,9},{9,8},{10,11... | collective-permute-start | bytes 2752520 | tf_op jit(solution)/shard_map/ppermute | solution.py:333
  152.9 7.3 %collective-permute-start.18 = (bf16[16,224,128]{2,1,0:T(8,128)(2,1)}, bf16[16,224,128]{2,1,0:T(8,128)(2,1)S(1)}, u32[]{:S(2)}, u32[]{:S(2)}) collective-permute-start(bf16[16,224,128]{2,1,0:T(8,128)(2,1)} %get-tuple-element.103), channel_id=1, source_target_pairs={{0,1},{1,0},{2,3},{3,2},{4,5},{5,4},{6,7},{7,6},{8,9},{9,8},{10,11... | collective-permute-start | bytes 2752520 | tf_op jit(solution)/shard_map/ppermute | solution.py:333
  155.1 4.9 %copy-start.14 = (bf16[16,224,128]{2,1,0:T(8,128)(2,1)S(1)}, bf16[16,224,128]{2,1,0:T(8,128)(2,1)}, u32[]{:S(2)}) copy-start(bf16[16,224,128]{2,1,0:T(8,128)(2,1)} %get-tuple-element.98) | copy-start | bytes 2752516
  156.7 15.1 %collective-permute-start.19 = (bf16[8,224,128]{2,1,0:T(8,128)(2,1)S(1)}, bf16[8,224,128]{2,1,0:T(8,128)(2,1)S(1)}, u32[]{:S(2)}, u32[]{:S(2)}) collective-permute-start(bf16[8,224,128]{2,1,0:T(8,128)(2,1)S(1)} %get-tuple-element.134), channel_id=1, source_target_pairs={{0,32},{32,64},{64,96},{96,0},{1,33},{33,65},{65,97},{97,1},{2,34}... | collective-permute-start | bytes 1376264 | tf_op jit(solution)/shard_map/ppermute | solution.py:333
  158.3 12.3 %collective-permute-start.17 = (bf16[8,224,128]{2,1,0:T(8,128)(2,1)S(1)}, bf16[8,224,128]{2,1,0:T(8,128)(2,1)S(1)}, u32[]{:S(2)}, u32[]{:S(2)}) collective-permute-start(bf16[8,224,128]{2,1,0:T(8,128)(2,1)S(1)} %get-tuple-element.135), channel_id=1, source_target_pairs={{0,96},{32,0},{64,32},{96,64},{1,97},{33,1},{65,33},{97,65},{2,98}... | collective-permute-start | bytes 1376264 | tf_op jit(solution)/shard_map/ppermute | solution.py:333
  177.2 38.4 %all-to-all-start.3 = ((bf16[32,48,768]{2,1,0:T(8,128)(2,1)}), bf16[32,48,768]{2,1,0:T(8,128)(2,1)S(1)}, u32[]{:S(2)}, u32[]{:S(2)}) async-start(bf16[32,48,768]{2,1,0:T(8,128)(2,1)} %get-tuple-element.107), calls=%async_computation.3 | async-start | bytes 4718592 | tf_op jit(solution)/shard_map/all_to_all | solution.py:328
  181.3 12.0 %collective-permute-start.14 = (bf16[16,224,128]{2,1,0:T(8,128)(2,1)}, bf16[16,224,128]{2,1,0:T(8,128)(2,1)S(1)}, u32[]{:S(2)}, u32[]{:S(2)}) collective-permute-start(bf16[16,224,128]{2,1,0:T(8,128)(2,1)} %get-tuple-element.96), channel_id=1, source_target_pairs={{0,1},{1,0},{2,3},{3,2},{4,5},{5,4},{6,7},{7,6},{8,9},{9,8},{10,11... | collective-permute-start | bytes 2752520 | tf_op jit(solution)/shard_map/ppermute | solution.py:333
  181.5 23.5 %collective-permute-start.20 = (bf16[16,224,128]{2,1,0:T(8,128)(2,1)}, bf16[16,224,128]{2,1,0:T(8,128)(2,1)S(1)}, u32[]{:S(2)}, u32[]{:S(2)}) collective-permute-start(bf16[16,224,128]{2,1,0:T(8,128)(2,1)} %pad_maximum_fusion), channel_id=1, source_target_pairs={{0,96},{32,0},{64,32},{96,64},{1,97},{33,1},{65,33},{97,65},{2,98}... | collective-permute-start | bytes 2752520 | tf_op jit(solution)/shard_map/ppermute | solution.py:333
  184.6 23.7 %collective-permute-start.21 = (bf16[16,224,128]{2,1,0:T(8,128)(2,1)}, bf16[16,224,128]{2,1,0:T(8,128)(2,1)S(1)}, u32[]{:S(2)}, u32[]{:S(2)}) collective-permute-start(bf16[16,224,128]{2,1,0:T(8,128)(2,1)} %pad_maximum_fusion.1), channel_id=1, source_target_pairs={{0,32},{32,64},{64,96},{96,0},{1,33},{33,65},{65,97},{97,1},{2,34}... | collective-permute-start | bytes 2752520 | tf_op jit(solution)/shard_map/ppermute | solution.py:333
  184.6 1.6 copy-start.3
  186.2 22.2 %copy-start.15 = (bf16[16,224,128]{2,1,0:T(8,128)(2,1)S(1)}, bf16[16,224,128]{2,1,0:T(8,128)(2,1)}, u32[]{:S(2)}) copy-start(bf16[16,224,128]{2,1,0:T(8,128)(2,1)} %get-tuple-element.95) | copy-start | bytes 2752516
  209.7 11.3 %collective-permute-start.24 = (bf16[4,224,128]{2,1,0:T(8,128)(2,1)}, bf16[4,224,128]{2,1,0:T(8,128)(2,1)}, u32[]{:S(2)}, u32[]{:S(2)}) collective-permute-start(bf16[4,224,128]{2,1,0:T(8,128)(2,1)} %get-tuple-element.130), channel_id=1, source_target_pairs={{0,8},{1,3},{2,10},{3,5},{4,12},{5,7},{6,14},{7,1},{8,16},{9,11},{... | collective-permute-start | bytes 688136 | tf_op jit(solution)/shard_map/ppermute | solution.py:357
  211.5 9.6 %collective-permute-start.23 = (bf16[4,224,128]{2,1,0:T(8,128)(2,1)}, bf16[4,224,128]{2,1,0:T(8,128)(2,1)}, u32[]{:S(2)}, u32[]{:S(2)}) collective-permute-start(bf16[4,224,128]{2,1,0:T(8,128)(2,1)} %get-tuple-element.131), channel_id=1, source_target_pairs={{0,16},{1,5},{2,18},{3,7},{4,20},{5,1},{6,22},{7,3},{8,24},{9,13},... | collective-permute-start | bytes 688136 | tf_op jit(solution)/shard_map/ppermute | solution.py:357
  214.3 6.8 %collective-permute-start.22 = (bf16[4,224,128]{2,1,0:T(8,128)(2,1)}, bf16[4,224,128]{2,1,0:T(8,128)(2,1)}, u32[]{:S(2)}, u32[]{:S(2)}) collective-permute-start(bf16[4,224,128]{2,1,0:T(8,128)(2,1)} %get-tuple-element.132), channel_id=1, source_target_pairs={{0,24},{1,7},{2,26},{3,1},{4,28},{5,3},{6,30},{7,5},{8,0},{9,15},{... | collective-permute-start | bytes 688136 | tf_op jit(solution)/shard_map/ppermute | solution.py:357
  215.7 1.6 copy-start.4
  222.4 7.6 %collective-permute-start.27 = (bf16[224,128]{1,0:T(8,128)(2,1)S(1)}, bf16[224,128]{1,0:T(8,128)(2,1)S(1)}, u32[]{:S(2)}, u32[]{:S(2)}) collective-permute-start(bf16[224,128]{1,0:T(8,128)(2,1)S(1)} %get-tuple-element.140), channel_id=1, source_target_pairs={{0,2},{1,9},{2,4},{3,11},{4,6},{5,13},{6,0},{7,15},{8,10},{9,17},{... | collective-permute-start | bytes 172040 | tf_op jit(solution)/shard_map/ppermute | solution.py:357
  224.0 10.9 %collective-permute-start.30 = (bf16[256,128]{1,0:T(8,128)(2,1)S(1)}, bf16[256,128]{1,0:T(8,128)(2,1)S(1)}, u32[]{:S(2)}, u32[]{:S(2)}) collective-permute-start(bf16[256,128]{1,0:T(8,128)(2,1)S(1)} %get-tuple-element.136), channel_id=1, source_target_pairs={{0,32},{32,64},{64,96},{96,0},{1,33},{33,65},{65,97},{97,1},{2,34}... | collective-permute-start | bytes 196616 | tf_op jit(solution)/shard_map/ppermute | solution.py:333
  224.1 10.8 %collective-permute-start.29 = (bf16[256,128]{1,0:T(8,128)(2,1)S(1)}, bf16[256,128]{1,0:T(8,128)(2,1)S(1)}, u32[]{:S(2)}, u32[]{:S(2)}) collective-permute-start(bf16[256,128]{1,0:T(8,128)(2,1)S(1)} %get-tuple-element.137), channel_id=1, source_target_pairs={{0,64},{32,96},{64,0},{96,32},{1,65},{33,97},{65,1},{97,33},{2,66}... | collective-permute-start | bytes 196616 | tf_op jit(solution)/shard_map/ppermute | solution.py:333
  225.8 9.1 %collective-permute-start.28 = (bf16[256,128]{1,0:T(8,128)(2,1)S(1)}, bf16[256,128]{1,0:T(8,128)(2,1)S(1)}, u32[]{:S(2)}, u32[]{:S(2)}) collective-permute-start(bf16[256,128]{1,0:T(8,128)(2,1)S(1)} %get-tuple-element.138), channel_id=1, source_target_pairs={{0,96},{32,0},{64,32},{96,64},{1,97},{33,1},{65,33},{97,65},{2,98}... | collective-permute-start | bytes 196616 | tf_op jit(solution)/shard_map/ppermute | solution.py:333
  227.3 7.6 %collective-permute-start.26 = (bf16[224,128]{1,0:T(8,128)(2,1)S(1)}, bf16[224,128]{1,0:T(8,128)(2,1)S(1)}, u32[]{:S(2)}, u32[]{:S(2)}) collective-permute-start(bf16[224,128]{1,0:T(8,128)(2,1)S(1)} %get-tuple-element.141), channel_id=1, source_target_pairs={{0,4},{1,17},{2,6},{3,19},{4,0},{5,21},{6,2},{7,23},{8,12},{9,25},... | collective-permute-start | bytes 172040 | tf_op jit(solution)/shard_map/ppermute | solution.py:357
  230.0 4.9 %collective-permute-start.25 = (bf16[224,128]{1,0:T(8,128)(2,1)S(1)}, bf16[224,128]{1,0:T(8,128)(2,1)S(1)}, u32[]{:S(2)}, u32[]{:S(2)}) collective-permute-start(bf16[224,128]{1,0:T(8,128)(2,1)S(1)} %get-tuple-element.142), channel_id=1, source_target_pairs={{0,6},{1,25},{2,0},{3,27},{4,2},{5,29},{6,4},{7,31},{8,14},{9,1},{... | collective-permute-start | bytes 172040 | tf_op jit(solution)/shard_map/ppermute | solution.py:357
  231.5 6.1 %copy-start.1 = (f32[512]{0:T(512)S(1)}, f32[512]{0:T(512)}, u32[]{:S(2)}) copy-start(f32[512]{0:T(512)} %param.20) | copy-start | bytes 6148
  (6 other events, 6.9 us)

commit v4 on v3

--- a/solution.py
+++ b/solution.py
@@ -12,7 +12,7 @@
 MIB = 1024 * 1024
 ROWS = 224
 GROUP = 8
-UNROLL = 8
+UNROLL = 4
 PARTS = (5, 3)
 
 
@@ -220,7 +220,7 @@
             ]
             + [weight_out] * 8,
             scratch_shapes=[
-                pltpu.VMEM((width * (nb + 1), 128), F32),
+                pltpu.VMEM((width * (nb + 1) + 128, 128), F32),
                 pltpu.VMEM((UNROLL, 128, width), BF16),
                 pltpu.VMEM((UNROLL, 128, width), F32),
             ],

time: 239 us -> 238 us (level)
  no operation moved by 1% of the time
where the time goes in v4:
time: 238 us; the launch traced here: 237 us
  waiting for transfers between devices  75.3 us (32%)
  Pallas kernels  75 us (32%)
  starting transfers between devices  60.8 us (26%)
  local copies, waits for them, and re-layouts  13.1 us (6%)
  other arithmetic  11.9 us (5%)
    ppermute x19, waiting for transfers between devices, shift(): return lax.ppermute(x, axis, [(i, (i + k) % n) for i in range(n)])  56 us
    pallas_call x2, Pallas kernels, middle(): pl.pallas_call(lambda *refs: middle_body(steps, len(before) > 0, *refs),...  55.4 us
    ppermute x12, starting transfers between devices, cross_shift(): return lax.ppermute(x, PLANE, moves)  23.3 us
    all_to_all x4, starting transfers between devices, exchange(): return lax.all_to_all(x, PLANE, split_axis=0, concat_axis=0, tiled=True)  19.7 us
    ppermute x19, starting transfers between devices, shift(): return lax.ppermute(x, axis, [(i, (i + k) % n) for i in range(n)])  17.8 us
    all_to_all x4, waiting for transfers between devices, exchange(): return lax.all_to_all(x, PLANE, split_axis=0, concat_axis=0, tiled=True)  16.6 us
    pallas_call x2, Pallas kernels, owner_backward(): pl.pallas_call(lambda *refs: owner_backward_body(later, *refs), grid=(par...  11 us
    unnamed x41, local copies, waits for them, and re-layouts  10.4 us
  transfers between devices with their start and end apart: 35, of which 12 were waited for; matrix products, arithmetic and copies ran while one was open for 4% of the time, Pallas kernels for 32%

profile of v4, /device:TPU:0, one launch (start us, length us, event | category | flops | bytes accessed | tf_op | source)
XLA Modules:
  0.0 237.2 jit_solution(74465421734562696)
XLA Ops:
  1.6 2.8 %collective-permute-start.2 = (bf16[1,224,128]{2,1,0:T(8,128)(2,1)S(1)}, bf16[1,224,128]{2,1,0:T(8,128)(2,1)S(1)}, u32[]{:S(2)}, u32[]{:S(2)}) collective-permute-start(bf16[1,224,128]{2,1,0:T(8,128)(2,1)S(1)} %fusion.4), channel_id=1, source_target_pairs={{0,6},{1,25},{2,0},{3,27},{4,2},{5,29},{6,4},{7,31},{8,14},{9,1},{... | collective-permute-start | bytes 172040 | tf_op jit(solution)/shard_map/ppermute | solution.py:357
  6.2 1.1 copy.30
  8.1 2.1 collective-permute-done.1
  11.8 4.0 %collective-permute-start.4 = (bf16[4,224,128]{2,1,0:T(8,128)(2,1)S(1)}, bf16[4,224,128]{2,1,0:T(8,128)(2,1)S(1)}, u32[]{:S(2)}, u32[]{:S(2)}) collective-permute-start(bf16[4,224,128]{2,1,0:T(8,128)(2,1)S(1)} %get-tuple-element.146), channel_id=1, source_target_pairs={{0,16},{1,5},{2,18},{3,7},{4,20},{5,1},{6,22},{7,3},{8,24},{9,13},... | collective-permute-start | bytes 688136 | tf_op jit(solution)/shard_map/ppermute | solution.py:357
  15.7 1.0 collective-permute-start.3
  16.7 2.2 collective-permute-start.5
  19.0 1.2 copy-done.5
  20.3 5.2 %owner_forward.1 = (bf16[32,80,768]{2,1,0:T(8,128)(2,1)}, bf16[32,48,768]{2,1,0:T(8,128)(2,1)}) custom-call(bf16[32,4096]{1,0:T(8,128)(2,1)S(1)} %bitcast.93, bf16[64,4096]{1,0:T(8,128)(2,1)S(1)} %bitcast.92, bf16[4096,128]{1,0:T(8,128)(2,1)S(1)} %bitcast.91, bf16[4096,256]{1,0:T(8,128)(2,1)S(1)} %bitcast.88, ...), custom_call_target="tpu_custom_call" | custom-call | flops 1073741824 | bytes 10223616 | tf_op jit(solution)/shard_map/owner_forward/pallas_call | solution.py:46
  25.7 4.8 %all-to-all-start = ((bf16[32,80,768]{2,1,0:T(8,128)(2,1)}), bf16[32,80,768]{2,1,0:T(8,128)(2,1)}, u32[]{:S(2)}, u32[]{:S(2)}) async-start(bf16[32,80,768]{2,1,0:T(8,128)(2,1)} %get-tuple-element.71), calls=%async_computation | async-start | bytes 7864320 | tf_op jit(solution)/shard_map/all_to_all | solution.py:328
  30.5 1.7 collective-permute-start.6
  32.2 1.6 collective-permute-start.8
  33.8 20.4 %collective-permute-done.6.refs_6_ = bf16[16,224,128]{2,1,0:T(8,128)(2,1)S(1)} collective-permute-done((bf16[16,224,128]{2,1,0:T(8,128)(2,1)S(1)}, bf16[16,224,128]{2,1,0:T(8,128)(2,1)S(1)}, u32[]{:S(2)}, u32[]{:S(2)}) %collective-permute-start.6) | collective-permute-done | bytes 917536 | tf_op jit(solution)/shard_map/ppermute | solution.py:333
  54.7 3.0 %collective-permute-start.9 = (bf16[8,224,128]{2,1,0:T(8,128)(2,1)S(1)}, bf16[8,224,128]{2,1,0:T(8,128)(2,1)S(1)}, u32[]{:S(2)}, u32[]{:S(2)}) collective-permute-start(bf16[8,224,128]{2,1,0:T(8,128)(2,1)S(1)} %slice.135), channel_id=1, source_target_pairs={{0,96},{32,0},{64,32},{96,64},{1,97},{33,1},{65,33},{97,65},{2,98}... | collective-permute-start | bytes 1376264 | tf_op jit(solution)/shard_map/ppermute | solution.py:333
  58.2 9.2 %collective-permute-done.7 = bf16[8,224,128]{2,1,0:T(8,128)(2,1)S(1)} collective-permute-done((bf16[8,224,128]{2,1,0:T(8,128)(2,1)S(1)}, bf16[8,224,128]{2,1,0:T(8,128)(2,1)S(1)}, u32[]{:S(2)}, u32[]{:S(2)}) %collective-permute-start.7) | collective-permute-done | bytes 458784 | tf_op jit(solution)/shard_map/ppermute | solution.py:333
  69.1 0.9 copy-done.18
  70.2 10.9 %all-to-all-done.refs_3_.refs_4_ = bf16[32,80,768]{2,1,0:T(8,128)(2,1)} async-done(((bf16[32,80,768]{2,1,0:T(8,128)(2,1)}), bf16[32,80,768]{2,1,0:T(8,128)(2,1)}, u32[]{:S(2)}, u32[]{:S(2)}) %all-to-all-start) | async-done | bytes 3932192 | tf_op jit(solution)/shard_map/all_to_all | solution.py:328
  81.1 4.1 %all-to-all-start.2 = ((bf16[32,48,768]{2,1,0:T(8,128)(2,1)}), bf16[32,48,768]{2,1,0:T(8,128)(2,1)S(1)}, u32[]{:S(2)}, u32[]{:S(2)}) async-start(bf16[32,48,768]{2,1,0:T(8,128)(2,1)} %get-tuple-element.86), calls=%async_computation.2 | async-start | bytes 4718592 | tf_op jit(solution)/shard_map/all_to_all | solution.py:328
  87.0 30.1 %middle.2 = (bf16[32,80,768]{2,1,0:T(8,128)(2,1)}, bf16[16,224,128]{2,1,0:T(8,128)(2,1)}, bf16[16,224,128]{2,1,0:T(8,128)(2,1)}, bf16[16,224,128]{2,1,0:T(8,128)...) custom-call(s32[3]{0:T(128)} %pad_add_fusion.refs_0_, ...), custom_call_target="tpu_custom_call" | custom-call | flops 8000000000 | bytes 35000000 | tf_op jit(solution)/shard_map/middle/pallas_call | solution.py:198
  117.2 1.1 all-to-all-done.2.refs_3_.refs_4_
  118.3 1.5 copy-done.8
  119.8 6.7 %all-to-all-start.1 = ((bf16[32,80,768]{2,1,0:T(8,128)(2,1)}), bf16[32,80,768]{2,1,0:T(8,128)(2,1)}, u32[]{:S(2)}, u32[]{:S(2)}) async-start(bf16[32,80,768]{2,1,0:T(8,128)(2,1)} %get-tuple-element.82), calls=%async_computation.1 | async-start | bytes 7864320 | tf_op jit(solution)/shard_map/all_to_all | solution.py:328
  126.5 25.3 %middle.3 = (bf16[32,48,768]{2,1,0:T(8,128)(2,1)}, bf16[16,224,128]{2,1,0:T(8,128)(2,1)}, bf16[16,224,128]{2,1,0:T(8,128)(2,1)}, bf16[16,224,128]{2,1,0:T(8,128)...) custom-call(s32[3]{0:T(128)} %pad_add_fusion.refs_0_, ...), custom_call_target="tpu_custom_call" | custom-call | flops 4800000000 | bytes 35000000 | tf_op jit(solution)/shard_map/middle/pallas_call | solution.py:198
  152.5 2.1 collective-permute-done.16
  154.6 1.5 add_convert_fusion.1
  156.1 1.7 collective-permute-start.19
  157.8 1.6 collective-permute-start.17
  161.0 9.1 %collective-permute-done.17 = bf16[8,224,128]{2,1,0:T(8,128)(2,1)S(1)} collective-permute-done((bf16[8,224,128]{2,1,0:T(8,128)(2,1)S(1)}, bf16[8,224,128]{2,1,0:T(8,128)(2,1)S(1)}, u32[]{:S(2)}, u32[]{:S(2)}) %collective-permute-start.17) | collective-permute-done | bytes 458784 | tf_op jit(solution)/shard_map/ppermute | solution.py:333
  170.2 1.0 pad_maximum_fusion
  171.3 1.0 pad_maximum_fusion.1
  172.3 4.6 %all-to-all-done.1.refs_0_.refs_1_ = bf16[32,80,768]{2,1,0:T(8,128)(2,1)} async-done(((bf16[32,80,768]{2,1,0:T(8,128)(2,1)}), bf16[32,80,768]{2,1,0:T(8,128)(2,1)}, u32[]{:S(2)}, u32[]{:S(2)}) %all-to-all-start.1) | async-done | bytes 3932192 | tf_op jit(solution)/shard_map/all_to_all | solution.py:328
  176.9 4.1 %all-to-all-start.3 = ((bf16[32,48,768]{2,1,0:T(8,128)(2,1)}), bf16[32,48,768]{2,1,0:T(8,128)(2,1)S(1)}, u32[]{:S(2)}, u32[]{:S(2)}) async-start(bf16[32,48,768]{2,1,0:T(8,128)(2,1)} %get-tuple-element.107), calls=%async_computation.3 | async-start | bytes 4718592 | tf_op jit(solution)/shard_map/all_to_all | solution.py:328
  181.2 3.0 %collective-permute-start.20 = (bf16[16,224,128]{2,1,0:T(8,128)(2,1)}, bf16[16,224,128]{2,1,0:T(8,128)(2,1)S(1)}, u32[]{:S(2)}, u32[]{:S(2)}) collective-permute-start(bf16[16,224,128]{2,1,0:T(8,128)(2,1)} %pad_maximum_fusion), channel_id=1, source_target_pairs={{0,96},{32,0},{64,32},{96,64},{1,97},{33,1},{65,33},{97,65},{2,98}... | collective-permute-start | bytes 2752520 | tf_op jit(solution)/shard_map/ppermute | solution.py:333
  184.2 1.6 copy-done.3
  185.8 7.2 %owner_backward.2 = (bf16[32,128,256]{2,1,0:T(8,128)(2,1)}, bf16[32,128,128]{2,1,0:T(8,128)(2,1)}, f32[256,512]{1,0:T(8,128)S(1)}) custom-call(bf16[32,80,768]{2,1,0:T(8,128)(2,1)} %all-to-all-done.1.refs_0_.refs_1_, bf16[32,80,768]{2,1,0:T(8,128)(2,1)} %all-to-all-done.1.refs_0_.refs_1_, bf16[32,128,256]{2,1,0:T(8,128)(2,1)S(1)} %bitcast.89, ...), custom_call_target="tpu_custom_call" | custom-call | flops 1342177280 | bytes 5242880 | tf_op jit(solution)/shard_map/owner_backward/pallas_call | solution.py:274
  193.0 11.7 %collective-permute-done.20 = bf16[16,224,128]{2,1,0:T(8,128)(2,1)S(1)} collective-permute-done((bf16[16,224,128]{2,1,0:T(8,128)(2,1)}, bf16[16,224,128]{2,1,0:T(8,128)(2,1)S(1)}, u32[]{:S(2)}, u32[]{:S(2)}) %collective-permute-start.20) | collective-permute-done | bytes 917536 | tf_op jit(solution)/shard_map/ppermute | solution.py:333
  204.7 3.3 %collective-permute-done.21 = bf16[16,224,128]{2,1,0:T(8,128)(2,1)S(1)} collective-permute-done((bf16[16,224,128]{2,1,0:T(8,128)(2,1)}, bf16[16,224,128]{2,1,0:T(8,128)(2,1)S(1)}, u32[]{:S(2)}, u32[]{:S(2)}) %collective-permute-start.21) | collective-permute-done | bytes 917536 | tf_op jit(solution)/shard_map/ppermute | solution.py:333
  209.4 1.7 collective-permute-start.24
  211.1 2.8 %collective-permute-start.23 = (bf16[4,224,128]{2,1,0:T(8,128)(2,1)}, bf16[4,224,128]{2,1,0:T(8,128)(2,1)}, u32[]{:S(2)}, u32[]{:S(2)}) collective-permute-start(bf16[4,224,128]{2,1,0:T(8,128)(2,1)} %get-tuple-element.131), channel_id=1, source_target_pairs={{0,16},{1,5},{2,18},{3,7},{4,20},{5,1},{6,22},{7,3},{8,24},{9,13},... | collective-permute-start | bytes 688136 | tf_op jit(solution)/shard_map/ppermute | solution.py:357
  213.9 1.4 collective-permute-start.22
  215.3 1.6 copy-done.4
  216.9 3.8 %owner_backward.3 = (bf16[32,128,256]{2,1,0:T(8,128)(2,1)}, bf16[32,128,128]{2,1,0:T(8,128)(2,1)}, bf16[256,512]{1,0:T(8,128)(2,1)S(1)}) custom-call(bf16[32,48,768]{2,1,0:T(8,128)(2,1)S(1)} %all-to-all-done.3.refs_0_.refs_1_, bf16[32,48,768]{2,1,0:T(8,128)(2,1)S(1)} %all-to-all-done.3.refs_0_.refs_1_, ...), custom_call_target="tpu_custom_call", output_to_operand_aliasing={{0}: (4, {}), {1}: (5, {})} | custom-call | flops 805306368 | bytes 3145728 | tf_op jit(solution)/shard_map/owner_backward/pallas_call | solution.py:274
  220.7 1.3 add_convert_fusion.2
  222.1 1.5 collective-permute-start.27
  223.7 1.7 collective-permute-start.29
  225.5 1.5 collective-permute-start.28
  227.0 2.7 %collective-permute-start.26 = (bf16[224,128]{1,0:T(8,128)(2,1)S(1)}, bf16[224,128]{1,0:T(8,128)(2,1)S(1)}, u32[]{:S(2)}, u32[]{:S(2)}) collective-permute-start(bf16[224,128]{1,0:T(8,128)(2,1)S(1)} %get-tuple-element.141), channel_id=1, source_target_pairs={{0,4},{1,17},{2,6},{3,19},{4,0},{5,21},{6,2},{7,23},{8,12},{9,25},... | collective-permute-start | bytes 172040 | tf_op jit(solution)/shard_map/ppermute | solution.py:357
  229.7 1.5 collective-permute-start.25
  231.1 3.4 %owner_split.1 = (bf16[32,4096]{1,0:T(8,128)(2,1)}, bf16[64,4096]{1,0:T(8,128)(2,1)}) custom-call(bf16[32,80,768]{2,1,0:T(8,128)(2,1)} %all-to-all-done.1.refs_0_.refs_1_, bf16[32,48,768]{2,1,0:T(8,128)(2,1)S(1)} %all-to-all-done.3.refs_0_.refs_1_), custom_call_target="tpu_custom_call" | custom-call | bytes 1835008 | tf_op jit(solution)/shard_map/owner_split/pallas_call | solution.py:307
  (105 shorter events, 16.7 us)
Async XLA Ops:
  0.6 84.6 %copy-start = (f32[512]{0:T(512)S(1)}, f32[512]{0:T(512)}, u32[]{:S(2)}) copy-start(f32[512]{0:T(512)} %param.20) | copy-start | bytes 6148
  0.7 18.3 %copy-start.2 = (bf16[4096,1,256]{2,0,1:T(8,128)(2,1)S(1)}, bf16[4096,1,256]{2,0,1:T(8,128)(2,1)}, u32[]{:S(2)}) copy-start(bf16[4096,1,256]{2,0,1:T(8,128)(2,1)} %param.14) | copy-start | bytes 6291460
  0.7 18.3 %copy-start.6 = (bf16[4096,1,64]{0,2,1:T(8,128)(2,1)S(1)}, bf16[4096,1,64]{0,2,1:T(8,128)(2,1)}, u32[]{:S(2)}) copy-start(bf16[4096,1,64]{0,2,1:T(8,128)(2,1)} %param.12) | copy-start | bytes 1572868
  0.7 18.3 %copy-start.7 = (bf16[4096,1,32]{0,2,1:T(8,128)(2,1)S(1)}, bf16[4096,1,32]{0,2,1:T(8,128)(2,1)}, u32[]{:S(2)}) copy-start(bf16[4096,1,32]{0,2,1:T(8,128)(2,1)} %param.11) | copy-start | bytes 786436
  1.6 6.5 %collective-permute-start.2 = (bf16[1,224,128]{2,1,0:T(8,128)(2,1)S(1)}, bf16[1,224,128]{2,1,0:T(8,128)(2,1)S(1)}, u32[]{:S(2)}, u32[]{:S(2)}) collective-permute-start(bf16[1,224,128]{2,1,0:T(8,128)(2,1)S(1)} %fusion.4), channel_id=1, source_target_pairs={{0,6},{1,25},{2,0},{3,27},{4,2},{5,29},{6,4},{7,31},{8,14},{9,1},{... | collective-permute-start | bytes 172040 | tf_op jit(solution)/shard_map/ppermute | solution.py:357
  4.5 5.8 %collective-permute-start.1 = (bf16[1,224,128]{2,1,0:T(8,128)(2,1)S(1)}, bf16[1,224,128]{2,1,0:T(8,128)(2,1)}, u32[]{:S(2)}, u32[]{:S(2)}) collective-permute-start(bf16[1,224,128]{2,1,0:T(8,128)(2,1)S(1)} %fusion.4), channel_id=1, source_target_pairs={{0,4},{1,17},{2,6},{3,19},{4,0},{5,21},{6,2},{7,23},{8,12},{9,25},... | collective-permute-start | bytes 172040 | tf_op jit(solution)/shard_map/ppermute | solution.py:357
  5.3 5.6 %collective-permute-start = (bf16[1,224,128]{2,1,0:T(8,128)(2,1)S(1)}, bf16[1,224,128]{2,1,0:T(8,128)(2,1)}, u32[]{:S(2)}, u32[]{:S(2)}) collective-permute-start(bf16[1,224,128]{2,1,0:T(8,128)(2,1)S(1)} %fusion.4), channel_id=1, source_target_pairs={{0,2},{1,9},{2,4},{3,11},{4,6},{5,13},{6,0},{7,15},{8,10},{9,17},{... | collective-permute-start | bytes 172040 | tf_op jit(solution)/shard_map/ppermute | solution.py:357
  11.8 13.7 %collective-permute-start.4 = (bf16[4,224,128]{2,1,0:T(8,128)(2,1)S(1)}, bf16[4,224,128]{2,1,0:T(8,128)(2,1)S(1)}, u32[]{:S(2)}, u32[]{:S(2)}) collective-permute-start(bf16[4,224,128]{2,1,0:T(8,128)(2,1)S(1)} %get-tuple-element.146), channel_id=1, source_target_pairs={{0,16},{1,5},{2,18},{3,7},{4,20},{5,1},{6,22},{7,3},{8,24},{9,13},... | collective-permute-start | bytes 688136 | tf_op jit(solution)/shard_map/ppermute | solution.py:357
  15.7 9.7 %collective-permute-start.3 = (bf16[4,224,128]{2,1,0:T(8,128)(2,1)S(1)}, bf16[4,224,128]{2,1,0:T(8,128)(2,1)S(1)}, u32[]{:S(2)}, u32[]{:S(2)}) collective-permute-start(bf16[4,224,128]{2,1,0:T(8,128)(2,1)S(1)} %get-tuple-element.146), channel_id=1, source_target_pairs={{0,8},{1,3},{2,10},{3,5},{4,12},{5,7},{6,14},{7,1},{8,16},{9,11},{... | collective-permute-start | bytes 688136 | tf_op jit(solution)/shard_map/ppermute | solution.py:357
  16.7 8.7 %collective-permute-start.5 = (bf16[4,224,128]{2,1,0:T(8,128)(2,1)S(1)}, bf16[4,224,128]{2,1,0:T(8,128)(2,1)S(1)}, u32[]{:S(2)}, u32[]{:S(2)}) collective-permute-start(bf16[4,224,128]{2,1,0:T(8,128)(2,1)S(1)} %get-tuple-element.146), channel_id=1, source_target_pairs={{0,24},{1,7},{2,26},{3,1},{4,28},{5,3},{6,30},{7,5},{8,0},{9,15},{... | collective-permute-start | bytes 688136 | tf_op jit(solution)/shard_map/ppermute | solution.py:357
  25.7 32.0 %copy-start.9 = (bf16[4,4,224,128]{3,2,1,0:T(8,128)(2,1)}, bf16[4,4,224,128]{3,2,1,0:T(8,128)(2,1)S(1)}, u32[]{:S(2)}) copy-start(bf16[4,4,224,128]{3,2,1,0:T(8,128)(2,1)S(1)} %maximum_select_fusion) | copy-start | bytes 2752516
  25.7 55.5 %all-to-all-start = ((bf16[32,80,768]{2,1,0:T(8,128)(2,1)}), bf16[32,80,768]{2,1,0:T(8,128)(2,1)}, u32[]{:S(2)}, u32[]{:S(2)}) async-start(bf16[32,80,768]{2,1,0:T(8,128)(2,1)} %get-tuple-element.71), calls=%async_computation | async-start | bytes 7864320 | tf_op jit(solution)/shard_map/all_to_all | solution.py:328
  30.5 23.7 %collective-permute-start.6 = (bf16[16,224,128]{2,1,0:T(8,128)(2,1)S(1)}, bf16[16,224,128]{2,1,0:T(8,128)(2,1)S(1)}, u32[]{:S(2)}, u32[]{:S(2)}) collective-permute-start(bf16[16,224,128]{2,1,0:T(8,128)(2,1)S(1)} %bitcast.94), channel_id=1, source_target_pairs={{0,32},{32,64},{64,96},{96,0},{1,33},{33,65},{65,97},{97,1},{2,34}... | collective-permute-start | bytes 2752520 | tf_op jit(solution)/shard_map/ppermute | solution.py:333
  32.2 22.5 %collective-permute-start.8 = (bf16[16,224,128]{2,1,0:T(8,128)(2,1)S(1)}, bf16[16,224,128]{2,1,0:T(8,128)(2,1)S(1)}, u32[]{:S(2)}, u32[]{:S(2)}) collective-permute-start(bf16[16,224,128]{2,1,0:T(8,128)(2,1)S(1)} %bitcast.95), channel_id=1, source_target_pairs={{0,96},{32,0},{64,32},{96,64},{1,97},{33,1},{65,33},{97,65},{2,98}... | collective-permute-start | bytes 2752520 | tf_op jit(solution)/shard_map/ppermute | solution.py:333
  54.2 13.3 %copy-start.10 = (bf16[16,224,128]{2,1,0:T(8,128)(2,1)}, bf16[16,224,128]{2,1,0:T(8,128)(2,1)S(1)}, u32[]{:S(2)}) copy-start(bf16[16,224,128]{2,1,0:T(8,128)(2,1)S(1)} %collective-permute-done.6.refs_6_) | copy-start | bytes 2752516
  54.3 13.2 %collective-permute-start.7 = (bf16[8,224,128]{2,1,0:T(8,128)(2,1)S(1)}, bf16[8,224,128]{2,1,0:T(8,128)(2,1)S(1)}, u32[]{:S(2)}, u32[]{:S(2)}) collective-permute-start(bf16[8,224,128]{2,1,0:T(8,128)(2,1)S(1)} %slice.134), channel_id=1, source_target_pairs={{0,32},{32,64},{64,96},{96,0},{1,33},{33,65},{65,97},{97,1},{2,34}... | collective-permute-start | bytes 1376264 | tf_op jit(solution)/shard_map/ppermute | solution.py:333
  54.7 26.5 %copy-start.11 = (bf16[16,224,128]{2,1,0:T(8,128)(2,1)}, bf16[16,224,128]{2,1,0:T(8,128)(2,1)S(1)}, u32[]{:S(2)}) copy-start(bf16[16,224,128]{2,1,0:T(8,128)(2,1)S(1)} %collective-permute-done.8.refs_8_) | copy-start | bytes 2752516
  54.7 12.8 %collective-permute-start.9 = (bf16[8,224,128]{2,1,0:T(8,128)(2,1)S(1)}, bf16[8,224,128]{2,1,0:T(8,128)(2,1)S(1)}, u32[]{:S(2)}, u32[]{:S(2)}) collective-permute-start(bf16[8,224,128]{2,1,0:T(8,128)(2,1)S(1)} %slice.135), channel_id=1, source_target_pairs={{0,96},{32,0},{64,32},{96,64},{1,97},{33,1},{65,33},{97,65},{2,98}... | collective-permute-start | bytes 1376264 | tf_op jit(solution)/shard_map/ppermute | solution.py:333
  57.7 10.0 %collective-permute-start.10 = (bf16[16,224,128]{2,1,0:T(8,128)(2,1)S(1)}, bf16[16,224,128]{2,1,0:T(8,128)(2,1)S(1)}, u32[]{:S(2)}, u32[]{:S(2)}) collective-permute-start(bf16[16,224,128]{2,1,0:T(8,128)(2,1)S(1)} %bitcast.96), channel_id=1, source_target_pairs={{0,1},{1,0},{2,3},{3,2},{4,5},{5,4},{6,7},{7,6},{8,9},{9,8},{10,11... | collective-permute-start | bytes 2752520 | tf_op jit(solution)/shard_map/ppermute | solution.py:333
  57.7 10.0 %collective-permute-start.13 = (bf16[16,224,128]{2,1,0:T(8,128)(2,1)S(1)}, bf16[16,224,128]{2,1,0:T(8,128)(2,1)S(1)}, u32[]{:S(2)}, u32[]{:S(2)}) collective-permute-start(bf16[16,224,128]{2,1,0:T(8,128)(2,1)S(1)} %collective-permute-done.8.refs_8_), channel_id=1, source_target_pairs={{0,1},{1,0},{2,3},{3,2},{4,5},{5,4},{6,7},{7,6},{8,9},{9,8},{10,11... | collective-permute-start | bytes 2752520 | tf_op jit(solution)/shard_map/ppermute | solution.py:333
  58.2 9.5 %collective-permute-start.11 = (bf16[16,224,128]{2,1,0:T(8,128)(2,1)S(1)}, bf16[16,224,128]{2,1,0:T(8,128)(2,1)S(1)}, u32[]{:S(2)}, u32[]{:S(2)}) collective-permute-start(bf16[16,224,128]{2,1,0:T(8,128)(2,1)S(1)} %collective-permute-done.6.refs_6_), channel_id=1, source_target_pairs={{0,1},{1,0},{2,3},{3,2},{4,5},{5,4},{6,7},{7,6},{8,9},{9,8},{10,11... | collective-permute-start | bytes 2752520 | tf_op jit(solution)/shard_map/ppermute | solution.py:333
  67.6 2.7 %collective-permute-start.12 = (bf16[16,224,128]{2,1,0:T(8,128)(2,1)S(1)}, bf16[16,224,128]{2,1,0:T(8,128)(2,1)}, u32[]{:S(2)}, u32[]{:S(2)}) collective-permute-start(bf16[16,224,128]{2,1,0:T(8,128)(2,1)S(1)} %constant_dynamic-update-slice_fusion.refs_7_), channel_id=1, source_target_pairs={{0,1},{1,0},{2,3},{3,2},{4,5},{5,4},{6,7},{7,6},{8,9},{9,8},{10,11... | collective-permute-start | bytes 2752520 | tf_op jit(solution)/shard_map/ppermute | solution.py:333
  81.1 37.2 %all-to-all-start.2 = ((bf16[32,48,768]{2,1,0:T(8,128)(2,1)}), bf16[32,48,768]{2,1,0:T(8,128)(2,1)S(1)}, u32[]{:S(2)}, u32[]{:S(2)}) async-start(bf16[32,48,768]{2,1,0:T(8,128)(2,1)} %get-tuple-element.86), calls=%async_computation.2 | async-start | bytes 4718592 | tf_op jit(solution)/shard_map/all_to_all | solution.py:328
  118.3 1.5 copy-start.8
  119.8 57.1 %all-to-all-start.1 = ((bf16[32,80,768]{2,1,0:T(8,128)(2,1)}), bf16[32,80,768]{2,1,0:T(8,128)(2,1)}, u32[]{:S(2)}, u32[]{:S(2)}) async-start(bf16[32,80,768]{2,1,0:T(8,128)(2,1)} %get-tuple-element.82), calls=%async_computation.1 | async-start | bytes 7864320 | tf_op jit(solution)/shard_map/all_to_all | solution.py:328
  151.8 2.8 %collective-permute-start.16 = (bf16[16,224,128]{2,1,0:T(8,128)(2,1)}, bf16[16,224,128]{2,1,0:T(8,128)(2,1)S(1)}, u32[]{:S(2)}, u32[]{:S(2)}) collective-permute-start(bf16[16,224,128]{2,1,0:T(8,128)(2,1)} %get-tuple-element.101), channel_id=1, source_target_pairs={{0,1},{1,0},{2,3},{3,2},{4,5},{5,4},{6,7},{7,6},{8,9},{9,8},{10,11... | collective-permute-start | bytes 2752520 | tf_op jit(solution)/shard_map/ppermute | solution.py:333
  151.9 7.5 %collective-permute-start.15 = (bf16[16,224,128]{2,1,0:T(8,128)(2,1)}, bf16[16,224,128]{2,1,0:T(8,128)(2,1)S(1)}, u32[]{:S(2)}, u32[]{:S(2)}) collective-permute-start(bf16[16,224,128]{2,1,0:T(8,128)(2,1)} %get-tuple-element.99), channel_id=1, source_target_pairs={{0,1},{1,0},{2,3},{3,2},{4,5},{5,4},{6,7},{7,6},{8,9},{9,8},{10,11... | collective-permute-start | bytes 2752520 | tf_op jit(solution)/shard_map/ppermute | solution.py:333
  152.4 7.3 %collective-permute-start.18 = (bf16[16,224,128]{2,1,0:T(8,128)(2,1)}, bf16[16,224,128]{2,1,0:T(8,128)(2,1)S(1)}, u32[]{:S(2)}, u32[]{:S(2)}) collective-permute-start(bf16[16,224,128]{2,1,0:T(8,128)(2,1)} %get-tuple-element.103), channel_id=1, source_target_pairs={{0,1},{1,0},{2,3},{3,2},{4,5},{5,4},{6,7},{7,6},{8,9},{9,8},{10,11... | collective-permute-start | bytes 2752520 | tf_op jit(solution)/shard_map/ppermute | solution.py:333
  154.6 4.9 %copy-start.14 = (bf16[16,224,128]{2,1,0:T(8,128)(2,1)S(1)}, bf16[16,224,128]{2,1,0:T(8,128)(2,1)}, u32[]{:S(2)}) copy-start(bf16[16,224,128]{2,1,0:T(8,128)(2,1)} %get-tuple-element.98) | copy-start | bytes 2752516
  156.1 15.1 %collective-permute-start.19 = (bf16[8,224,128]{2,1,0:T(8,128)(2,1)S(1)}, bf16[8,224,128]{2,1,0:T(8,128)(2,1)S(1)}, u32[]{:S(2)}, u32[]{:S(2)}) collective-permute-start(bf16[8,224,128]{2,1,0:T(8,128)(2,1)S(1)} %get-tuple-element.134), channel_id=1, source_target_pairs={{0,32},{32,64},{64,96},{96,0},{1,33},{33,65},{65,97},{97,1},{2,34}... | collective-permute-start | bytes 1376264 | tf_op jit(solution)/shard_map/ppermute | solution.py:333
  157.8 12.3 %collective-permute-start.17 = (bf16[8,224,128]{2,1,0:T(8,128)(2,1)S(1)}, bf16[8,224,128]{2,1,0:T(8,128)(2,1)S(1)}, u32[]{:S(2)}, u32[]{:S(2)}) collective-permute-start(bf16[8,224,128]{2,1,0:T(8,128)(2,1)S(1)} %get-tuple-element.135), channel_id=1, source_target_pairs={{0,96},{32,0},{64,32},{96,64},{1,97},{33,1},{65,33},{97,65},{2,98}... | collective-permute-start | bytes 1376264 | tf_op jit(solution)/shard_map/ppermute | solution.py:333
  176.9 38.4 %all-to-all-start.3 = ((bf16[32,48,768]{2,1,0:T(8,128)(2,1)}), bf16[32,48,768]{2,1,0:T(8,128)(2,1)S(1)}, u32[]{:S(2)}, u32[]{:S(2)}) async-start(bf16[32,48,768]{2,1,0:T(8,128)(2,1)} %get-tuple-element.107), calls=%async_computation.3 | async-start | bytes 4718592 | tf_op jit(solution)/shard_map/all_to_all | solution.py:328
  181.0 12.0 %collective-permute-start.14 = (bf16[16,224,128]{2,1,0:T(8,128)(2,1)}, bf16[16,224,128]{2,1,0:T(8,128)(2,1)S(1)}, u32[]{:S(2)}, u32[]{:S(2)}) collective-permute-start(bf16[16,224,128]{2,1,0:T(8,128)(2,1)} %get-tuple-element.96), channel_id=1, source_target_pairs={{0,1},{1,0},{2,3},{3,2},{4,5},{5,4},{6,7},{7,6},{8,9},{9,8},{10,11... | collective-permute-start | bytes 2752520 | tf_op jit(solution)/shard_map/ppermute | solution.py:333
  181.2 23.5 %collective-permute-start.20 = (bf16[16,224,128]{2,1,0:T(8,128)(2,1)}, bf16[16,224,128]{2,1,0:T(8,128)(2,1)S(1)}, u32[]{:S(2)}, u32[]{:S(2)}) collective-permute-start(bf16[16,224,128]{2,1,0:T(8,128)(2,1)} %pad_maximum_fusion), channel_id=1, source_target_pairs={{0,96},{32,0},{64,32},{96,64},{1,97},{33,1},{65,33},{97,65},{2,98}... | collective-permute-start | bytes 2752520 | tf_op jit(solution)/shard_map/ppermute | solution.py:333
  184.2 23.7 %collective-permute-start.21 = (bf16[16,224,128]{2,1,0:T(8,128)(2,1)}, bf16[16,224,128]{2,1,0:T(8,128)(2,1)S(1)}, u32[]{:S(2)}, u32[]{:S(2)}) collective-permute-start(bf16[16,224,128]{2,1,0:T(8,128)(2,1)} %pad_maximum_fusion.1), channel_id=1, source_target_pairs={{0,32},{32,64},{64,96},{96,0},{1,33},{33,65},{65,97},{97,1},{2,34}... | collective-permute-start | bytes 2752520 | tf_op jit(solution)/shard_map/ppermute | solution.py:333
  184.2 1.6 copy-start.3
  185.8 22.2 %copy-start.15 = (bf16[16,224,128]{2,1,0:T(8,128)(2,1)S(1)}, bf16[16,224,128]{2,1,0:T(8,128)(2,1)}, u32[]{:S(2)}) copy-start(bf16[16,224,128]{2,1,0:T(8,128)(2,1)} %get-tuple-element.95) | copy-start | bytes 2752516
  209.4 11.3 %collective-permute-start.24 = (bf16[4,224,128]{2,1,0:T(8,128)(2,1)}, bf16[4,224,128]{2,1,0:T(8,128)(2,1)}, u32[]{:S(2)}, u32[]{:S(2)}) collective-permute-start(bf16[4,224,128]{2,1,0:T(8,128)(2,1)} %get-tuple-element.130), channel_id=1, source_target_pairs={{0,8},{1,3},{2,10},{3,5},{4,12},{5,7},{6,14},{7,1},{8,16},{9,11},{... | collective-permute-start | bytes 688136 | tf_op jit(solution)/shard_map/ppermute | solution.py:357
  211.1 9.6 %collective-permute-start.23 = (bf16[4,224,128]{2,1,0:T(8,128)(2,1)}, bf16[4,224,128]{2,1,0:T(8,128)(2,1)}, u32[]{:S(2)}, u32[]{:S(2)}) collective-permute-start(bf16[4,224,128]{2,1,0:T(8,128)(2,1)} %get-tuple-element.131), channel_id=1, source_target_pairs={{0,16},{1,5},{2,18},{3,7},{4,20},{5,1},{6,22},{7,3},{8,24},{9,13},... | collective-permute-start | bytes 688136 | tf_op jit(solution)/shard_map/ppermute | solution.py:357
  213.9 6.8 %collective-permute-start.22 = (bf16[4,224,128]{2,1,0:T(8,128)(2,1)}, bf16[4,224,128]{2,1,0:T(8,128)(2,1)}, u32[]{:S(2)}, u32[]{:S(2)}) collective-permute-start(bf16[4,224,128]{2,1,0:T(8,128)(2,1)} %get-tuple-element.132), channel_id=1, source_target_pairs={{0,24},{1,7},{2,26},{3,1},{4,28},{5,3},{6,30},{7,5},{8,0},{9,15},{... | collective-permute-start | bytes 688136 | tf_op jit(solution)/shard_map/ppermute | solution.py:357
  215.3 1.6 copy-start.4
  222.1 7.6 %collective-permute-start.27 = (bf16[224,128]{1,0:T(8,128)(2,1)S(1)}, bf16[224,128]{1,0:T(8,128)(2,1)S(1)}, u32[]{:S(2)}, u32[]{:S(2)}) collective-permute-start(bf16[224,128]{1,0:T(8,128)(2,1)S(1)} %get-tuple-element.140), channel_id=1, source_target_pairs={{0,2},{1,9},{2,4},{3,11},{4,6},{5,13},{6,0},{7,15},{8,10},{9,17},{... | collective-permute-start | bytes 172040 | tf_op jit(solution)/shard_map/ppermute | solution.py:357
  223.7 10.9 %collective-permute-start.30 = (bf16[256,128]{1,0:T(8,128)(2,1)S(1)}, bf16[256,128]{1,0:T(8,128)(2,1)S(1)}, u32[]{:S(2)}, u32[]{:S(2)}) collective-permute-start(bf16[256,128]{1,0:T(8,128)(2,1)S(1)} %get-tuple-element.136), channel_id=1, source_target_pairs={{0,32},{32,64},{64,96},{96,0},{1,33},{33,65},{65,97},{97,1},{2,34}... | collective-permute-start | bytes 196616 | tf_op jit(solution)/shard_map/ppermute | solution.py:333
  223.7 10.8 %collective-permute-start.29 = (bf16[256,128]{1,0:T(8,128)(2,1)S(1)}, bf16[256,128]{1,0:T(8,128)(2,1)S(1)}, u32[]{:S(2)}, u32[]{:S(2)}) collective-permute-start(bf16[256,128]{1,0:T(8,128)(2,1)S(1)} %get-tuple-element.137), channel_id=1, source_target_pairs={{0,64},{32,96},{64,0},{96,32},{1,65},{33,97},{65,1},{97,33},{2,66}... | collective-permute-start | bytes 196616 | tf_op jit(solution)/shard_map/ppermute | solution.py:333
  225.5 9.1 %collective-permute-start.28 = (bf16[256,128]{1,0:T(8,128)(2,1)S(1)}, bf16[256,128]{1,0:T(8,128)(2,1)S(1)}, u32[]{:S(2)}, u32[]{:S(2)}) collective-permute-start(bf16[256,128]{1,0:T(8,128)(2,1)S(1)} %get-tuple-element.138), channel_id=1, source_target_pairs={{0,96},{32,0},{64,32},{96,64},{1,97},{33,1},{65,33},{97,65},{2,98}... | collective-permute-start | bytes 196616 | tf_op jit(solution)/shard_map/ppermute | solution.py:333
  227.0 7.6 %collective-permute-start.26 = (bf16[224,128]{1,0:T(8,128)(2,1)S(1)}, bf16[224,128]{1,0:T(8,128)(2,1)S(1)}, u32[]{:S(2)}, u32[]{:S(2)}) collective-permute-start(bf16[224,128]{1,0:T(8,128)(2,1)S(1)} %get-tuple-element.141), channel_id=1, source_target_pairs={{0,4},{1,17},{2,6},{3,19},{4,0},{5,21},{6,2},{7,23},{8,12},{9,25},... | collective-permute-start | bytes 172040 | tf_op jit(solution)/shard_map/ppermute | solution.py:357
  229.7 4.9 %collective-permute-start.25 = (bf16[224,128]{1,0:T(8,128)(2,1)S(1)}, bf16[224,128]{1,0:T(8,128)(2,1)S(1)}, u32[]{:S(2)}, u32[]{:S(2)}) collective-permute-start(bf16[224,128]{1,0:T(8,128)(2,1)S(1)} %get-tuple-element.142), channel_id=1, source_target_pairs={{0,6},{1,25},{2,0},{3,27},{4,2},{5,29},{6,4},{7,31},{8,14},{9,1},{... | collective-permute-start | bytes 172040 | tf_op jit(solution)/shard_map/ppermute | solution.py:357
  231.1 6.1 %copy-start.1 = (f32[512]{0:T(512)S(1)}, f32[512]{0:T(512)}, u32[]{:S(2)}) copy-start(f32[512]{0:T(512)} %param.20) | copy-start | bytes 6148
  (6 other events, 6.9 us)

commit v5 on v4

--- a/solution.py
+++ b/solution.py
@@ -227,7 +227,7 @@
         ),
         out_shape=[pltpu.HBM((ntab, nb, full), BF16)]
         + [jax.ShapeDtypeStruct((16, ROWS, 128), BF16)] * 8,
-        compiler_params=pltpu.CompilerParams(vmem_limit_bytes=58 * MIB),
+        compiler_params=pltpu.CompilerParams(vmem_limit_bytes=62 * MIB),
         cost_estimate=pl.CostEstimate(
             flops=nb * 10**8, bytes_accessed=35 * 10**6, transcendentals=0
         ),
@@ -259,6 +259,7 @@
     owners, nb, wdim = d.shape
     width = wd.shape[1]
     part = gu.shape[1]
+    d = pltpu.with_memory_space_constraint(d, pltpu.HBM)
     later = len(before) > 0
     whole = pl.BlockSpec((wdim, width), lambda i: (0, 0))
     d_spec = pl.BlockSpec((owners, per, wdim), lambda i: (0, start // per + i, 0))
@@ -301,6 +302,7 @@
 
 
 def owner_split(gus, group=8):
+    gus = [pltpu.with_memory_space_constraint(gu, pltpu.HBM) for gu in gus]
     owners, _, full = gus[0].shape
     nb = sum(gu.shape[1] for gu in gus)
     total, rows = owners * nb, group * nb

time: 238 us -> 237 us (level)
  local copies, waits for them, and re-layouts: 13.1 us -> 8.71 us
    unnamed x41 -> x37, local copies, waits for them, and re-layouts: 10.4 us -> 6.08 us
  transfers between devices with their start and end apart: 35 -> 35, of which waited for: 12 -> 13; matrix products, arithmetic and copies ran while one was open for 4% -> 4% of each run, Pallas kernels for 32% -> 32%
where the time goes in v5:
time: 237 us; the launch traced here: 236 us
  waiting for transfers between devices  76.9 us (32%)
  Pallas kernels  76.6 us (32%)
  starting transfers between devices  61.5 us (26%)
  other arithmetic  11 us (5%)
  local copies, waits for them, and re-layouts  8.71 us (4%)
    ppermute x19, waiting for transfers between devices, shift(): return lax.ppermute(x, axis, [(i, (i + k) % n) for i in range(n)])  57.3 us
    pallas_call x2, Pallas kernels, middle(): pl.pallas_call(lambda *refs: middle_body(steps, len(before) > 0, *refs),...  55.5 us
    ppermute x12, starting transfers between devices, cross_shift(): return lax.ppermute(x, PLANE, moves)  23.3 us
    all_to_all x4, starting transfers between devices, exchange(): return lax.all_to_all(x, PLANE, split_axis=0, concat_axis=0, tiled=True)  20.3 us
    ppermute x19, starting transfers between devices, shift(): return lax.ppermute(x, axis, [(i, (i + k) % n) for i in range(n)])  17.8 us
    all_to_all x4, waiting for transfers between devices, exchange(): return lax.all_to_all(x, PLANE, split_axis=0, concat_axis=0, tiled=True)  16.6 us
    pallas_call x2, Pallas kernels, owner_backward(): pl.pallas_call(lambda *refs: owner_backward_body(later, *refs), grid=(par...  12.3 us
    unnamed x37, local copies, waits for them, and re-layouts  6.08 us
  transfers between devices with their start and end apart: 35, of which 13 were waited for; matrix products, arithmetic and copies ran while one was open for 4% of the time, Pallas kernels for 32%

profile of v5, /device:TPU:0, one launch (start us, length us, event | category | flops | bytes accessed | tf_op | source)
XLA Modules:
  0.0 235.8 jit_solution(11342724089006698880)
XLA Ops:
  0.7 0.9 fusion.4
  1.6 2.8 %collective-permute-start.2 = (bf16[1,224,128]{2,1,0:T(8,128)(2,1)S(1)}, bf16[1,224,128]{2,1,0:T(8,128)(2,1)S(1)}, u32[]{:S(2)}, u32[]{:S(2)}) collective-permute-start(bf16[1,224,128]{2,1,0:T(8,128)(2,1)S(1)} %fusion.4), channel_id=1, source_target_pairs={{0,6},{1,25},{2,0},{3,27},{4,2},{5,29},{6,4},{7,31},{8,14},{9,1},{... | collective-permute-start | bytes 172040 | tf_op jit(solution)/shard_map/ppermute | solution.py:359
  5.2 0.9 collective-permute-start
  6.2 1.1 copy.30
  8.1 2.0 collective-permute-done.1
  10.8 4.0 %collective-permute-start.4 = (bf16[4,224,128]{2,1,0:T(8,128)(2,1)S(1)}, bf16[4,224,128]{2,1,0:T(8,128)(2,1)S(1)}, u32[]{:S(2)}, u32[]{:S(2)}) collective-permute-start(bf16[4,224,128]{2,1,0:T(8,128)(2,1)S(1)} %get-tuple-element.146), channel_id=1, source_target_pairs={{0,16},{1,5},{2,18},{3,7},{4,20},{5,1},{6,22},{7,3},{8,24},{9,13},... | collective-permute-start | bytes 688136 | tf_op jit(solution)/shard_map/ppermute | solution.py:359
  14.7 1.0 collective-permute-start.3
  15.8 2.2 collective-permute-start.5
  18.1 1.6 copy-done.3
  19.6 5.2 %owner_forward.1 = (bf16[32,80,768]{2,1,0:T(8,128)(2,1)}, bf16[32,48,768]{2,1,0:T(8,128)(2,1)}) custom-call(bf16[32,4096]{1,0:T(8,128)(2,1)S(1)} %bitcast.93, bf16[64,4096]{1,0:T(8,128)(2,1)S(1)} %bitcast.92, bf16[4096,128]{1,0:T(8,128)(2,1)S(1)} %bitcast.91, bf16[4096,256]{1,0:T(8,128)(2,1)S(1)} %bitcast.90, ...), custom_call_target="tpu_custom_call" | custom-call | flops 1073741824 | bytes 10223616 | tf_op jit(solution)/shard_map/owner_forward/pallas_call | solution.py:46
  25.1 4.9 %all-to-all-start = ((bf16[32,80,768]{2,1,0:T(8,128)(2,1)}), bf16[32,80,768]{2,1,0:T(8,128)(2,1)}, u32[]{:S(2)}, u32[]{:S(2)}) async-start(bf16[32,80,768]{2,1,0:T(8,128)(2,1)} %get-tuple-element.71), calls=%async_computation | async-start | bytes 7864320 | tf_op jit(solution)/shard_map/all_to_all | solution.py:330
  29.9 1.6 collective-permute-start.6
  31.6 1.7 collective-permute-start.8
  33.2 20.4 %collective-permute-done.6.refs_6_ = bf16[16,224,128]{2,1,0:T(8,128)(2,1)S(1)} collective-permute-done((bf16[16,224,128]{2,1,0:T(8,128)(2,1)S(1)}, bf16[16,224,128]{2,1,0:T(8,128)(2,1)S(1)}, u32[]{:S(2)}, u32[]{:S(2)}) %collective-permute-start.6) | collective-permute-done | bytes 917536 | tf_op jit(solution)/shard_map/ppermute | solution.py:335
  54.1 3.0 %collective-permute-start.9 = (bf16[8,224,128]{2,1,0:T(8,128)(2,1)S(1)}, bf16[8,224,128]{2,1,0:T(8,128)(2,1)S(1)}, u32[]{:S(2)}, u32[]{:S(2)}) collective-permute-start(bf16[8,224,128]{2,1,0:T(8,128)(2,1)S(1)} %slice.135), channel_id=1, source_target_pairs={{0,96},{32,0},{64,32},{96,64},{1,97},{33,1},{65,33},{97,65},{2,98}... | collective-permute-start | bytes 1376264 | tf_op jit(solution)/shard_map/ppermute | solution.py:335
  57.6 9.2 %collective-permute-done.7 = bf16[8,224,128]{2,1,0:T(8,128)(2,1)S(1)} collective-permute-done((bf16[8,224,128]{2,1,0:T(8,128)(2,1)S(1)}, bf16[8,224,128]{2,1,0:T(8,128)(2,1)S(1)}, u32[]{:S(2)}, u32[]{:S(2)}) %collective-permute-start.7) | collective-permute-done | bytes 458784 | tf_op jit(solution)/shard_map/ppermute | solution.py:335
  68.5 0.9 copy-done.16
  69.6 10.9 %all-to-all-done.refs_3_.refs_4_ = bf16[32,80,768]{2,1,0:T(8,128)(2,1)} async-done(((bf16[32,80,768]{2,1,0:T(8,128)(2,1)}), bf16[32,80,768]{2,1,0:T(8,128)(2,1)}, u32[]{:S(2)}, u32[]{:S(2)}) %all-to-all-start) | async-done | bytes 3932192 | tf_op jit(solution)/shard_map/all_to_all | solution.py:330
  80.5 4.8 %all-to-all-start.2 = ((bf16[32,48,768]{2,1,0:T(8,128)(2,1)}), bf16[32,48,768]{2,1,0:T(8,128)(2,1)}, u32[]{:S(2)}, u32[]{:S(2)}) async-start(bf16[32,48,768]{2,1,0:T(8,128)(2,1)} %get-tuple-element.86), calls=%async_computation.2 | async-start | bytes 4718592 | tf_op jit(solution)/shard_map/all_to_all | solution.py:330
  87.2 30.2 %middle.2 = (bf16[32,80,768]{2,1,0:T(8,128)(2,1)}, bf16[16,224,128]{2,1,0:T(8,128)(2,1)}, bf16[16,224,128]{2,1,0:T(8,128)(2,1)}, bf16[16,224,128]{2,1,0:T(8,128)...) custom-call(s32[3]{0:T(128)} %pad_add_fusion.refs_0_, ...), custom_call_target="tpu_custom_call" | custom-call | flops 8000000000 | bytes 35000000 | tf_op jit(solution)/shard_map/middle/pallas_call | solution.py:198
  117.3 1.1 all-to-all-done.2.refs_3_.refs_4_
  118.4 6.6 %all-to-all-start.1 = ((bf16[32,80,768]{2,1,0:T(8,128)(2,1)}), bf16[32,80,768]{2,1,0:T(8,128)(2,1)}, u32[]{:S(2)}, u32[]{:S(2)}) async-start(bf16[32,80,768]{2,1,0:T(8,128)(2,1)} %get-tuple-element.82), calls=%async_computation.1 | async-start | bytes 7864320 | tf_op jit(solution)/shard_map/all_to_all | solution.py:330
  125.0 25.3 %middle.3 = (bf16[32,48,768]{2,1,0:T(8,128)(2,1)}, bf16[16,224,128]{2,1,0:T(8,128)(2,1)}, bf16[16,224,128]{2,1,0:T(8,128)(2,1)}, bf16[16,224,128]{2,1,0:T(8,128)...) custom-call(s32[3]{0:T(128)} %pad_add_fusion.refs_0_, ...), custom_call_target="tpu_custom_call" | custom-call | flops 4800000000 | bytes 35000000 | tf_op jit(solution)/shard_map/middle/pallas_call | solution.py:198
  151.0 2.1 collective-permute-done.16
  153.1 1.5 add_convert_fusion.1
  154.7 1.6 collective-permute-start.19
  156.3 1.7 collective-permute-start.17
  158.3 0.9 copy-done.11
  159.6 9.0 %collective-permute-done.17 = bf16[8,224,128]{2,1,0:T(8,128)(2,1)S(1)} collective-permute-done((bf16[8,224,128]{2,1,0:T(8,128)(2,1)S(1)}, bf16[8,224,128]{2,1,0:T(8,128)(2,1)S(1)}, u32[]{:S(2)}, u32[]{:S(2)}) %collective-permute-start.17) | collective-permute-done | bytes 458784 | tf_op jit(solution)/shard_map/ppermute | solution.py:335
  168.7 1.0 pad_maximum_fusion
  169.8 1.0 pad_maximum_fusion.1
  170.8 4.6 %all-to-all-done.1.refs_0_.refs_1_ = bf16[32,80,768]{2,1,0:T(8,128)(2,1)} async-done(((bf16[32,80,768]{2,1,0:T(8,128)(2,1)}), bf16[32,80,768]{2,1,0:T(8,128)(2,1)}, u32[]{:S(2)}, u32[]{:S(2)}) %all-to-all-start.1) | async-done | bytes 3932192 | tf_op jit(solution)/shard_map/all_to_all | solution.py:330
  175.4 4.1 %all-to-all-start.3 = ((bf16[32,48,768]{2,1,0:T(8,128)(2,1)}), bf16[32,48,768]{2,1,0:T(8,128)(2,1)S(1)}, u32[]{:S(2)}, u32[]{:S(2)}) async-start(bf16[32,48,768]{2,1,0:T(8,128)(2,1)} %get-tuple-element.107), calls=%async_computation.3 | async-start | bytes 4718592 | tf_op jit(solution)/shard_map/all_to_all | solution.py:330
  179.7 3.0 %collective-permute-start.20 = (bf16[16,224,128]{2,1,0:T(8,128)(2,1)}, bf16[16,224,128]{2,1,0:T(8,128)(2,1)S(1)}, u32[]{:S(2)}, u32[]{:S(2)}) collective-permute-start(bf16[16,224,128]{2,1,0:T(8,128)(2,1)} %pad_maximum_fusion), channel_id=1, source_target_pairs={{0,96},{32,0},{64,32},{96,64},{1,97},{33,1},{65,33},{97,65},{2,98}... | collective-permute-start | bytes 2752520 | tf_op jit(solution)/shard_map/ppermute | solution.py:335
  182.8 7.4 %owner_backward.2 = (bf16[32,128,256]{2,1,0:T(8,128)(2,1)}, bf16[32,128,128]{2,1,0:T(8,128)(2,1)}, f32[256,512]{1,0:T(8,128)S(1)}) custom-call(bf16[32,80,768]{2,1,0:T(8,128)(2,1)} %all-to-all-done.1.refs_0_.refs_1_, bf16[32,80,768]{2,1,0:T(8,128)(2,1)} %all-to-all-done.1.refs_0_.refs_1_, bf16[32,128,256]{2,1,0:T(8,128)(2,1)} %bitcast.88, ...), custom_call_target="tpu_custom_call" | custom-call | flops 1342177280 | bytes 5242880 | tf_op jit(solution)/shard_map/owner_backward/pallas_call | solution.py:275
  190.2 13.0 %collective-permute-done.20 = bf16[16,224,128]{2,1,0:T(8,128)(2,1)S(1)} collective-permute-done((bf16[16,224,128]{2,1,0:T(8,128)(2,1)}, bf16[16,224,128]{2,1,0:T(8,128)(2,1)S(1)}, u32[]{:S(2)}, u32[]{:S(2)}) %collective-permute-start.20) | collective-permute-done | bytes 917536 | tf_op jit(solution)/shard_map/ppermute | solution.py:335
  203.2 3.3 %collective-permute-done.21 = bf16[16,224,128]{2,1,0:T(8,128)(2,1)S(1)} collective-permute-done((bf16[16,224,128]{2,1,0:T(8,128)(2,1)}, bf16[16,224,128]{2,1,0:T(8,128)(2,1)S(1)}, u32[]{:S(2)}, u32[]{:S(2)}) %collective-permute-start.21) | collective-permute-done | bytes 917536 | tf_op jit(solution)/shard_map/ppermute | solution.py:335
  207.9 1.7 collective-permute-start.24
  209.7 2.8 %collective-permute-start.23 = (bf16[4,224,128]{2,1,0:T(8,128)(2,1)}, bf16[4,224,128]{2,1,0:T(8,128)(2,1)}, u32[]{:S(2)}, u32[]{:S(2)}) collective-permute-start(bf16[4,224,128]{2,1,0:T(8,128)(2,1)} %get-tuple-element.131), channel_id=1, source_target_pairs={{0,16},{1,5},{2,18},{3,7},{4,20},{5,1},{6,22},{7,3},{8,24},{9,13},... | collective-permute-start | bytes 688136 | tf_op jit(solution)/shard_map/ppermute | solution.py:359
  212.4 1.4 collective-permute-start.22
  213.9 4.9 %owner_backward.3 = (bf16[32,128,256]{2,1,0:T(8,128)(2,1)}, bf16[32,128,128]{2,1,0:T(8,128)(2,1)}, bf16[256,512]{1,0:T(8,128)(2,1)S(1)}) custom-call(bf16[32,48,768]{2,1,0:T(8,128)(2,1)S(1)} %all-to-all-done.3.refs_0_.refs_1_, bf16[32,48,768]{2,1,0:T(8,128)(2,1)S(1)} %all-to-all-done.3.refs_0_.refs_1_, ...), custom_call_target="tpu_custom_call", output_to_operand_aliasing={{0}: (4, {}), {1}: (5, {})} | custom-call | flops 805306368 | bytes 3145728 | tf_op jit(solution)/shard_map/owner_backward/pallas_call | solution.py:275
  219.2 1.3 add_convert_fusion.2
  220.5 1.5 collective-permute-start.27
  222.2 1.7 collective-permute-start.29
  223.9 1.5 collective-permute-start.28
  225.4 2.7 %collective-permute-start.26 = (bf16[224,128]{1,0:T(8,128)(2,1)S(1)}, bf16[224,128]{1,0:T(8,128)(2,1)S(1)}, u32[]{:S(2)}, u32[]{:S(2)}) collective-permute-start(bf16[224,128]{1,0:T(8,128)(2,1)S(1)} %get-tuple-element.141), channel_id=1, source_target_pairs={{0,4},{1,17},{2,6},{3,19},{4,0},{5,21},{6,2},{7,23},{8,12},{9,25},... | collective-permute-start | bytes 172040 | tf_op jit(solution)/shard_map/ppermute | solution.py:359
  228.1 1.4 collective-permute-start.25
  229.6 3.6 %owner_split.1 = (bf16[32,4096]{1,0:T(8,128)(2,1)}, bf16[64,4096]{1,0:T(8,128)(2,1)}) custom-call(bf16[32,80,768]{2,1,0:T(8,128)(2,1)} %all-to-all-done.1.refs_0_.refs_1_, bf16[32,48,768]{2,1,0:T(8,128)(2,1)} %copy-done.2), custom_call_target="tpu_custom_call" | custom-call | bytes 1835008 | tf_op jit(solution)/shard_map/owner_split/pallas_call | solution.py:309
  (101 shorter events, 13.5 us)
Async XLA Ops:
  0.6 84.7 %copy-start = (f32[512]{0:T(512)S(1)}, f32[512]{0:T(512)}, u32[]{:S(2)}) copy-start(f32[512]{0:T(512)} %param.20) | copy-start | bytes 6148
  0.7 17.4 %copy-start.4 = (bf16[4096,1,128]{2,0,1:T(8,128)(2,1)S(1)}, bf16[4096,1,128]{2,0,1:T(8,128)(2,1)}, u32[]{:S(2)}) copy-start(bf16[4096,1,128]{2,0,1:T(8,128)(2,1)} %param.13) | copy-start | bytes 3145732
  0.7 17.4 %copy-start.5 = (bf16[4096,1,64]{0,2,1:T(8,128)(2,1)S(1)}, bf16[4096,1,64]{0,2,1:T(8,128)(2,1)}, u32[]{:S(2)}) copy-start(bf16[4096,1,64]{0,2,1:T(8,128)(2,1)} %param.12) | copy-start | bytes 1572868
  0.7 17.4 %copy-start.6 = (bf16[4096,1,32]{0,2,1:T(8,128)(2,1)S(1)}, bf16[4096,1,32]{0,2,1:T(8,128)(2,1)}, u32[]{:S(2)}) copy-start(bf16[4096,1,32]{0,2,1:T(8,128)(2,1)} %param.11) | copy-start | bytes 786436
  1.6 6.5 %collective-permute-start.2 = (bf16[1,224,128]{2,1,0:T(8,128)(2,1)S(1)}, bf16[1,224,128]{2,1,0:T(8,128)(2,1)S(1)}, u32[]{:S(2)}, u32[]{:S(2)}) collective-permute-start(bf16[1,224,128]{2,1,0:T(8,128)(2,1)S(1)} %fusion.4), channel_id=1, source_target_pairs={{0,6},{1,25},{2,0},{3,27},{4,2},{5,29},{6,4},{7,31},{8,14},{9,1},{... | collective-permute-start | bytes 172040 | tf_op jit(solution)/shard_map/ppermute | solution.py:359
  4.4 5.7 %collective-permute-start.1 = (bf16[1,224,128]{2,1,0:T(8,128)(2,1)S(1)}, bf16[1,224,128]{2,1,0:T(8,128)(2,1)S(1)}, u32[]{:S(2)}, u32[]{:S(2)}) collective-permute-start(bf16[1,224,128]{2,1,0:T(8,128)(2,1)S(1)} %fusion.4), channel_id=1, source_target_pairs={{0,4},{1,17},{2,6},{3,19},{4,0},{5,21},{6,2},{7,23},{8,12},{9,25},... | collective-permute-start | bytes 172040 | tf_op jit(solution)/shard_map/ppermute | solution.py:359
  5.2 5.5 %collective-permute-start = (bf16[1,224,128]{2,1,0:T(8,128)(2,1)S(1)}, bf16[1,224,128]{2,1,0:T(8,128)(2,1)S(1)}, u32[]{:S(2)}, u32[]{:S(2)}) collective-permute-start(bf16[1,224,128]{2,1,0:T(8,128)(2,1)S(1)} %fusion.4), channel_id=1, source_target_pairs={{0,2},{1,9},{2,4},{3,11},{4,6},{5,13},{6,0},{7,15},{8,10},{9,17},{... | collective-permute-start | bytes 172040 | tf_op jit(solution)/shard_map/ppermute | solution.py:359
  10.8 14.0 %collective-permute-start.4 = (bf16[4,224,128]{2,1,0:T(8,128)(2,1)S(1)}, bf16[4,224,128]{2,1,0:T(8,128)(2,1)S(1)}, u32[]{:S(2)}, u32[]{:S(2)}) collective-permute-start(bf16[4,224,128]{2,1,0:T(8,128)(2,1)S(1)} %get-tuple-element.146), channel_id=1, source_target_pairs={{0,16},{1,5},{2,18},{3,7},{4,20},{5,1},{6,22},{7,3},{8,24},{9,13},... | collective-permute-start | bytes 688136 | tf_op jit(solution)/shard_map/ppermute | solution.py:359
  14.7 10.1 %collective-permute-start.3 = (bf16[4,224,128]{2,1,0:T(8,128)(2,1)S(1)}, bf16[4,224,128]{2,1,0:T(8,128)(2,1)S(1)}, u32[]{:S(2)}, u32[]{:S(2)}) collective-permute-start(bf16[4,224,128]{2,1,0:T(8,128)(2,1)S(1)} %get-tuple-element.146), channel_id=1, source_target_pairs={{0,8},{1,3},{2,10},{3,5},{4,12},{5,7},{6,14},{7,1},{8,16},{9,11},{... | collective-permute-start | bytes 688136 | tf_op jit(solution)/shard_map/ppermute | solution.py:359
  15.8 9.1 %collective-permute-start.5 = (bf16[4,224,128]{2,1,0:T(8,128)(2,1)S(1)}, bf16[4,224,128]{2,1,0:T(8,128)(2,1)S(1)}, u32[]{:S(2)}, u32[]{:S(2)}) collective-permute-start(bf16[4,224,128]{2,1,0:T(8,128)(2,1)S(1)} %get-tuple-element.146), channel_id=1, source_target_pairs={{0,24},{1,7},{2,26},{3,1},{4,28},{5,3},{6,30},{7,5},{8,0},{9,15},{... | collective-permute-start | bytes 688136 | tf_op jit(solution)/shard_map/ppermute | solution.py:359
  18.1 1.6 copy-start.3
  25.0 32.0 %copy-start.7 = (bf16[4,4,224,128]{3,2,1,0:T(8,128)(2,1)}, bf16[4,4,224,128]{3,2,1,0:T(8,128)(2,1)S(1)}, u32[]{:S(2)}) copy-start(bf16[4,4,224,128]{3,2,1,0:T(8,128)(2,1)S(1)} %maximum_select_fusion) | copy-start | bytes 2752516
  25.1 55.5 %all-to-all-start = ((bf16[32,80,768]{2,1,0:T(8,128)(2,1)}), bf16[32,80,768]{2,1,0:T(8,128)(2,1)}, u32[]{:S(2)}, u32[]{:S(2)}) async-start(bf16[32,80,768]{2,1,0:T(8,128)(2,1)} %get-tuple-element.71), calls=%async_computation | async-start | bytes 7864320 | tf_op jit(solution)/shard_map/all_to_all | solution.py:330
  29.9 23.7 %collective-permute-start.6 = (bf16[16,224,128]{2,1,0:T(8,128)(2,1)S(1)}, bf16[16,224,128]{2,1,0:T(8,128)(2,1)S(1)}, u32[]{:S(2)}, u32[]{:S(2)}) collective-permute-start(bf16[16,224,128]{2,1,0:T(8,128)(2,1)S(1)} %bitcast.94), channel_id=1, source_target_pairs={{0,32},{32,64},{64,96},{96,0},{1,33},{33,65},{65,97},{97,1},{2,34}... | collective-permute-start | bytes 2752520 | tf_op jit(solution)/shard_map/ppermute | solution.py:335
  31.6 22.5 %collective-permute-start.8 = (bf16[16,224,128]{2,1,0:T(8,128)(2,1)S(1)}, bf16[16,224,128]{2,1,0:T(8,128)(2,1)S(1)}, u32[]{:S(2)}, u32[]{:S(2)}) collective-permute-start(bf16[16,224,128]{2,1,0:T(8,128)(2,1)S(1)} %bitcast.95), channel_id=1, source_target_pairs={{0,96},{32,0},{64,32},{96,64},{1,97},{33,1},{65,33},{97,65},{2,98}... | collective-permute-start | bytes 2752520 | tf_op jit(solution)/shard_map/ppermute | solution.py:335
  53.6 13.3 %copy-start.8 = (bf16[16,224,128]{2,1,0:T(8,128)(2,1)}, bf16[16,224,128]{2,1,0:T(8,128)(2,1)S(1)}, u32[]{:S(2)}) copy-start(bf16[16,224,128]{2,1,0:T(8,128)(2,1)S(1)} %collective-permute-done.6.refs_6_) | copy-start | bytes 2752516
  53.7 13.1 %collective-permute-start.7 = (bf16[8,224,128]{2,1,0:T(8,128)(2,1)S(1)}, bf16[8,224,128]{2,1,0:T(8,128)(2,1)S(1)}, u32[]{:S(2)}, u32[]{:S(2)}) collective-permute-start(bf16[8,224,128]{2,1,0:T(8,128)(2,1)S(1)} %slice.134), channel_id=1, source_target_pairs={{0,32},{32,64},{64,96},{96,0},{1,33},{33,65},{65,97},{97,1},{2,34}... | collective-permute-start | bytes 1376264 | tf_op jit(solution)/shard_map/ppermute | solution.py:335
  54.0 13.0 %copy-start.9 = (bf16[16,224,128]{2,1,0:T(8,128)(2,1)}, bf16[16,224,128]{2,1,0:T(8,128)(2,1)S(1)}, u32[]{:S(2)}) copy-start(bf16[16,224,128]{2,1,0:T(8,128)(2,1)S(1)} %collective-permute-done.8.refs_8_) | copy-start | bytes 2752516
  54.1 12.8 %collective-permute-start.9 = (bf16[8,224,128]{2,1,0:T(8,128)(2,1)S(1)}, bf16[8,224,128]{2,1,0:T(8,128)(2,1)S(1)}, u32[]{:S(2)}, u32[]{:S(2)}) collective-permute-start(bf16[8,224,128]{2,1,0:T(8,128)(2,1)S(1)} %slice.135), channel_id=1, source_target_pairs={{0,96},{32,0},{64,32},{96,64},{1,97},{33,1},{65,33},{97,65},{2,98}... | collective-permute-start | bytes 1376264 | tf_op jit(solution)/shard_map/ppermute | solution.py:335
  57.1 9.9 %collective-permute-start.10 = (bf16[16,224,128]{2,1,0:T(8,128)(2,1)S(1)}, bf16[16,224,128]{2,1,0:T(8,128)(2,1)S(1)}, u32[]{:S(2)}, u32[]{:S(2)}) collective-permute-start(bf16[16,224,128]{2,1,0:T(8,128)(2,1)S(1)} %bitcast.96), channel_id=1, source_target_pairs={{0,1},{1,0},{2,3},{3,2},{4,5},{5,4},{6,7},{7,6},{8,9},{9,8},{10,11... | collective-permute-start | bytes 2752520 | tf_op jit(solution)/shard_map/ppermute | solution.py:335
  57.1 10.0 %collective-permute-start.13 = (bf16[16,224,128]{2,1,0:T(8,128)(2,1)S(1)}, bf16[16,224,128]{2,1,0:T(8,128)(2,1)S(1)}, u32[]{:S(2)}, u32[]{:S(2)}) collective-permute-start(bf16[16,224,128]{2,1,0:T(8,128)(2,1)S(1)} %collective-permute-done.8.refs_8_), channel_id=1, source_target_pairs={{0,1},{1,0},{2,3},{3,2},{4,5},{5,4},{6,7},{7,6},{8,9},{9,8},{10,11... | collective-permute-start | bytes 2752520 | tf_op jit(solution)/shard_map/ppermute | solution.py:335
  57.6 9.5 %collective-permute-start.11 = (bf16[16,224,128]{2,1,0:T(8,128)(2,1)S(1)}, bf16[16,224,128]{2,1,0:T(8,128)(2,1)S(1)}, u32[]{:S(2)}, u32[]{:S(2)}) collective-permute-start(bf16[16,224,128]{2,1,0:T(8,128)(2,1)S(1)} %collective-permute-done.6.refs_6_), channel_id=1, source_target_pairs={{0,1},{1,0},{2,3},{3,2},{4,5},{5,4},{6,7},{7,6},{8,9},{9,8},{10,11... | collective-permute-start | bytes 2752520 | tf_op jit(solution)/shard_map/ppermute | solution.py:335
  66.9 2.7 %collective-permute-start.12 = (bf16[16,224,128]{2,1,0:T(8,128)(2,1)S(1)}, bf16[16,224,128]{2,1,0:T(8,128)(2,1)}, u32[]{:S(2)}, u32[]{:S(2)}) collective-permute-start(bf16[16,224,128]{2,1,0:T(8,128)(2,1)S(1)} %constant_dynamic-update-slice_fusion.refs_7_), channel_id=1, source_target_pairs={{0,1},{1,0},{2,3},{3,2},{4,5},{5,4},{6,7},{7,6},{8,9},{9,8},{10,11... | collective-permute-start | bytes 2752520 | tf_op jit(solution)/shard_map/ppermute | solution.py:335
  67.0 1.4 copy-start.15
  80.5 37.9 %all-to-all-start.2 = ((bf16[32,48,768]{2,1,0:T(8,128)(2,1)}), bf16[32,48,768]{2,1,0:T(8,128)(2,1)}, u32[]{:S(2)}, u32[]{:S(2)}) async-start(bf16[32,48,768]{2,1,0:T(8,128)(2,1)} %get-tuple-element.86), calls=%async_computation.2 | async-start | bytes 4718592 | tf_op jit(solution)/shard_map/all_to_all | solution.py:330
  118.4 57.0 %all-to-all-start.1 = ((bf16[32,80,768]{2,1,0:T(8,128)(2,1)}), bf16[32,80,768]{2,1,0:T(8,128)(2,1)}, u32[]{:S(2)}, u32[]{:S(2)}) async-start(bf16[32,80,768]{2,1,0:T(8,128)(2,1)} %get-tuple-element.82), calls=%async_computation.1 | async-start | bytes 7864320 | tf_op jit(solution)/shard_map/all_to_all | solution.py:330
  150.4 2.8 %collective-permute-start.16 = (bf16[16,224,128]{2,1,0:T(8,128)(2,1)}, bf16[16,224,128]{2,1,0:T(8,128)(2,1)S(1)}, u32[]{:S(2)}, u32[]{:S(2)}) collective-permute-start(bf16[16,224,128]{2,1,0:T(8,128)(2,1)} %get-tuple-element.101), channel_id=1, source_target_pairs={{0,1},{1,0},{2,3},{3,2},{4,5},{5,4},{6,7},{7,6},{8,9},{9,8},{10,11... | collective-permute-start | bytes 2752520 | tf_op jit(solution)/shard_map/ppermute | solution.py:335
  150.5 7.5 %collective-permute-start.15 = (bf16[16,224,128]{2,1,0:T(8,128)(2,1)}, bf16[16,224,128]{2,1,0:T(8,128)(2,1)S(1)}, u32[]{:S(2)}, u32[]{:S(2)}) collective-permute-start(bf16[16,224,128]{2,1,0:T(8,128)(2,1)} %get-tuple-element.99), channel_id=1, source_target_pairs={{0,1},{1,0},{2,3},{3,2},{4,5},{5,4},{6,7},{7,6},{8,9},{9,8},{10,11... | collective-permute-start | bytes 2752520 | tf_op jit(solution)/shard_map/ppermute | solution.py:335
  150.9 7.3 %collective-permute-start.18 = (bf16[16,224,128]{2,1,0:T(8,128)(2,1)}, bf16[16,224,128]{2,1,0:T(8,128)(2,1)S(1)}, u32[]{:S(2)}, u32[]{:S(2)}) collective-permute-start(bf16[16,224,128]{2,1,0:T(8,128)(2,1)} %get-tuple-element.103), channel_id=1, source_target_pairs={{0,1},{1,0},{2,3},{3,2},{4,5},{5,4},{6,7},{7,6},{8,9},{9,8},{10,11... | collective-permute-start | bytes 2752520 | tf_op jit(solution)/shard_map/ppermute | solution.py:335
  153.1 4.9 %copy-start.12 = (bf16[16,224,128]{2,1,0:T(8,128)(2,1)S(1)}, bf16[16,224,128]{2,1,0:T(8,128)(2,1)}, u32[]{:S(2)}) copy-start(bf16[16,224,128]{2,1,0:T(8,128)(2,1)} %get-tuple-element.98) | copy-start | bytes 2752516
  154.7 15.0 %collective-permute-start.19 = (bf16[8,224,128]{2,1,0:T(8,128)(2,1)S(1)}, bf16[8,224,128]{2,1,0:T(8,128)(2,1)S(1)}, u32[]{:S(2)}, u32[]{:S(2)}) collective-permute-start(bf16[8,224,128]{2,1,0:T(8,128)(2,1)S(1)} %get-tuple-element.134), channel_id=1, source_target_pairs={{0,32},{32,64},{64,96},{96,0},{1,33},{33,65},{65,97},{97,1},{2,34}... | collective-permute-start | bytes 1376264 | tf_op jit(solution)/shard_map/ppermute | solution.py:335
  156.3 12.3 %collective-permute-start.17 = (bf16[8,224,128]{2,1,0:T(8,128)(2,1)S(1)}, bf16[8,224,128]{2,1,0:T(8,128)(2,1)S(1)}, u32[]{:S(2)}, u32[]{:S(2)}) collective-permute-start(bf16[8,224,128]{2,1,0:T(8,128)(2,1)S(1)} %get-tuple-element.135), channel_id=1, source_target_pairs={{0,96},{32,0},{64,32},{96,64},{1,97},{33,1},{65,33},{97,65},{2,98}... | collective-permute-start | bytes 1376264 | tf_op jit(solution)/shard_map/ppermute | solution.py:335
  175.4 38.4 %all-to-all-start.3 = ((bf16[32,48,768]{2,1,0:T(8,128)(2,1)}), bf16[32,48,768]{2,1,0:T(8,128)(2,1)S(1)}, u32[]{:S(2)}, u32[]{:S(2)}) async-start(bf16[32,48,768]{2,1,0:T(8,128)(2,1)} %get-tuple-element.107), calls=%async_computation.3 | async-start | bytes 4718592 | tf_op jit(solution)/shard_map/all_to_all | solution.py:330
  179.5 10.7 %collective-permute-start.14 = (bf16[16,224,128]{2,1,0:T(8,128)(2,1)}, bf16[16,224,128]{2,1,0:T(8,128)(2,1)S(1)}, u32[]{:S(2)}, u32[]{:S(2)}) collective-permute-start(bf16[16,224,128]{2,1,0:T(8,128)(2,1)} %get-tuple-element.96), channel_id=1, source_target_pairs={{0,1},{1,0},{2,3},{3,2},{4,5},{5,4},{6,7},{7,6},{8,9},{9,8},{10,11... | collective-permute-start | bytes 2752520 | tf_op jit(solution)/shard_map/ppermute | solution.py:335
  179.7 23.4 %collective-permute-start.20 = (bf16[16,224,128]{2,1,0:T(8,128)(2,1)}, bf16[16,224,128]{2,1,0:T(8,128)(2,1)S(1)}, u32[]{:S(2)}, u32[]{:S(2)}) collective-permute-start(bf16[16,224,128]{2,1,0:T(8,128)(2,1)} %pad_maximum_fusion), channel_id=1, source_target_pairs={{0,96},{32,0},{64,32},{96,64},{1,97},{33,1},{65,33},{97,65},{2,98}... | collective-permute-start | bytes 2752520 | tf_op jit(solution)/shard_map/ppermute | solution.py:335
  182.8 23.7 %collective-permute-start.21 = (bf16[16,224,128]{2,1,0:T(8,128)(2,1)}, bf16[16,224,128]{2,1,0:T(8,128)(2,1)S(1)}, u32[]{:S(2)}, u32[]{:S(2)}) collective-permute-start(bf16[16,224,128]{2,1,0:T(8,128)(2,1)} %pad_maximum_fusion.1), channel_id=1, source_target_pairs={{0,32},{32,64},{64,96},{96,0},{1,33},{33,65},{65,97},{97,1},{2,34}... | collective-permute-start | bytes 2752520 | tf_op jit(solution)/shard_map/ppermute | solution.py:335
  182.8 23.7 %copy-start.13 = (bf16[16,224,128]{2,1,0:T(8,128)(2,1)S(1)}, bf16[16,224,128]{2,1,0:T(8,128)(2,1)}, u32[]{:S(2)}) copy-start(bf16[16,224,128]{2,1,0:T(8,128)(2,1)} %get-tuple-element.95) | copy-start | bytes 2752516
  207.9 10.9 %collective-permute-start.24 = (bf16[4,224,128]{2,1,0:T(8,128)(2,1)}, bf16[4,224,128]{2,1,0:T(8,128)(2,1)}, u32[]{:S(2)}, u32[]{:S(2)}) collective-permute-start(bf16[4,224,128]{2,1,0:T(8,128)(2,1)} %get-tuple-element.130), channel_id=1, source_target_pairs={{0,8},{1,3},{2,10},{3,5},{4,12},{5,7},{6,14},{7,1},{8,16},{9,11},{... | collective-permute-start | bytes 688136 | tf_op jit(solution)/shard_map/ppermute | solution.py:359
  209.7 9.6 %collective-permute-start.23 = (bf16[4,224,128]{2,1,0:T(8,128)(2,1)}, bf16[4,224,128]{2,1,0:T(8,128)(2,1)}, u32[]{:S(2)}, u32[]{:S(2)}) collective-permute-start(bf16[4,224,128]{2,1,0:T(8,128)(2,1)} %get-tuple-element.131), channel_id=1, source_target_pairs={{0,16},{1,5},{2,18},{3,7},{4,20},{5,1},{6,22},{7,3},{8,24},{9,13},... | collective-permute-start | bytes 688136 | tf_op jit(solution)/shard_map/ppermute | solution.py:359
  212.4 6.8 %collective-permute-start.22 = (bf16[4,224,128]{2,1,0:T(8,128)(2,1)}, bf16[4,224,128]{2,1,0:T(8,128)(2,1)}, u32[]{:S(2)}, u32[]{:S(2)}) collective-permute-start(bf16[4,224,128]{2,1,0:T(8,128)(2,1)} %get-tuple-element.132), channel_id=1, source_target_pairs={{0,24},{1,7},{2,26},{3,1},{4,28},{5,3},{6,30},{7,5},{8,0},{9,15},{... | collective-permute-start | bytes 688136 | tf_op jit(solution)/shard_map/ppermute | solution.py:359
  213.9 4.9 %copy-start.2 = (bf16[32,48,768]{2,1,0:T(8,128)(2,1)}, bf16[32,48,768]{2,1,0:T(8,128)(2,1)S(1)}, u32[]{:S(2)}) copy-start(bf16[32,48,768]{2,1,0:T(8,128)(2,1)S(1)} %all-to-all-done.3.refs_0_.refs_1_) | copy-start | bytes 7077892
  220.5 7.6 %collective-permute-start.27 = (bf16[224,128]{1,0:T(8,128)(2,1)S(1)}, bf16[224,128]{1,0:T(8,128)(2,1)S(1)}, u32[]{:S(2)}, u32[]{:S(2)}) collective-permute-start(bf16[224,128]{1,0:T(8,128)(2,1)S(1)} %get-tuple-element.140), channel_id=1, source_target_pairs={{0,2},{1,9},{2,4},{3,11},{4,6},{5,13},{6,0},{7,15},{8,10},{9,17},{... | collective-permute-start | bytes 172040 | tf_op jit(solution)/shard_map/ppermute | solution.py:359
  222.1 11.0 %collective-permute-start.30 = (bf16[256,128]{1,0:T(8,128)(2,1)S(1)}, bf16[256,128]{1,0:T(8,128)(2,1)S(1)}, u32[]{:S(2)}, u32[]{:S(2)}) collective-permute-start(bf16[256,128]{1,0:T(8,128)(2,1)S(1)} %get-tuple-element.136), channel_id=1, source_target_pairs={{0,32},{32,64},{64,96},{96,0},{1,33},{33,65},{65,97},{97,1},{2,34}... | collective-permute-start | bytes 196616 | tf_op jit(solution)/shard_map/ppermute | solution.py:335
  222.2 11.0 %collective-permute-start.29 = (bf16[256,128]{1,0:T(8,128)(2,1)S(1)}, bf16[256,128]{1,0:T(8,128)(2,1)S(1)}, u32[]{:S(2)}, u32[]{:S(2)}) collective-permute-start(bf16[256,128]{1,0:T(8,128)(2,1)S(1)} %get-tuple-element.137), channel_id=1, source_target_pairs={{0,64},{32,96},{64,0},{96,32},{1,65},{33,97},{65,1},{97,33},{2,66}... | collective-permute-start | bytes 196616 | tf_op jit(solution)/shard_map/ppermute | solution.py:335
  223.9 9.2 %collective-permute-start.28 = (bf16[256,128]{1,0:T(8,128)(2,1)S(1)}, bf16[256,128]{1,0:T(8,128)(2,1)S(1)}, u32[]{:S(2)}, u32[]{:S(2)}) collective-permute-start(bf16[256,128]{1,0:T(8,128)(2,1)S(1)} %get-tuple-element.138), channel_id=1, source_target_pairs={{0,96},{32,0},{64,32},{96,64},{1,97},{33,1},{65,33},{97,65},{2,98}... | collective-permute-start | bytes 196616 | tf_op jit(solution)/shard_map/ppermute | solution.py:335
  225.4 7.7 %collective-permute-start.26 = (bf16[224,128]{1,0:T(8,128)(2,1)S(1)}, bf16[224,128]{1,0:T(8,128)(2,1)S(1)}, u32[]{:S(2)}, u32[]{:S(2)}) collective-permute-start(bf16[224,128]{1,0:T(8,128)(2,1)S(1)} %get-tuple-element.141), channel_id=1, source_target_pairs={{0,4},{1,17},{2,6},{3,19},{4,0},{5,21},{6,2},{7,23},{8,12},{9,25},... | collective-permute-start | bytes 172040 | tf_op jit(solution)/shard_map/ppermute | solution.py:359
  228.1 5.0 %collective-permute-start.25 = (bf16[224,128]{1,0:T(8,128)(2,1)S(1)}, bf16[224,128]{1,0:T(8,128)(2,1)S(1)}, u32[]{:S(2)}, u32[]{:S(2)}) collective-permute-start(bf16[224,128]{1,0:T(8,128)(2,1)S(1)} %get-tuple-element.142), channel_id=1, source_target_pairs={{0,6},{1,25},{2,0},{3,27},{4,2},{5,29},{6,4},{7,31},{8,14},{9,1},{... | collective-permute-start | bytes 172040 | tf_op jit(solution)/shard_map/ppermute | solution.py:359
  229.6 6.2 %copy-start.1 = (f32[512]{0:T(512)S(1)}, f32[512]{0:T(512)}, u32[]{:S(2)}) copy-start(f32[512]{0:T(512)} %param.20) | copy-start | bytes 6148
  (4 other events, 4.2 us)
